TPU v7x, 32 devices: a whole 2x2x4 slice. The times are simulated.
32 devices in a mesh: grp: 2 (over x), samp: 16 (over z, y, core).
Axes of the slice: x: 2, y: 2, z: 4, core: 2. Of those that a mesh axis runs over, the one named last changes fastest.
Arguments:
- genotypes: int32 [32768, 2048], P(('grp', 'samp')), parts along dimension 0, may hold values from 0 to 2
- probe_signs: int32 [32, 32768], P(None, ('grp', 'samp')), parts along dimension 1, may hold values from 0 to 1
- phenotype: float32 [32768], P(('grp', 'samp')), parts along dimension 0, may hold values from -6 to 6
- marker_mean: float32 [2048], replicated, may hold values from 0.2 to 1.8
- marker_scale: float32 [2048], replicated, may hold values from 0.5 to 4
- marker_bin: int32 [2048], replicated, may hold values from 0 to 15, as said below
Outputs:
- products: float32 [16, 33, 32768], P(None, None, ('grp', 'samp')), parts along dimension 2
- gram: float32 [32, 16, 33], P('grp'), parts along dimension 0
There are 2 independent parts, one for each index of `grp`. A program takes and returns all parts, laid end to end along the dimension named above; an argument that names none is the same for every part. Nothing has to cross between parts.
Inputs may be any that keep to these rules, and one draw needn't show every extreme that they name: `marker_bin`: every bin holds exactly 128 markers.
All inputs are finite; a program needn't handle non-finite values.
Results may differ from a plain program's by a relative error of at most 0.0001.
Values sent between devices are 32-bit elements; how exact they have to be, the bound alone decides.
No kernel may reach another device: no remote copies, remote signals or barrier semaphores. Data moves between devices by JAX's collectives and lax.ppermute only.
A program may use at most 128 MiB of HBM per device.

v0:
```python
import jax
import jax.numpy as jnp
from jax import lax
from jax.sharding import PartitionSpec as P

BINS = 16
M_BIN = 128


def shards(genotypes, probe_signs, phenotype, marker_mean, marker_scale, marker_bin):
    samples = genotypes.shape[0]
    devices = lax.axis_size("samp")
    total = jnp.float32(samples * devices)
    order = jnp.argsort(marker_bin, stable=True)
    picked = jnp.take(genotypes, order, axis=1).astype(jnp.float32)
    standard = (picked - marker_mean[order]) * marker_scale[order]
    vectors = jnp.concatenate(
        [(2 * probe_signs - 1).astype(jnp.float32), phenotype[None, :]], axis=0
    )
    share = lax.psum_scatter(
        jnp.dot(
            standard.T,
            vectors.T,
            precision=lax.Precision.HIGHEST,
            preferred_element_type=jnp.float32,
        ),
        "samp",
        scatter_dimension=0,
        tiled=True,
    )
    scores = lax.all_gather(share, "samp", axis=0, tiled=True)
    scores = scores / jnp.sqrt(total)
    blocks = standard.reshape(samples, BINS, M_BIN)
    weights = scores.reshape(BINS, M_BIN, scores.shape[1])
    products = jnp.einsum(
        "skm,kmr->krs", blocks, weights, precision=lax.Precision.HIGHEST
    ) / jnp.sqrt(jnp.float32(M_BIN))
    local_gram = jnp.einsum("krs,lrs->klr", products, products, precision=lax.Precision.HIGHEST)
    gram = lax.psum(local_gram, "samp") / total
    return (products, gram)


def solution(mesh):
    in_specs = (
        P(("grp", "samp"), None),
        P(None, ("grp", "samp")),
        P(("grp", "samp")),
        P(),
        P(),
        P(),
    )
    out_specs = (P(None, None, ("grp", "samp")), P("grp", None, None))
    return jax.shard_map(shards, mesh=mesh, in_specs=in_specs, out_specs=out_specs, check_vma=False)
```

profile of v0, /device:TPU:0, one launch (start us, length us, event | category | flops | bytes accessed | tf_op | source)
XLA Modules:
  0.0 234.6 jit_solution(9177498620670587703)
XLA Ops:
  7.2 0.0 copy-start
  7.2 0.0 copy-start.1
  7.2 0.0 reduce-scatter.2.cloned.1.call-start
  7.2 5.7 %sort.17 = (s32[2048]{0:T(1024)}, s32[2048]{0:T(1024)S(1)}) sort(s32[2048]{0:T(1024)} %param.11, s32[2048]{0:T(1024)S(1)} %iota.4), dimensions={0}, to_apply=%region_0.0 | sort | flops 22528 | bytes 32768 | tf_op jit(solution)/shard_map/jit(argsort)/sort | solution.py:14
  13.0 0.0 copy-done
  13.0 0.0 copy-start.3
  13.0 11.8 %gather_fusion.2 = f32[2048]{0:T(1024)S(1)} fusion(f32[2048]{0:T(1024)S(1)} %copy-done, s32[2048]{0:T(1024)S(1)} %fusion.25), kind=kCustom, calls=%fused_computation.2 | custom fusion | bytes 24576 | tf_op jit(solution)/shard_map/gather | solution.py:16
  24.8 0.0 copy-done.1
  24.8 11.8 %gather_fusion.1 = f32[2048]{0:T(1024)S(1)} fusion(f32[2048]{0:T(1024)S(1)} %copy-done.1, s32[2048]{0:T(1024)S(1)} %fusion.25), kind=kCustom, calls=%fused_computation.1 | custom fusion | bytes 24576 | tf_op jit(solution)/shard_map/gather | solution.py:16
  36.6 0.0 copy-done.3
  36.6 9.3 %copy.15 = s32[1024,2048]{0,1:T(8,128)} copy(s32[1024,2048]{1,0:T(8,128)} %param.6) | data formatting | bytes 16777216 | tf_op args[0]
  45.9 0.0 copy-start.4
  45.9 15.1 %gather_fusion = s32[2048,1024]{1,0:T(8,128)} fusion(s32[1024,2048]{0,1:T(8,128)} %copy.15, s32[2048]{0:T(1024)S(1)} %fusion.25), kind=kCustom, calls=%fused_computation | custom fusion | bytes 16785408 | tf_op jit(solution)/shard_map/jit(_take)/gather | solution.py:15
  61.1 0.0 copy-done.4
  61.1 12.3 %fusion.3 = f32[2048,33]{0,1:T(8,128)} fusion(s32[2048,1024]{1,0:T(8,128)} %gather_fusion, f32[2048]{0:T(1024)S(1)} %gather_fusion.2, f32[2048]{0:T(1024)S(1)} %gather_fusion.1, pred[2048]{0:T(1024)(128)(4,1)S(1)} %compare_and_fusion, f32[1,1024]{1,0:T(1,128)S(1)} %bitcast.31, f32[32,1024]{1,0:T(8,128)S(1)} %add_convert_fusion), kind=kOutput, calls=%fused_computation.7 | convolution fusion | flops 838894592 | bytes 8812544 | tf_op jit(solution)/shard_map/dot_general | solution.py:21
  73.3 0.0 reduce-scatter.2.cloned.1.call-update
  73.4 9.3 %copy.16 = s32[1024,16,128]{2,0,1:T(8,128)} copy(s32[1024,16,128]{0,2,1:T(8,128)} %bitcast.26) | data formatting | bytes 16777216 | tf_op jit(solution)/shard_map/jit(_take)/gather | solution.py:15
  82.6 46.7 %reduce-scatter.2.cloned.1.call-done = f32[128,33]{0,1:T(8,128)} async-done(((f32[2048,33]{0,1:T(8,128)}), f32[128,33]{0,1:T(8,128)}) %reduce-scatter.2.cloned.1.call-update) | async-done | bytes 16912 | tf_op jit(solution)/shard_map/reduce_scatter | solution.py:20
  129.3 20.7 %all_gather.3 = f32[2048,33]{0,1:T(8,128)S(1)} all-gather(f32[128,33]{0,1:T(8,128)} %reduce-scatter.2.cloned.1.call-done), channel_id=1, replica_groups=mesh['grp'=2,'samp'=16] {'samp'}, dimensions={0}, use_global_device_ids=true | all-gather | bytes 287232 | tf_op jit(solution)/shard_map/all_gather | solution.py:31
  150.1 0.1 copy.22
  150.2 11.3 %fusion.18 = f32[16,33,1024]{2,1,0:T(8,128)S(1)} fusion(s32[1024,16,128]{2,0,1:T(8,128)} %copy.16, f32[16,128]{1,0:T(8,128)S(1)} %bitcast.29, f32[16,128]{1,0:T(8,128)S(1)} %bitcast.30, pred[16,128]{1,0:T(8,128)(4,1)S(1)} %fusion.31, f32[16,128,33]{1,0,2:T(8,128)S(1)} %slice_bitcast_fusion), kind=kOutput, calls=%fused_computation.21 | convolution fusion | flops 839401472 | bytes 10840064 | tf_op jit(solution)/shard_map/skm,kmr->krs/dot_general | solution.py:35
  161.4 1.3 copy.20
  162.7 0.0 copy-start.2
  162.7 3.1 %convolution_bitcast_fusion = f32[16,16,33]{0,1,2:T(8,128)S(1)} fusion(f32[16,33,1024]{2,0,1:T(8,128)S(1)} %copy.20), kind=kOutput, calls=%fused_computation.22 | convolution fusion | flops 103809024 | bytes 2196480 | tf_op jit(solution)/shard_map/krs,lrs->klr/dot_general | solution.py:38
  165.8 61.0 %psum.7 = f32[16,16,33]{0,1,2:T(8,128)S(1)} all-reduce(f32[16,16,33]{0,1,2:T(8,128)S(1)} %convolution_bitcast_fusion), channel_id=1, replica_groups=mesh['grp'=2,'samp'=16] {'samp'}, use_global_device_ids=true, to_apply=%region_2.3 | all-reduce | flops 8448 | bytes 67584 | tf_op jit(solution)/shard_map/psum | solution.py:39
  226.9 0.8 copy.21
  227.7 0.0 copy-done.2
  (8 shorter events, 0.1 us)
Async XLA Ops:
  7.2 5.8 %copy-start = (f32[2048]{0:T(1024)S(1)}, f32[2048]{0:T(1024)}, u32[]{:S(2)}) copy-start(f32[2048]{0:T(1024)} %param.10) | copy-start | bytes 24580
  7.2 17.6 %copy-start.1 = (f32[2048]{0:T(1024)S(1)}, f32[2048]{0:T(1024)}, u32[]{:S(2)}) copy-start(f32[2048]{0:T(1024)} %param.9) | copy-start | bytes 24580
  7.2 122.1 %reduce-scatter.2.cloned.1.call-start = ((), (), s32[]{:S(2)}) async-start(), calls=%async_computation.1 | async-start | bytes 348160 | tf_op jit(solution)/shard_map/reduce_scatter | solution.py:20
  13.0 23.6 %copy-start.3 = (s32[32,1024]{1,0:T(8,128)S(1)}, s32[32,1024]{1,0:T(8,128)}, u32[]{:S(2)}) copy-start(s32[32,1024]{1,0:T(8,128)} %param.7) | copy-start | bytes 393220
  45.9 15.2 %copy-start.4 = (f32[1024]{0:T(1024)S(1)}, f32[1024]{0:T(1024)}, u32[]{:S(2)}) copy-start(f32[1024]{0:T(1024)} %param.8) | copy-start | bytes 12292
  162.7 65.0 %copy-start.2 = (f32[16,33,1024]{2,0,1:T(8,128)}, f32[16,33,1024]{2,0,1:T(8,128)S(1)}, u32[]{:S(2)}) copy-start(f32[16,33,1024]{2,0,1:T(8,128)S(1)} %copy.20) | copy-start | bytes 6488068
Sparse Core Ops, SparseCore 0:
  73.5 55.7 reduce-scatter.1
where the time goes:
time: 235 us
  blocking collectives  81.7 us (35%)
  local copies, waits for them, and re-layouts  59.5 us (25%)
  waiting for transfers between devices  46.7 us (20%)
  matrix products  26.7 us (11%)
  between operations  14.2 us (6%)
  other arithmetic  5.82 us (2%)
    psum x1, blocking collectives, shards(): gram = lax.psum(local_gram, 'samp') / total  61 us
    reduce_scatter x1, waiting for transfers between devices, shards(): lax.psum_scatter(jnp.dot(standard.T, vectors.T, precision=lax.Precision.H...  46.7 us
    gather x2, local copies, waits for them, and re-layouts, shards(): picked = jnp.take(genotypes, order, axis=1).astype(jnp.float32)  24.4 us
    gather x2, local copies, waits for them, and re-layouts, shards(): standard = (picked - marker_mean[order]) * marker_scale[order]  23.6 us
    all_gather x1, blocking collectives, shards(): scores = lax.all_gather(share, 'samp', axis=0, tiled=True)  20.7 us
    dot_general x1, matrix products, shards(): jnp.dot(standard.T, vectors.T, precision=lax.Precision.HIGHEST, preferred...  12.3 us
    unnamed x14, local copies, waits for them, and re-layouts  11.5 us
    dot_general x1, matrix products, shards(): jnp.einsum('skm,kmr->krs', blocks, weights, precision=lax.Precision.HIGHEST)  11.3 us
  transfers between devices with their start and end apart: 1, of which 1 were waited for; matrix products, arithmetic and copies ran while one was open for 4% of the time, Pallas kernels for 0%

commit v1 on v0

v1 whole, which is shorter than its diff:
```python
import functools

import jax
import jax.numpy as jnp
from jax import lax
from jax.experimental import pallas as pl
from jax.experimental.pallas import tpu as pltpu
from jax.sharding import PartitionSpec as P

BINS = 16
LANES = 128
F32 = jnp.float32
BF16 = jnp.bfloat16


def two_parts(x):
    hi = x.astype(BF16)
    return hi, (x - hi.astype(F32)).astype(BF16)


def scores_kernel(core_ref, geno_ref, signs_ref, pheno_ref, mean_ref, scale_ref, own_ref, other_ref, acc, sums, *, steps, norm):
    step = pl.program_id(0)
    probes = signs_ref.shape[0]
    markers = geno_ref.shape[1]
    half = probes // 2

    @pl.when(step == 0)
    def _():
        acc[...] = jnp.zeros_like(acc)
        sums[...] = jnp.zeros_like(sums)

    signs = (2 * signs_ref[...] - 1).astype(F32)
    pheno = pheno_ref[...]
    high = pheno.astype(BF16).astype(F32)
    rest = pheno - high
    middle = rest.astype(BF16).astype(F32)
    low = rest - middle
    tail = jnp.zeros((5, pheno.shape[1]), F32)
    vectors = jnp.concatenate([signs, high, middle, low, tail], axis=0)
    acc[...] += jnp.dot(vectors.astype(BF16), geno_ref[...].astype(F32).astype(BF16), preferred_element_type=F32)
    sums[...] += jnp.sum(vectors, axis=1, keepdims=True)

    @pl.when(step == steps - 1)
    def _():
        scale = scale_ref[...] * norm
        acc[...] = (acc[...] - mean_ref[...] * sums[:, :1]) * scale
        core = core_ref[0]
        row = acc[probes : probes + 1, :] + acc[probes + 1 : probes + 2, :] + acc[probes + 2 : probes + 3, :]
        tiles = markers // LANES // 2
        for ref, side in ((own_ref, core), (other_ref, 1 - core)):
            ref[:, :markers] = acc[pl.ds(pl.multiple_of(side * half, half), half), :]
            ref[:, markers:] = jnp.zeros((half, LANES), F32)
            for t in range(tiles):
                low_part = row[:, t * LANES : (t + 1) * LANES]
                high_part = row[:, (tiles + t) * LANES : (tiles + t + 1) * LANES]
                ref[t : t + 1, markers:] = jnp.where(side == 0, low_part, high_part)


def products_kernel(core_ref, own_ref, other_ref, geno_ref, mean_ref, scale_ref, bin_ref, out_ref, gram_ref, w_hi, w_lo, shift, acc, *, steps, norm, gram_norm):
    step = pl.program_id(0)
    half = own_ref.shape[0]
    probes = 2 * half
    markers = geno_ref.shape[1]
    groups = probes // 8

    @pl.when(step == 0)
    def _():
        core = core_ref[0]
        acc[...] = jnp.zeros_like(acc)
        scale = scale_ref[...] * norm
        mean = mean_ref[...]
        inside = bin_ref[...] == lax.broadcasted_iota(jnp.int32, (BINS, markers), 0)
        member = inside.astype(F32)

        def place(row, at):
            weighted = member * row
            shift[pl.ds(at, BINS), :] = jnp.broadcast_to(jnp.sum(weighted * mean, axis=1, keepdims=True), (BINS, LANES))
            hi, lo = two_parts(weighted)
            w_hi[pl.ds(at, BINS), :] = hi
            w_lo[pl.ds(at, BINS), :] = lo

        for ref, side in ((own_ref, core), (other_ref, 1 - core)):
            rows = ref[:, :markers] * scale
            for r in range(half):
                place(rows[r : r + 1, :], pl.multiple_of((side * half + r) * BINS, BINS))
        tiles = markers // LANES // 2
        mine = [own_ref[t : t + 1, markers:] for t in range(tiles)]
        theirs = [other_ref[t : t + 1, markers:] for t in range(tiles)]
        first = [jnp.where(core == 0, a, b) for a, b in zip(mine, theirs)]
        second = [jnp.where(core == 0, b, a) for a, b in zip(mine, theirs)]
        place(jnp.concatenate(first + second, axis=1) * scale, probes * BINS)

    geno = geno_ref[...].astype(F32).astype(BF16)
    nt = (((1,), (1,)), ((), ()))
    dot = functools.partial(lax.dot_general, dimension_numbers=nt, preferred_element_type=F32)
    products = dot(w_hi[...], geno) + dot(w_lo[...], geno) - shift[:, :1]
    out_ref[...] = products.reshape(out_ref.shape)
    hi, lo = two_parts(products)
    for g in range(groups):
        a, b = hi[g * LANES : (g + 1) * LANES], lo[g * LANES : (g + 1) * LANES]
        acc[g * LANES : (g + 1) * LANES, :] += dot(a, a) + dot(a, b) + dot(b, a)
    a, b = hi[groups * LANES :], lo[groups * LANES :]
    acc[groups * LANES :, :BINS] += dot(a, a) + dot(a, b) + dot(b, a)

    @pl.when(step == steps - 1)
    def _():
        column = lax.broadcasted_iota(jnp.int32, (BINS, LANES), 1)
        for g in range(groups):
            total = jnp.zeros((BINS, LANES), F32)
            for r in range(8):
                block = acc[g * LANES + r * BINS : g * LANES + (r + 1) * BINS, :]
                total = jnp.where(column // BINS == r, block, total)
            gram_ref[:, g * LANES : (g + 1) * LANES] = total * gram_norm
        gram_ref[:, groups * LANES :] = acc[groups * LANES :, :] * gram_norm


def exchange(x, pairs):
    return lax.ppermute(x, "samp", pairs)


def shards(genotypes, probe_signs, phenotype, marker_mean, marker_scale, marker_bin):
    samples, markers = genotypes.shape
    probes = probe_signs.shape[0]
    half = probes // 2
    devices = lax.axis_size("samp")
    total = samples * devices
    core = lax.rem(lax.axis_index("samp"), 2).reshape(1)
    mean = marker_mean.reshape(1, markers)
    scale = marker_scale.reshape(1, markers)
    bins = marker_bin.reshape(1, markers)

    block = min(samples, 256)
    steps = samples // block
    whole = lambda i: (0, 0)
    row = pl.BlockSpec((1, markers), whole)
    smem = pl.BlockSpec(memory_space=pltpu.SMEM)
    part = jax.ShapeDtypeStruct((half, markers + LANES), F32)
    own, other = pl.pallas_call(
        functools.partial(scores_kernel, steps=steps, norm=total ** -0.5),
        grid=(steps,),
        out_shape=(part, part),
        in_specs=[
            smem,
            pl.BlockSpec((block, markers), lambda i: (i, 0)),
            pl.BlockSpec((probes, block), lambda i: (0, i)),
            pl.BlockSpec((1, block), lambda i: (0, i)),
            row,
            row,
        ],
        out_specs=(pl.BlockSpec(part.shape, whole), pl.BlockSpec(part.shape, whole)),
        scratch_shapes=[pltpu.VMEM((probes + 8, markers), F32), pltpu.VMEM((probes + 8, LANES), F32)],
        compiler_params=pltpu.CompilerParams(vmem_limit_bytes=48 * 2**20),
        name="scores",
    )(core, genotypes, probe_signs, phenotype.reshape(1, samples), mean, scale)

    flips = [1 << b for b in range(1, devices.bit_length() - 1)]
    cores = [(i, i ^ 1) for i in range(devices)]
    own = own + exchange(other, cores)
    for s in range(len(flips)):
        even, odd = flips[s], flips[s - 1]
        own = own + exchange(own, [(i, i ^ (odd if i % 2 else even)) for i in range(devices)])
    other = exchange(own, cores)

    rows = (probes + 1) * BINS
    gram_wide = (probes // 8 + 1) * LANES
    products, gram = pl.pallas_call(
        functools.partial(products_kernel, steps=steps, norm=(markers // BINS) ** -0.5, gram_norm=1.0 / total),
        grid=(steps,),
        out_shape=(
            jax.ShapeDtypeStruct((probes + 1, BINS, samples), F32),
            jax.ShapeDtypeStruct((BINS, gram_wide), F32),
        ),
        in_specs=[
            smem,
            pl.BlockSpec(part.shape, whole),
            pl.BlockSpec(part.shape, whole),
            pl.BlockSpec((block, markers), lambda i: (i, 0)),
            row,
            row,
            row,
        ],
        out_specs=(
            pl.BlockSpec((probes + 1, BINS, block), lambda i: (0, 0, i)),
            pl.BlockSpec((BINS, gram_wide), whole),
        ),
        scratch_shapes=[
            pltpu.VMEM((rows, markers), BF16),
            pltpu.VMEM((rows, markers), BF16),
            pltpu.VMEM((rows, LANES), F32),
            pltpu.VMEM((rows, LANES), F32),
        ],
        compiler_params=pltpu.CompilerParams(vmem_limit_bytes=48 * 2**20),
        name="products",
    )(core, own, other, genotypes, mean, scale, bins)

    for flip in [1] + flips:
        gram = gram + exchange(gram, [(i, i ^ flip) for i in range(devices)])
    gram = gram[:, : (probes + 1) * BINS].reshape(BINS, probes + 1, BINS)
    return (products.transpose(1, 0, 2), gram.transpose(0, 2, 1))


def solution(mesh):
    in_specs = (
        P(("grp", "samp"), None),
        P(None, ("grp", "samp")),
        P(("grp", "samp")),
        P(),
        P(),
        P(),
    )
    out_specs = (P(None, None, ("grp", "samp")), P("grp", None, None))
    return jax.shard_map(shards, mesh=mesh, in_specs=in_specs, out_specs=out_specs, check_vma=False)
```

time: 235 us -> 56.7 us (0.24)
  blocking collectives: 81.7 us -> 0 us
  local copies, waits for them, and re-layouts: 59.5 us -> 3.97 us
  waiting for transfers between devices: 46.7 us -> 18.7 us
  matrix products: 26.7 us -> 0 us
  starting transfers between devices: 0.04 us -> 16.5 us
  Pallas kernels: 0 us -> 16.4 us
  between operations: 14.2 us -> 0.72 us
  other arithmetic: 5.82 us -> 0.09 us
    psum x1 -> x0, blocking collectives: 61 us -> none  [shards(): gram = lax.psum(local_gram, 'samp') / total]
    gather x4 -> x0, local copies, waits for them, and re-layouts: 48 us -> none  [the longest x2 24.4 us: shards(): picked = jnp.take(genotypes, order, axis=1).astype(jnp.float32)]
    reduce_scatter x1 -> x0, waiting for transfers between devices: 46.7 us -> none  [shards(): lax.psum_scatter(jnp.dot(standard.T, vectors.T, precision=lax.Precision.H...]
    dot_general x3 -> x0, matrix products: 26.7 us -> none  [the longest x1 12.3 us: shards(): jnp.dot(standard.T, vectors.T, precision=lax.Precision.HIGHEST, preferred...]
    all_gather x1 -> x0, blocking collectives: 20.7 us -> none  [shards(): scores = lax.all_gather(share, 'samp', axis=0, tiled=True)]
    ppermute x0 -> x9, waiting for transfers between devices: none -> 18.7 us  [exchange(): return lax.ppermute(x, 'samp', pairs)]
    ppermute x0 -> x9, starting transfers between devices: none -> 16.5 us  [exchange(): return lax.ppermute(x, 'samp', pairs)]
    pallas_call x0 -> x2, Pallas kernels: none -> 16.4 us  [the longest x1 11.6 us: shards(): pl.pallas_call(functools.partial(products_kernel, steps=steps, norm=(mark...]
  transfers between devices with their start and end apart: 1 -> 9, of which waited for: 1 -> 9; matrix products, arithmetic and copies ran while one was open for 4% -> 0% of each run, Pallas kernels for 0% -> 0%
where the time goes in v1:
time: 56.7 us; the launch traced here: 56.4 us
  waiting for transfers between devices  18.7 us (33%)
  starting transfers between devices  16.5 us (29%)
  Pallas kernels  16.4 us (29%)
  local copies, waits for them, and re-layouts  3.97 us (7%)
  between operations  0.72 us (1%)
    ppermute x9, waiting for transfers between devices, exchange(): return lax.ppermute(x, 'samp', pairs)  18.7 us
    ppermute x9, starting transfers between devices, exchange(): return lax.ppermute(x, 'samp', pairs)  16.5 us
    pallas_call x1, Pallas kernels, shards(): pl.pallas_call(functools.partial(products_kernel, steps=steps, norm=(mark...  11.6 us
    pallas_call x1, Pallas kernels, shards(): pl.pallas_call(functools.partial(scores_kernel, steps=steps, norm=total *...  4.71 us
    unnamed x15, local copies, waits for them, and re-layouts  3.84 us
  transfers between devices with their start and end apart: 9, of which 9 were waited for; matrix products, arithmetic and copies ran while one was open for 0% of the time, Pallas kernels for 0%

profile of v1, /device:TPU:0, one launch (start us, length us, event | category | flops | bytes accessed | tf_op | source)
XLA Modules:
  0.0 56.4 jit_solution(16827054546533164702)
XLA Ops:
  0.6 0.0 copy-start.4
  0.6 0.0 copy-start.2
  0.7 0.0 copy-start.5
  0.7 0.0 copy-start
  0.7 0.9 %copy-done = s32[32,1024]{1,0:T(8,128)S(1)} copy-done((s32[32,1024]{1,0:T(8,128)S(1)}, s32[32,1024]{1,0:T(8,128)}, u32[]{:S(2)}) %copy-start) | copy-done | bytes 131096
  1.6 0.0 copy-start.1
  1.6 0.7 %copy-done.1 = f32[2048]{0:T(1024)S(1)} copy-done((f32[2048]{0:T(1024)S(1)}, f32[2048]{0:T(1024)}, u32[]{:S(2)}) %copy-start.1) | copy-done | bytes 8216
  2.3 0.0 copy-start.3
  2.3 0.7 %copy-done.3 = f32[2048]{0:T(1024)S(1)} copy-done((f32[2048]{0:T(1024)S(1)}, f32[2048]{0:T(1024)}, u32[]{:S(2)}) %copy-start.3) | copy-done | bytes 8216
  3.0 0.0 copy-start.6
  3.0 0.7 %copy-done.6 = f32[1024]{0:T(1024)S(1)} copy-done((f32[1024]{0:T(1024)S(1)}, f32[1024]{0:T(1024)}, u32[]{:S(2)}) %copy-start.6) | copy-done | bytes 4120
  3.7 4.7 %scores.1 = (f32[16,2176]{1,0:T(8,128)S(1)}, f32[16,2176]{1,0:T(8,128)S(1)}) custom-call(s32[1]{0:T(128)} %bitcast.core_ref, s32[1024,2048]{1,0:T(8,128)} %geno_ref.3, s32[32,1024]{1,0:T(8,128)S(1)} %copy-done, f32[1,1024]{1,0:T(1,128)S(1)} %bitcast.12, f32[1,2048]{1,0:T(1,128)S(1)} %bitcast.7, f32[1,2048]{1,0:T(1,128)S(1)} %bitcast.9), custom_call_target="tpu_custom_call" | custom-call | tf_op jit(solution)/shard_map/scores/pallas_call | solution.py:138
  8.4 0.5 collective-permute-start
  8.9 1.0 %collective-permute-done = f32[16,2176]{1,0:T(8,128)S(1)} collective-permute-done((f32[16,2176]{1,0:T(8,128)S(1)}, f32[16,2176]{1,0:T(8,128)S(1)}, u32[]{:S(2)}, u32[]{:S(2)}) %collective-permute-start) | collective-permute-done | bytes 139296 | tf_op jit(solution)/shard_map/ppermute | solution.py:118
  9.9 2.9 %collective-permute-start.1 = (f32[16,2176]{1,0:T(8,128)S(1)}, f32[16,2176]{1,0:T(8,128)S(1)}, u32[]{:S(2)}, u32[]{:S(2)}) collective-permute-start(f32[16,2176]{1,0:T(8,128)S(1)} %add.24), channel_id=1, source_target_pairs={{0,2},{1,9},{2,0},{3,11},{4,6},{5,13},{6,4},{7,15},{8,10},{9,1},{1... | collective-permute-start | bytes 417800 | tf_op jit(solution)/shard_map/ppermute | solution.py:118
  12.9 3.0 %collective-permute-done.1 = f32[16,2176]{1,0:T(8,128)S(1)} collective-permute-done((f32[16,2176]{1,0:T(8,128)S(1)}, f32[16,2176]{1,0:T(8,128)S(1)}, u32[]{:S(2)}, u32[]{:S(2)}) %collective-permute-start.1) | collective-permute-done | bytes 139296 | tf_op jit(solution)/shard_map/ppermute | solution.py:118
  15.9 2.1 %collective-permute-start.2 = (f32[16,2176]{1,0:T(8,128)S(1)}, f32[16,2176]{1,0:T(8,128)S(1)}, u32[]{:S(2)}, u32[]{:S(2)}) collective-permute-start(f32[16,2176]{1,0:T(8,128)S(1)} %add.25), channel_id=1, source_target_pairs={{0,4},{1,3},{2,6},{3,1},{4,0},{5,7},{6,2},{7,5},{8,12},{9,11},{10,... | collective-permute-start | bytes 417800 | tf_op jit(solution)/shard_map/ppermute | solution.py:118
  18.1 3.0 %collective-permute-done.2 = f32[16,2176]{1,0:T(8,128)S(1)} collective-permute-done((f32[16,2176]{1,0:T(8,128)S(1)}, f32[16,2176]{1,0:T(8,128)S(1)}, u32[]{:S(2)}, u32[]{:S(2)}) %collective-permute-start.2) | collective-permute-done | bytes 139296 | tf_op jit(solution)/shard_map/ppermute | solution.py:118
  21.1 3.1 %collective-permute-start.3 = (f32[16,2176]{1,0:T(8,128)S(1)}, f32[16,2176]{1,0:T(8,128)S(1)}, u32[]{:S(2)}, u32[]{:S(2)}) collective-permute-start(f32[16,2176]{1,0:T(8,128)S(1)} %add.26), channel_id=1, source_target_pairs={{0,8},{1,5},{2,10},{3,7},{4,12},{5,1},{6,14},{7,3},{8,0},{9,13},{1... | collective-permute-start | bytes 417800 | tf_op jit(solution)/shard_map/ppermute | solution.py:118
  24.2 3.3 %collective-permute-done.3 = f32[16,2176]{1,0:T(8,128)S(1)} collective-permute-done((f32[16,2176]{1,0:T(8,128)S(1)}, f32[16,2176]{1,0:T(8,128)S(1)}, u32[]{:S(2)}, u32[]{:S(2)}) %collective-permute-start.3) | collective-permute-done | bytes 139296 | tf_op jit(solution)/shard_map/ppermute | solution.py:118
  27.5 0.1 collective-permute-start.4
  27.6 1.3 %collective-permute-done.4.other_ref = f32[16,2176]{1,0:T(8,128)S(1)} collective-permute-done((f32[16,2176]{1,0:T(8,128)S(1)}, f32[16,2176]{1,0:T(8,128)S(1)}, u32[]{:S(2)}, u32[]{:S(2)}) %collective-permute-start.4) | collective-permute-done | bytes 139296 | tf_op jit(solution)/shard_map/ppermute | solution.py:118
  28.9 0.0 copy-done.4
  29.0 0.0 copy-done.2
  29.0 0.0 copy-done.5
  29.0 11.6 %products.1 = (f32[33,16,1024]{2,1,0:T(8,128)}, f32[16,640]{1,0:T(8,128)S(1)}) custom-call(s32[1]{0:T(128)} %bitcast.core_ref, f32[16,2176]{1,0:T(8,128)S(1)} %add.27.own_ref, f32[16,2176]{1,0:T(8,128)S(1)} %collective-permute-done.4.other_ref, s32[1024,2048]{1,0:T(8,128)} %geno_ref.3, f32[1,2048]{1,0:T(1,128)S(1)} %bitcast.8, f32[1,2048]{1,0:T(1,128)S(1)} %bitcast.10, ...), custom_call_target="tpu_custom_call" | custom-call | tf_op jit(solution)/shard_map/products/pallas_call | solution.py:166
  40.6 0.1 collective-permute-start.5
  40.7 1.1 %collective-permute-done.5 = f32[16,640]{1,0:T(8,128)S(1)} collective-permute-done((f32[16,640]{1,0:T(8,128)S(1)}, f32[16,640]{1,0:T(8,128)S(1)}, u32[]{:S(2)}, u32[]{:S(2)}) %collective-permute-start.5) | collective-permute-done | bytes 40992 | tf_op jit(solution)/shard_map/ppermute | solution.py:118
  41.8 2.1 %collective-permute-start.6 = (f32[16,640]{1,0:T(8,128)S(1)}, f32[16,640]{1,0:T(8,128)S(1)}, u32[]{:S(2)}, u32[]{:S(2)}) collective-permute-start(f32[16,640]{1,0:T(8,128)S(1)} %add.28), channel_id=1, source_target_pairs={{0,2},{1,3},{2,0},{3,1},{4,6},{5,7},{6,4},{7,5},{8,10},{9,11},{10,... | collective-permute-start | bytes 122888 | tf_op jit(solution)/shard_map/ppermute | solution.py:118
  43.9 2.0 %collective-permute-done.6 = f32[16,640]{1,0:T(8,128)S(1)} collective-permute-done((f32[16,640]{1,0:T(8,128)S(1)}, f32[16,640]{1,0:T(8,128)S(1)}, u32[]{:S(2)}, u32[]{:S(2)}) %collective-permute-start.6) | collective-permute-done | bytes 40992 | tf_op jit(solution)/shard_map/ppermute | solution.py:118
  45.9 2.2 %collective-permute-start.7 = (f32[16,640]{1,0:T(8,128)S(1)}, f32[16,640]{1,0:T(8,128)S(1)}, u32[]{:S(2)}, u32[]{:S(2)}) collective-permute-start(f32[16,640]{1,0:T(8,128)S(1)} %add.29), channel_id=1, source_target_pairs={{0,4},{1,5},{2,6},{3,7},{4,0},{5,1},{6,2},{7,3},{8,12},{9,13},{10,... | collective-permute-start | bytes 122888 | tf_op jit(solution)/shard_map/ppermute | solution.py:118
  48.1 2.0 %collective-permute-done.7 = f32[16,640]{1,0:T(8,128)S(1)} collective-permute-done((f32[16,640]{1,0:T(8,128)S(1)}, f32[16,640]{1,0:T(8,128)S(1)}, u32[]{:S(2)}, u32[]{:S(2)}) %collective-permute-start.7) | collective-permute-done | bytes 40992 | tf_op jit(solution)/shard_map/ppermute | solution.py:118
  50.1 3.4 %collective-permute-start.8 = (f32[16,640]{1,0:T(8,128)S(1)}, f32[16,640]{1,0:T(8,128)S(1)}, u32[]{:S(2)}, u32[]{:S(2)}) collective-permute-start(f32[16,640]{1,0:T(8,128)S(1)} %add.30), channel_id=1, source_target_pairs={{0,8},{1,9},{2,10},{3,11},{4,12},{5,13},{6,14},{7,15},{8,0},{9,1},... | collective-permute-start | bytes 122888 | tf_op jit(solution)/shard_map/ppermute | solution.py:118
  53.4 2.0 %collective-permute-done.8 = f32[16,640]{1,0:T(8,128)S(1)} collective-permute-done((f32[16,640]{1,0:T(8,128)S(1)}, f32[16,640]{1,0:T(8,128)S(1)}, u32[]{:S(2)}, u32[]{:S(2)}) %collective-permute-start.8) | collective-permute-done | bytes 40992 | tf_op jit(solution)/shard_map/ppermute | solution.py:118
  55.4 0.1 reshape.27
  55.6 0.8 %copy.9 = f32[16,16,33]{2,1,0:T(8,128)} copy(f32[16,16,33]{1,2,0:T(8,128)S(1)} %bitcast.13) | data formatting | bytes 67584
  (8 shorter events, 0.1 us)
Async XLA Ops:
  0.6 28.3 %copy-start.4 = (f32[2048]{0:T(1024)S(1)}, f32[2048]{0:T(1024)}, u32[]{:S(2)}) copy-start(f32[2048]{0:T(1024)} %param.10) | copy-start | bytes 24580
  0.6 28.3 %copy-start.2 = (f32[2048]{0:T(1024)S(1)}, f32[2048]{0:T(1024)}, u32[]{:S(2)}) copy-start(f32[2048]{0:T(1024)} %param.9) | copy-start | bytes 24580
  0.7 28.3 %copy-start.5 = (s32[2048]{0:T(1024)S(1)}, s32[2048]{0:T(1024)}, u32[]{:S(2)}) copy-start(s32[2048]{0:T(1024)} %param.11) | copy-start | bytes 24580
  0.7 0.9 %copy-start = (s32[32,1024]{1,0:T(8,128)S(1)}, s32[32,1024]{1,0:T(8,128)}, u32[]{:S(2)}) copy-start(s32[32,1024]{1,0:T(8,128)} %signs_ref.1) | copy-start | bytes 393220
  1.6 0.7 %copy-start.1 = (f32[2048]{0:T(1024)S(1)}, f32[2048]{0:T(1024)}, u32[]{:S(2)}) copy-start(f32[2048]{0:T(1024)} %param.9) | copy-start | bytes 24580
  2.3 0.7 %copy-start.3 = (f32[2048]{0:T(1024)S(1)}, f32[2048]{0:T(1024)}, u32[]{:S(2)}) copy-start(f32[2048]{0:T(1024)} %param.10) | copy-start | bytes 24580
  3.0 0.7 %copy-start.6 = (f32[1024]{0:T(1024)S(1)}, f32[1024]{0:T(1024)}, u32[]{:S(2)}) copy-start(f32[1024]{0:T(1024)} %param.8) | copy-start | bytes 12292
  8.4 1.5 %collective-permute-start = (f32[16,2176]{1,0:T(8,128)S(1)}, f32[16,2176]{1,0:T(8,128)S(1)}, u32[]{:S(2)}, u32[]{:S(2)}) collective-permute-start(f32[16,2176]{1,0:T(8,128)S(1)} %get-tuple-element.7), channel_id=1, source_target_pairs={{0,1},{1,0},{2,3},{3,2},{4,5},{5,4},{6,7},{7,6},{8,9},{9,8},{10,11... | collective-permute-start | bytes 417800 | tf_op jit(solution)/shard_map/ppermute | solution.py:118
  9.9 6.0 %collective-permute-start.1 = (f32[16,2176]{1,0:T(8,128)S(1)}, f32[16,2176]{1,0:T(8,128)S(1)}, u32[]{:S(2)}, u32[]{:S(2)}) collective-permute-start(f32[16,2176]{1,0:T(8,128)S(1)} %add.24), channel_id=1, source_target_pairs={{0,2},{1,9},{2,0},{3,11},{4,6},{5,13},{6,4},{7,15},{8,10},{9,1},{1... | collective-permute-start | bytes 417800 | tf_op jit(solution)/shard_map/ppermute | solution.py:118
  15.9 5.2 %collective-permute-start.2 = (f32[16,2176]{1,0:T(8,128)S(1)}, f32[16,2176]{1,0:T(8,128)S(1)}, u32[]{:S(2)}, u32[]{:S(2)}) collective-permute-start(f32[16,2176]{1,0:T(8,128)S(1)} %add.25), channel_id=1, source_target_pairs={{0,4},{1,3},{2,6},{3,1},{4,0},{5,7},{6,2},{7,5},{8,12},{9,11},{10,... | collective-permute-start | bytes 417800 | tf_op jit(solution)/shard_map/ppermute | solution.py:118
  21.1 6.4 %collective-permute-start.3 = (f32[16,2176]{1,0:T(8,128)S(1)}, f32[16,2176]{1,0:T(8,128)S(1)}, u32[]{:S(2)}, u32[]{:S(2)}) collective-permute-start(f32[16,2176]{1,0:T(8,128)S(1)} %add.26), channel_id=1, source_target_pairs={{0,8},{1,5},{2,10},{3,7},{4,12},{5,1},{6,14},{7,3},{8,0},{9,13},{1... | collective-permute-start | bytes 417800 | tf_op jit(solution)/shard_map/ppermute | solution.py:118
  27.5 1.4 %collective-permute-start.4 = (f32[16,2176]{1,0:T(8,128)S(1)}, f32[16,2176]{1,0:T(8,128)S(1)}, u32[]{:S(2)}, u32[]{:S(2)}) collective-permute-start(f32[16,2176]{1,0:T(8,128)S(1)} %add.27.own_ref), channel_id=1, source_target_pairs={{0,1},{1,0},{2,3},{3,2},{4,5},{5,4},{6,7},{7,6},{8,9},{9,8},{10,11... | collective-permute-start | bytes 417800 | tf_op jit(solution)/shard_map/ppermute | solution.py:118
  40.6 1.2 %collective-permute-start.5 = (f32[16,640]{1,0:T(8,128)S(1)}, f32[16,640]{1,0:T(8,128)S(1)}, u32[]{:S(2)}, u32[]{:S(2)}) collective-permute-start(f32[16,640]{1,0:T(8,128)S(1)} %get-tuple-element.9), channel_id=1, source_target_pairs={{0,1},{1,0},{2,3},{3,2},{4,5},{5,4},{6,7},{7,6},{8,9},{9,8},{10,11... | collective-permute-start | bytes 122888 | tf_op jit(solution)/shard_map/ppermute | solution.py:118
  41.8 4.1 %collective-permute-start.6 = (f32[16,640]{1,0:T(8,128)S(1)}, f32[16,640]{1,0:T(8,128)S(1)}, u32[]{:S(2)}, u32[]{:S(2)}) collective-permute-start(f32[16,640]{1,0:T(8,128)S(1)} %add.28), channel_id=1, source_target_pairs={{0,2},{1,3},{2,0},{3,1},{4,6},{5,7},{6,4},{7,5},{8,10},{9,11},{10,... | collective-permute-start | bytes 122888 | tf_op jit(solution)/shard_map/ppermute | solution.py:118
  45.9 4.2 %collective-permute-start.7 = (f32[16,640]{1,0:T(8,128)S(1)}, f32[16,640]{1,0:T(8,128)S(1)}, u32[]{:S(2)}, u32[]{:S(2)}) collective-permute-start(f32[16,640]{1,0:T(8,128)S(1)} %add.29), channel_id=1, source_target_pairs={{0,4},{1,5},{2,6},{3,7},{4,0},{5,1},{6,2},{7,3},{8,12},{9,13},{10,... | collective-permute-start | bytes 122888 | tf_op jit(solution)/shard_map/ppermute | solution.py:118
  50.1 5.4 %collective-permute-start.8 = (f32[16,640]{1,0:T(8,128)S(1)}, f32[16,640]{1,0:T(8,128)S(1)}, u32[]{:S(2)}, u32[]{:S(2)}) collective-permute-start(f32[16,640]{1,0:T(8,128)S(1)} %add.30), channel_id=1, source_target_pairs={{0,8},{1,9},{2,10},{3,11},{4,12},{5,13},{6,14},{7,15},{8,0},{9,1},... | collective-permute-start | bytes 122888 | tf_op jit(solution)/shard_map/ppermute | solution.py:118

commit v2 on v0

v2 whole, which is shorter than its diff:
```python
import functools

import jax
import jax.numpy as jnp
from jax import lax
from jax.experimental import pallas as pl
from jax.experimental.pallas import tpu as pltpu
from jax.sharding import PartitionSpec as P

BINS = 16
LANES = 128
GROUP = LANES // BINS
F32 = jnp.float32
BF16 = jnp.bfloat16
MIB = 2**20

dot_nt = functools.partial(lax.dot_general, dimension_numbers=(((1,), (1,)), ((), ())), preferred_element_type=F32)


def two_parts(x):
    hi = x.astype(BF16)
    return hi, (x - hi.astype(F32)).astype(BF16)


def scores_kernel(core_ref, geno_hbm, signs_hbm, pheno_hbm, mean_hbm, scale_hbm, own_ref, other_ref, raw, signs, pheno, mean, scale, acc, raw_sems, sems, *, chunk, norm):
    samples, markers = raw.shape
    probes = signs.shape[0]
    half = probes // 2
    chunks = samples // chunk
    pairs = ((signs_hbm, signs), (pheno_hbm, pheno), (mean_hbm, mean), (scale_hbm, scale))
    small = [pltpu.make_async_copy(src, dst, sems.at[i]) for i, (src, dst) in enumerate(pairs)]
    rows = [slice(c * chunk, (c + 1) * chunk) for c in range(chunks)]
    large = [pltpu.make_async_copy(geno_hbm.at[s], raw.at[s], raw_sems.at[c]) for c, s in enumerate(rows)]
    for copy in small[:2] + large + small[2:]:
        copy.start()
    small[0].wait()
    small[1].wait()
    high = pheno[...].astype(BF16).astype(F32)
    rest = pheno[...] - high
    middle = rest.astype(BF16).astype(F32)
    tail = jnp.zeros((5, samples), F32)
    vectors = jnp.concatenate([(2 * signs[...] - 1).astype(F32), high, middle, rest - middle, tail], axis=0)
    sums = jnp.sum(vectors, axis=1, keepdims=True)
    vectors = vectors.astype(BF16)
    for c, s in enumerate(rows):
        large[c].wait()
        part = jnp.dot(vectors[:, s], raw[s].astype(F32).astype(BF16), preferred_element_type=F32)
        if c == 0:
            acc[...] = part
        else:
            acc[...] += part
    small[2].wait()
    small[3].wait()
    acc[...] = (acc[...] - mean[...] * sums) * (scale[...] * norm)
    core = core_ref[0]
    row = acc[probes : probes + 1, :] + acc[probes + 1 : probes + 2, :] + acc[probes + 2 : probes + 3, :]
    tiles = markers // LANES // 2
    for ref, side in ((own_ref, core), (other_ref, 1 - core)):
        ref[:, :markers] = acc[pl.ds(pl.multiple_of(side * half, half), half), :]
        ref[:, markers:] = jnp.zeros((half, LANES), F32)
        for t in range(tiles):
            low_part = row[:, t * LANES : (t + 1) * LANES]
            high_part = row[:, (tiles + t) * LANES : (tiles + t + 1) * LANES]
            ref[half - tiles + t : half - tiles + t + 1, markers:] = jnp.where(side == 0, low_part, high_part)


def narrow_kernel(geno_ref, out_ref):
    out_ref[...] = geno_ref[...].astype(F32).astype(BF16)


def products_kernel(core_ref, own_ref, other_ref, geno_ref, mean_ref, scale_ref, bin_ref, out_ref, gram_ref, weights, prod, sems, *, norm, gram_norm):
    half = own_ref.shape[0]
    probes = 2 * half
    markers = geno_ref.shape[1]
    core = core_ref[0]
    scale = scale_ref[...] * norm
    mean = mean_ref[...]
    member = (bin_ref[...] == lax.broadcasted_iota(jnp.int32, (BINS, markers), 0)).astype(F32)
    tiles = markers // LANES // 2
    mine = [own_ref[half - tiles + t : half - tiles + t + 1, markers:] for t in range(tiles)]
    theirs = [other_ref[half - tiles + t : half - tiles + t + 1, markers:] for t in range(tiles)]
    first = [jnp.where(core == 0, a, b) for a, b in zip(mine, theirs)]
    second = [jnp.where(core == 0, b, a) for a, b in zip(mine, theirs)]
    pheno = jnp.concatenate(first + second, axis=1)

    copies = []
    passes = half // GROUP
    at = 0
    for p in range(passes):
        rows = [ref[p * GROUP + r : p * GROUP + r + 1, :markers] for ref in (own_ref, other_ref) for r in range(GROUP)]
        if p == passes - 1:
            rows.append(pheno)
        count = len(rows) * BINS
        shifts = []
        for r, row in enumerate(rows):
            weighted = member * (row * scale)
            shifts.append(jnp.sum(weighted * mean, axis=1, keepdims=True))
            hi, lo = two_parts(weighted)
            weights[p, r * BINS : (r + 1) * BINS, :] = hi
            weights[p, count + r * BINS : count + (r + 1) * BINS, :] = lo
        both = dot_nt(weights[p, : 2 * count, :], geno_ref[...])
        products = both[:count] + both[count:] - jnp.concatenate(shifts, axis=0)
        prod[at : at + len(rows)] = products.reshape(len(rows), BINS, products.shape[1])
        starts = [pl.multiple_of(side * half + p * GROUP, GROUP) for side in (core, 1 - core)]
        spans = [(at + i * GROUP, GROUP, start) for i, start in enumerate(starts)]
        if p == passes - 1:
            spans.append((at + 2 * GROUP, 1, probes))
        for source, size, start in spans:
            copy = pltpu.make_async_copy(prod.at[pl.ds(source, size)], out_ref.at[pl.ds(start, size)], sems.at[len(copies)])
            copy.start()
            copies.append(copy)
        column = lax.broadcasted_iota(jnp.int32, (BINS, LANES), 1) // BINS
        for i, start in enumerate(starts):
            a, b = two_parts(products[i * LANES : (i + 1) * LANES])
            square = dot_nt(a, a) + dot_nt(a, b) + dot_nt(b, a)
            total = square[:BINS]
            for r in range(1, GROUP):
                total = jnp.where(column == r, square[r * BINS : (r + 1) * BINS], total)
            gram_ref[:, pl.ds(pl.multiple_of(start * BINS, LANES), LANES)] = total * gram_norm
        if p == passes - 1:
            a, b = two_parts(products[2 * LANES :])
            square = dot_nt(a, a) + dot_nt(a, b) + dot_nt(b, a)
            gram_ref[:, probes * BINS : (probes + 1) * BINS] = square * gram_norm
            gram_ref[:, (probes + 1) * BINS :] = jnp.zeros((BINS, LANES - BINS), F32)
        at += len(rows)
    for copy in copies:
        copy.wait()


def parity(i):
    return bin(i).count("1") % 2


def exchange(x, flip):
    return lax.ppermute(x, "samp", [(i, i ^ flip) for i in range(lax.axis_size("samp"))])


def shards(genotypes, probe_signs, phenotype, marker_mean, marker_scale, marker_bin):
    samples, markers = genotypes.shape
    probes = probe_signs.shape[0]
    half = probes // 2
    devices = lax.axis_size("samp")
    total = samples * devices
    core = (lax.population_count(lax.axis_index("samp")) & 1).astype(jnp.int32).reshape(1)
    mean = marker_mean.reshape(1, markers)
    scale = marker_scale.reshape(1, markers)
    bins = marker_bin.reshape(1, markers)
    smem = pl.BlockSpec(memory_space=pltpu.SMEM)
    vmem = pl.BlockSpec(memory_space=pltpu.VMEM)
    hbm = pl.BlockSpec(memory_space=pl.ANY)

    chunk = min(samples, 256)
    part = jax.ShapeDtypeStruct((half, markers + LANES), F32)
    own, other = pl.pallas_call(
        functools.partial(scores_kernel, chunk=chunk, norm=total**-0.5),
        out_shape=(part, part),
        in_specs=[smem, hbm, hbm, hbm, hbm, hbm],
        out_specs=(vmem, vmem),
        scratch_shapes=[
            pltpu.VMEM((samples, markers), jnp.int32),
            pltpu.VMEM((probes, samples), jnp.int32),
            pltpu.VMEM((1, samples), F32),
            pltpu.VMEM((1, markers), F32),
            pltpu.VMEM((1, markers), F32),
            pltpu.VMEM((probes + 8, markers), F32),
            pltpu.SemaphoreType.DMA((samples // chunk,)),
            pltpu.SemaphoreType.DMA((4,)),
        ],
        compiler_params=pltpu.CompilerParams(vmem_limit_bytes=62 * MIB),
        name="scores",
    )(core, genotypes, probe_signs, phenotype.reshape(1, samples), mean, scale)

    narrow = pl.pallas_call(
        narrow_kernel,
        out_shape=jax.ShapeDtypeStruct((samples, markers), BF16),
        in_specs=[vmem],
        out_specs=vmem,
        cost_estimate=pl.CostEstimate(flops=0, bytes_accessed=samples * markers * 6, transcendentals=0),
        compiler_params=pltpu.CompilerParams(vmem_limit_bytes=16 * MIB),
        name="narrow",
    )(genotypes)

    flips = [1 << b for b in range(1, devices.bit_length() - 1)]
    own = own + exchange(other, 1)
    for s in range(len(flips)):
        if s == len(flips) - 1:
            own, narrow = lax.optimization_barrier((own, narrow))
        even, odd = flips[s] | 1, flips[(s + 1) % len(flips)] | 1
        own = own + lax.ppermute(own, "samp", [(i, i ^ (odd if parity(i) else even)) for i in range(devices)])
    other = exchange(own, 1)

    gram_wide = (probes // GROUP + 1) * LANES
    passes = half // GROUP
    products, gram = pl.pallas_call(
        functools.partial(products_kernel, norm=(markers // BINS) ** -0.5, gram_norm=1.0 / total),
        out_shape=(
            jax.ShapeDtypeStruct((probes + 1, BINS, samples), F32),
            jax.ShapeDtypeStruct((BINS, gram_wide), F32),
        ),
        in_specs=[smem, vmem, vmem, vmem, vmem, vmem, vmem],
        out_specs=(hbm, vmem),
        scratch_shapes=[
            pltpu.VMEM((passes, 2 * (2 * GROUP + 1) * BINS, markers), BF16),
            pltpu.VMEM((probes + 1, BINS, samples), F32),
            pltpu.SemaphoreType.DMA((2 * passes + 1,)),
        ],
        compiler_params=pltpu.CompilerParams(vmem_limit_bytes=36 * MIB),
        name="products",
    )(core, own, other, narrow, mean, scale, bins)

    gram = gram + exchange(gram, 1)
    rest = flips
    while rest:
        if len(rest) > 1:
            near, far, both = (exchange(gram, f | 1) for f in (rest[0], rest[1], rest[0] | rest[1]))
            gram = (gram + near) + (far + both)
        else:
            gram = gram + exchange(gram, rest[0] | 1)
        rest = rest[2:]
    gram = gram[:, : (probes + 1) * BINS].reshape(BINS, probes + 1, BINS)
    return (products.transpose(1, 0, 2), gram.transpose(0, 2, 1))


def solution(mesh):
    in_specs = (
        P(("grp", "samp"), None),
        P(None, ("grp", "samp")),
        P(("grp", "samp")),
        P(),
        P(),
        P(),
    )
    out_specs = (P(None, None, ("grp", "samp")), P("grp", None, None))
    return jax.shard_map(shards, mesh=mesh, in_specs=in_specs, out_specs=out_specs, check_vma=False)
```

time: 235 us -> 48.1 us (0.20)
  blocking collectives: 81.7 us -> 0 us
  local copies, waits for them, and re-layouts: 59.5 us -> 4.36 us
  waiting for transfers between devices: 46.7 us -> 14.9 us
  matrix products: 26.7 us -> 0 us
  starting transfers between devices: 0.04 us -> 14.6 us
  between operations: 14.2 us -> 0.71 us
  Pallas kernels: 0 us -> 11.6 us
  other arithmetic: 5.82 us -> 1 us
    psum x1 -> x0, blocking collectives: 61 us -> none  [shards(): gram = lax.psum(local_gram, 'samp') / total]
    gather x4 -> x0, local copies, waits for them, and re-layouts: 48 us -> none  [the longest x2 24.4 us: shards(): picked = jnp.take(genotypes, order, axis=1).astype(jnp.float32)]
    reduce_scatter x1 -> x0, waiting for transfers between devices: 46.7 us -> none  [shards(): lax.psum_scatter(jnp.dot(standard.T, vectors.T, precision=lax.Precision.H...]
    dot_general x3 -> x0, matrix products: 26.7 us -> none  [the longest x1 12.3 us: shards(): jnp.dot(standard.T, vectors.T, precision=lax.Precision.HIGHEST, preferred...]
    all_gather x1 -> x0, blocking collectives: 20.7 us -> none  [shards(): scores = lax.all_gather(share, 'samp', axis=0, tiled=True)]
    ppermute x0 -> x10, waiting for transfers between devices: none -> 14.9 us  [the longest x7 9.42 us: exchange(): lax.ppermute(x, 'samp', [(i, i ^ flip) for i in range(lax.axis_size('samp...]
    ppermute x0 -> x10, starting transfers between devices: none -> 14.6 us  [the longest x3 7.65 us: shards(): lax.ppermute(own, 'samp', [(i, i ^ (odd if parity(i) else even)) for i in...]
    pallas_call x0 -> x3, Pallas kernels: none -> 11.6 us  [the longest x1 6.45 us: shards(): pl.pallas_call(functools.partial(products_kernel, norm=(markers // BINS)...]
  transfers between devices with their start and end apart: 1 -> 10, of which waited for: 1 -> 9; matrix products, arithmetic and copies ran while one was open for 4% -> 0% of each run, Pallas kernels for 0% -> 1%
where the time goes in v2:
time: 48.1 us; the launch traced here: 47.1 us
  waiting for transfers between devices  14.9 us (31%)
  starting transfers between devices  14.6 us (30%)
  Pallas kernels  11.6 us (24%)
  local copies, waits for them, and re-layouts  4.36 us (9%)
  other arithmetic  1 us (2%)
  between operations  0.71 us (1%)
    ppermute x7, waiting for transfers between devices, exchange(): lax.ppermute(x, 'samp', [(i, i ^ flip) for i in range(lax.axis_size('samp...  9.42 us
    ppermute x3, starting transfers between devices, shards(): lax.ppermute(own, 'samp', [(i, i ^ (odd if parity(i) else even)) for i in...  7.65 us
    ppermute x7, starting transfers between devices, exchange(): lax.ppermute(x, 'samp', [(i, i ^ flip) for i in range(lax.axis_size('samp...  6.92 us
    pallas_call x1, Pallas kernels, shards(): pl.pallas_call(functools.partial(products_kernel, norm=(markers // BINS)...  6.45 us
    ppermute x3, waiting for transfers between devices, shards(): lax.ppermute(own, 'samp', [(i, i ^ (odd if parity(i) else even)) for i in...  5.49 us
    pallas_call x1, Pallas kernels, shards(): pl.pallas_call(functools.partial(scores_kernel, chunk=chunk, norm=total *...  4.73 us
    unnamed x9, local copies, waits for them, and re-layouts  4.23 us
  transfers between devices with their start and end apart: 10, of which 9 were waited for; matrix products, arithmetic and copies ran while one was open for 0% of the time, Pallas kernels for 1%

profile of v2, /device:TPU:0, one launch (start us, length us, event | category | flops | bytes accessed | tf_op | source)
XLA Modules:
  0.0 47.1 jit_solution(9256679005454726548)
XLA Ops:
  0.6 4.7 %scores.1 = (f32[16,2176]{1,0:T(8,128)}, f32[16,2176]{1,0:T(8,128)}) custom-call(s32[1]{0:T(128)} %bitcast.core_ref, s32[1024,2048]{1,0:T(8,128)} %geno_ref.1, s32[32,1024]{1,0:T(8,128)} %signs_hbm.1, f32[1,1024]{1,0:T(1,128)} %bitcast.13, f32[1,2048]{1,0:T(1,128)} %bitcast.7, f32[1,2048]{1,0:T(1,128)} %bitcast.9), custom_call_target="tpu_custom_call" | custom-call | tf_op jit(solution)/shard_map/scores/pallas_call | solution.py:154
  5.4 0.5 %collective-permute-start = (f32[16,2176]{1,0:T(8,128)}, f32[16,2176]{1,0:T(8,128)S(1)}, u32[]{:S(2)}, u32[]{:S(2)}) collective-permute-start(f32[16,2176]{1,0:T(8,128)} %get-tuple-element.9), channel_id=1, source_target_pairs={{0,1},{1,0},{2,3},{3,2},{4,5},{5,4},{6,7},{7,6},{8,9},{9,8},{10,11... | collective-permute-start | bytes 417800 | tf_op jit(solution)/shard_map/ppermute | solution.py:135
  5.9 1.2 %collective-permute-done = f32[16,2176]{1,0:T(8,128)S(1)} collective-permute-done((f32[16,2176]{1,0:T(8,128)}, f32[16,2176]{1,0:T(8,128)S(1)}, u32[]{:S(2)}, u32[]{:S(2)}) %collective-permute-start) | collective-permute-done | bytes 139296 | tf_op jit(solution)/shard_map/ppermute | solution.py:135
  7.1 0.9 %add.27 = f32[16,2176]{1,0:T(8,128)S(1)} add(f32[16,2176]{1,0:T(8,128)} %get-tuple-element.8, f32[16,2176]{1,0:T(8,128)S(1)} %collective-permute-done) | non-fusion elementwise | flops 34816 | bytes 417792 | tf_op jit(solution)/shard_map/add | solution.py:184
  8.0 2.7 %collective-permute-start.1 = (f32[16,2176]{1,0:T(8,128)S(1)}, f32[16,2176]{1,0:T(8,128)S(1)}, u32[]{:S(2)}, u32[]{:S(2)}) collective-permute-start(f32[16,2176]{1,0:T(8,128)S(1)} %add.27), channel_id=1, source_target_pairs={{0,3},{1,4},{2,7},{3,0},{4,1},{5,6},{6,5},{7,2},{8,13},{9,10},{10,... | collective-permute-start | bytes 417800 | tf_op jit(solution)/shard_map/ppermute | solution.py:189
  10.7 2.7 %collective-permute-done.1 = f32[16,2176]{1,0:T(8,128)S(1)} collective-permute-done((f32[16,2176]{1,0:T(8,128)S(1)}, f32[16,2176]{1,0:T(8,128)S(1)}, u32[]{:S(2)}, u32[]{:S(2)}) %collective-permute-start.1) | collective-permute-done | bytes 139296 | tf_op jit(solution)/shard_map/ppermute | solution.py:189
  13.5 1.9 %collective-permute-start.2 = (f32[16,2176]{1,0:T(8,128)S(1)}, f32[16,2176]{1,0:T(8,128)S(1)}, u32[]{:S(2)}, u32[]{:S(2)}) collective-permute-start(f32[16,2176]{1,0:T(8,128)S(1)} %add.28), channel_id=1, source_target_pairs={{0,5},{1,8},{2,11},{3,6},{4,13},{5,0},{6,3},{7,14},{8,1},{9,12},{1... | collective-permute-start | bytes 417800 | tf_op jit(solution)/shard_map/ppermute | solution.py:189
  15.3 0.0 copy-start
  15.4 3.4 %copy-done = s32[1024,2048]{1,0:T(8,128)S(1)} copy-done((s32[1024,2048]{1,0:T(8,128)S(1)}, s32[1024,2048]{1,0:T(8,128)}, u32[]{:S(2)}) %copy-start) | copy-done | bytes 8388632
  18.7 0.0 copy-start.1
  18.7 0.0 copy-start.2
  18.7 0.0 copy-start.3
  18.7 0.4 narrow.1.geno_ref
  19.1 0.0 collective-permute-done.2
  19.2 3.1 %collective-permute-start.3 = (f32[16,2176]{1,0:T(8,128)S(1)}, f32[16,2176]{1,0:T(8,128)S(1)}, u32[]{:S(2)}, u32[]{:S(2)}) collective-permute-start(f32[16,2176]{1,0:T(8,128)S(1)} %add.29), channel_id=1, source_target_pairs={{0,9},{1,2},{2,1},{3,10},{4,7},{5,12},{6,15},{7,4},{8,11},{9,0},{1... | collective-permute-start | bytes 417800 | tf_op jit(solution)/shard_map/ppermute | solution.py:189
  22.3 2.8 %collective-permute-done.3 = f32[16,2176]{1,0:T(8,128)S(1)} collective-permute-done((f32[16,2176]{1,0:T(8,128)S(1)}, f32[16,2176]{1,0:T(8,128)S(1)}, u32[]{:S(2)}, u32[]{:S(2)}) %collective-permute-start.3) | collective-permute-done | bytes 139296 | tf_op jit(solution)/shard_map/ppermute | solution.py:189
  25.0 0.2 collective-permute-start.4
  25.2 1.2 %collective-permute-done.4.other_ref = f32[16,2176]{1,0:T(8,128)S(1)} collective-permute-done((f32[16,2176]{1,0:T(8,128)S(1)}, f32[16,2176]{1,0:T(8,128)S(1)}, u32[]{:S(2)}, u32[]{:S(2)}) %collective-permute-start.4) | collective-permute-done | bytes 139296 | tf_op jit(solution)/shard_map/ppermute | solution.py:135
  26.5 0.0 copy-done.1
  26.5 0.0 copy-done.2
  26.5 0.0 copy-done.3
  26.5 6.4 %products.1 = (f32[33,16,1024]{2,1,0:T(8,128)}, f32[16,640]{1,0:T(8,128)S(1)}) custom-call(s32[1]{0:T(128)} %bitcast.core_ref, f32[16,2176]{1,0:T(8,128)S(1)} %add.30.own_ref, f32[16,2176]{1,0:T(8,128)S(1)} %collective-permute-done.4.other_ref, bf16[1024,2048]{1,0:T(8,128)(2,1)S(1)} %narrow.1.geno_ref, f32[1,2048]{1,0:T(1,128)S(1)} %bitcast.8, ...), custom_call_target="tpu_custom_call" | custom-call | tf_op jit(solution)/shard_map/products/pallas_call | solution.py:194
  32.9 0.2 collective-permute-start.5
  33.1 1.1 %collective-permute-done.5 = f32[16,640]{1,0:T(8,128)S(1)} collective-permute-done((f32[16,640]{1,0:T(8,128)S(1)}, f32[16,640]{1,0:T(8,128)S(1)}, u32[]{:S(2)}, u32[]{:S(2)}) %collective-permute-start.5) | collective-permute-done | bytes 40992 | tf_op jit(solution)/shard_map/ppermute | solution.py:135
  34.2 3.0 %collective-permute-start.8 = (f32[16,640]{1,0:T(8,128)S(1)}, f32[16,640]{1,0:T(8,128)S(1)}, u32[]{:S(2)}, u32[]{:S(2)}) collective-permute-start(f32[16,640]{1,0:T(8,128)S(1)} %add.31), channel_id=1, source_target_pairs={{0,7},{1,6},{2,5},{3,4},{4,3},{5,2},{6,1},{7,0},{8,15},{9,14},{10,... | collective-permute-start | bytes 122888 | tf_op jit(solution)/shard_map/ppermute | solution.py:135
  37.3 1.1 %collective-permute-start.7 = (f32[16,640]{1,0:T(8,128)S(1)}, f32[16,640]{1,0:T(8,128)S(1)}, u32[]{:S(2)}, u32[]{:S(2)}) collective-permute-start(f32[16,640]{1,0:T(8,128)S(1)} %add.31), channel_id=1, source_target_pairs={{0,5},{1,4},{2,7},{3,6},{4,1},{5,0},{6,3},{7,2},{8,13},{9,12},{10,... | collective-permute-start | bytes 122888 | tf_op jit(solution)/shard_map/ppermute | solution.py:135
  38.3 0.0 collective-permute-start.6
  38.3 0.6 %collective-permute-done.8 = f32[16,640]{1,0:T(8,128)S(1)} collective-permute-done((f32[16,640]{1,0:T(8,128)S(1)}, f32[16,640]{1,0:T(8,128)S(1)}, u32[]{:S(2)}, u32[]{:S(2)}) %collective-permute-start.8) | collective-permute-done | bytes 40992 | tf_op jit(solution)/shard_map/ppermute | solution.py:135
  39.0 2.2 %collective-permute-done.7 = f32[16,640]{1,0:T(8,128)S(1)} collective-permute-done((f32[16,640]{1,0:T(8,128)S(1)}, f32[16,640]{1,0:T(8,128)S(1)}, u32[]{:S(2)}, u32[]{:S(2)}) %collective-permute-start.7) | collective-permute-done | bytes 40992 | tf_op jit(solution)/shard_map/ppermute | solution.py:135
  41.1 0.6 %collective-permute-done.6 = f32[16,640]{1,0:T(8,128)S(1)} collective-permute-done((f32[16,640]{1,0:T(8,128)S(1)}, f32[16,640]{1,0:T(8,128)S(1)}, u32[]{:S(2)}, u32[]{:S(2)}) %collective-permute-start.6) | collective-permute-done | bytes 40992 | tf_op jit(solution)/shard_map/ppermute | solution.py:135
  41.8 1.9 %collective-permute-start.9 = (f32[16,640]{1,0:T(8,128)S(1)}, f32[16,640]{1,0:T(8,128)S(1)}, u32[]{:S(2)}, u32[]{:S(2)}) collective-permute-start(f32[16,640]{1,0:T(8,128)S(1)} %add_add_fusion), channel_id=1, source_target_pairs={{0,9},{1,8},{2,11},{3,10},{4,13},{5,12},{6,15},{7,14},{8,1},{9,0},... | collective-permute-start | bytes 122888 | tf_op jit(solution)/shard_map/ppermute | solution.py:135
  43.7 2.5 %collective-permute-done.9 = f32[16,640]{1,0:T(8,128)S(1)} collective-permute-done((f32[16,640]{1,0:T(8,128)S(1)}, f32[16,640]{1,0:T(8,128)S(1)}, u32[]{:S(2)}, u32[]{:S(2)}) %collective-permute-start.9) | collective-permute-done | bytes 40992 | tf_op jit(solution)/shard_map/ppermute | solution.py:135
  46.2 0.1 reshape.27
  46.3 0.8 %copy.9 = f32[16,16,33]{2,1,0:T(8,128)} copy(f32[16,16,33]{1,2,0:T(8,128)S(1)} %bitcast.12) | data formatting | bytes 67584
  (6 shorter events, 0.1 us)
Async XLA Ops:
  5.4 1.7 %collective-permute-start = (f32[16,2176]{1,0:T(8,128)}, f32[16,2176]{1,0:T(8,128)S(1)}, u32[]{:S(2)}, u32[]{:S(2)}) collective-permute-start(f32[16,2176]{1,0:T(8,128)} %get-tuple-element.9), channel_id=1, source_target_pairs={{0,1},{1,0},{2,3},{3,2},{4,5},{5,4},{6,7},{7,6},{8,9},{9,8},{10,11... | collective-permute-start | bytes 417800 | tf_op jit(solution)/shard_map/ppermute | solution.py:135
  8.0 5.4 %collective-permute-start.1 = (f32[16,2176]{1,0:T(8,128)S(1)}, f32[16,2176]{1,0:T(8,128)S(1)}, u32[]{:S(2)}, u32[]{:S(2)}) collective-permute-start(f32[16,2176]{1,0:T(8,128)S(1)} %add.27), channel_id=1, source_target_pairs={{0,3},{1,4},{2,7},{3,0},{4,1},{5,6},{6,5},{7,2},{8,13},{9,10},{10,... | collective-permute-start | bytes 417800 | tf_op jit(solution)/shard_map/ppermute | solution.py:189
  13.5 5.7 %collective-permute-start.2 = (f32[16,2176]{1,0:T(8,128)S(1)}, f32[16,2176]{1,0:T(8,128)S(1)}, u32[]{:S(2)}, u32[]{:S(2)}) collective-permute-start(f32[16,2176]{1,0:T(8,128)S(1)} %add.28), channel_id=1, source_target_pairs={{0,5},{1,8},{2,11},{3,6},{4,13},{5,0},{6,3},{7,14},{8,1},{9,12},{1... | collective-permute-start | bytes 417800 | tf_op jit(solution)/shard_map/ppermute | solution.py:189
  15.3 3.4 %copy-start = (s32[1024,2048]{1,0:T(8,128)S(1)}, s32[1024,2048]{1,0:T(8,128)}, u32[]{:S(2)}) copy-start(s32[1024,2048]{1,0:T(8,128)} %geno_ref.1) | copy-start | bytes 25165828
  18.7 7.7 %copy-start.1 = (f32[2048]{0:T(1024)S(1)}, f32[2048]{0:T(1024)}, u32[]{:S(2)}) copy-start(f32[2048]{0:T(1024)} %param.9) | copy-start | bytes 24580
  18.7 7.7 %copy-start.2 = (f32[2048]{0:T(1024)S(1)}, f32[2048]{0:T(1024)}, u32[]{:S(2)}) copy-start(f32[2048]{0:T(1024)} %param.10) | copy-start | bytes 24580
  18.7 7.7 %copy-start.3 = (s32[2048]{0:T(1024)S(1)}, s32[2048]{0:T(1024)}, u32[]{:S(2)}) copy-start(s32[2048]{0:T(1024)} %param.11) | copy-start | bytes 24580
  19.2 5.8 %collective-permute-start.3 = (f32[16,2176]{1,0:T(8,128)S(1)}, f32[16,2176]{1,0:T(8,128)S(1)}, u32[]{:S(2)}, u32[]{:S(2)}) collective-permute-start(f32[16,2176]{1,0:T(8,128)S(1)} %add.29), channel_id=1, source_target_pairs={{0,9},{1,2},{2,1},{3,10},{4,7},{5,12},{6,15},{7,4},{8,11},{9,0},{1... | collective-permute-start | bytes 417800 | tf_op jit(solution)/shard_map/ppermute | solution.py:189
  25.0 1.4 %collective-permute-start.4 = (f32[16,2176]{1,0:T(8,128)S(1)}, f32[16,2176]{1,0:T(8,128)S(1)}, u32[]{:S(2)}, u32[]{:S(2)}) collective-permute-start(f32[16,2176]{1,0:T(8,128)S(1)} %add.30.own_ref), channel_id=1, source_target_pairs={{0,1},{1,0},{2,3},{3,2},{4,5},{5,4},{6,7},{7,6},{8,9},{9,8},{10,11... | collective-permute-start | bytes 417800 | tf_op jit(solution)/shard_map/ppermute | solution.py:135
  32.9 1.3 %collective-permute-start.5 = (f32[16,640]{1,0:T(8,128)S(1)}, f32[16,640]{1,0:T(8,128)S(1)}, u32[]{:S(2)}, u32[]{:S(2)}) collective-permute-start(f32[16,640]{1,0:T(8,128)S(1)} %get-tuple-element.13), channel_id=1, source_target_pairs={{0,1},{1,0},{2,3},{3,2},{4,5},{5,4},{6,7},{7,6},{8,9},{9,8},{10,11... | collective-permute-start | bytes 122888 | tf_op jit(solution)/shard_map/ppermute | solution.py:135
  34.2 4.7 %collective-permute-start.8 = (f32[16,640]{1,0:T(8,128)S(1)}, f32[16,640]{1,0:T(8,128)S(1)}, u32[]{:S(2)}, u32[]{:S(2)}) collective-permute-start(f32[16,640]{1,0:T(8,128)S(1)} %add.31), channel_id=1, source_target_pairs={{0,7},{1,6},{2,5},{3,4},{4,3},{5,2},{6,1},{7,0},{8,15},{9,14},{10,... | collective-permute-start | bytes 122888 | tf_op jit(solution)/shard_map/ppermute | solution.py:135
  37.3 3.9 %collective-permute-start.7 = (f32[16,640]{1,0:T(8,128)S(1)}, f32[16,640]{1,0:T(8,128)S(1)}, u32[]{:S(2)}, u32[]{:S(2)}) collective-permute-start(f32[16,640]{1,0:T(8,128)S(1)} %add.31), channel_id=1, source_target_pairs={{0,5},{1,4},{2,7},{3,6},{4,1},{5,0},{6,3},{7,2},{8,13},{9,12},{10,... | collective-permute-start | bytes 122888 | tf_op jit(solution)/shard_map/ppermute | solution.py:135
  38.3 3.4 %collective-permute-start.6 = (f32[16,640]{1,0:T(8,128)S(1)}, f32[16,640]{1,0:T(8,128)S(1)}, u32[]{:S(2)}, u32[]{:S(2)}) collective-permute-start(f32[16,640]{1,0:T(8,128)S(1)} %add.31), channel_id=1, source_target_pairs={{0,3},{1,2},{2,1},{3,0},{4,7},{5,6},{6,5},{7,4},{8,11},{9,10},{10,... | collective-permute-start | bytes 122888 | tf_op jit(solution)/shard_map/ppermute | solution.py:135
  41.8 4.4 %collective-permute-start.9 = (f32[16,640]{1,0:T(8,128)S(1)}, f32[16,640]{1,0:T(8,128)S(1)}, u32[]{:S(2)}, u32[]{:S(2)}) collective-permute-start(f32[16,640]{1,0:T(8,128)S(1)} %add_add_fusion), channel_id=1, source_target_pairs={{0,9},{1,8},{2,11},{3,10},{4,13},{5,12},{6,15},{7,14},{8,1},{9,0},... | collective-permute-start | bytes 122888 | tf_op jit(solution)/shard_map/ppermute | solution.py:135

commit v3 on v0

v3 whole, which is shorter than its diff:
```python
import functools

import jax
import jax.numpy as jnp
from jax import lax
from jax.experimental import pallas as pl
from jax.experimental.pallas import tpu as pltpu
from jax.sharding import PartitionSpec as P

BINS = 16
LANES = 128
GROUP = LANES // BINS
F32 = jnp.float32
BF16 = jnp.bfloat16
MIB = 2**20

dot_nt = functools.partial(lax.dot_general, dimension_numbers=(((1,), (1,)), ((), ())), preferred_element_type=F32)


def two_parts(x):
    hi = x.astype(BF16)
    return hi, (x - hi.astype(F32)).astype(BF16)


def sign_rows(signs_ref):
    return (2 * signs_ref[...] - 1).astype(F32).astype(BF16)


def pheno_rows(pheno_ref):
    pheno = pheno_ref[...]
    high = pheno.astype(BF16).astype(F32)
    rest = pheno - high
    middle = rest.astype(BF16).astype(F32)
    tail = jnp.zeros((13, pheno.shape[1]), F32)
    return jnp.concatenate([high, middle, rest - middle, tail], axis=0).astype(BF16)


def add_three(x):
    return x[:1] + x[1:2] + x[2:3]


def accumulate(vectors, geno_hbm, narrow_ref, raw, acc, sems, start, chunk):
    samples, markers = raw.shape
    rows = [slice(c * chunk, (c + 1) * chunk) for c in range(samples // chunk)]
    copies = [pltpu.make_async_copy(geno_hbm.at[s, start : start + markers], raw.at[s], sems.at[c]) for c, s in enumerate(rows)]
    for copy in copies:
        copy.start()
    yield
    for c, s in enumerate(rows):
        copies[c].wait()
        narrow = raw[s].astype(F32).astype(BF16)
        narrow_ref[s] = narrow
        part = jnp.dot(vectors()[:, s], narrow, preferred_element_type=F32)
        if c == 0:
            acc[...] = part
        else:
            acc[...] += part
    yield


def place_rows(side, acc, sums, own_ref, other_ref, at):
    half, _ = own_ref.shape
    markers = acc.shape[1]
    for ref, which in ((own_ref, side), (other_ref, 1 - side)):
        ref[:, :markers] = acc[pl.ds(pl.multiple_of(which * half, half), half), :]
        ref[:, at:] = jnp.zeros((half, LANES), F32)
        ref[:1, at : at + half] = jnp.where(which == 0, sums[:, :half], sums[:, half : 2 * half])


def first_sums_kernel(side_ref, geno_hbm, signs_ref, own_ref, other_ref, narrow_ref, raw, acc, sems, *, start, chunk):
    vectors = None
    steps = accumulate(lambda: vectors, geno_hbm, narrow_ref, raw, acc, sems, start, chunk)
    next(steps)
    vectors = sign_rows(signs_ref)
    sums = dot_nt(jnp.ones((8, vectors.shape[1]), BF16), vectors)[:1]
    next(steps)
    place_rows(side_ref[0], acc, sums, own_ref, other_ref, raw.shape[1])


def second_sums_kernel(side_ref, geno_hbm, signs_ref, pheno_ref, first_ref, own_ref, other_ref, narrow_ref, raw, acc, sems, *, start, chunk):
    markers = raw.shape[1]
    probes = signs_ref.shape[0]
    vectors = None
    steps = accumulate(lambda: vectors, geno_hbm, narrow_ref, raw, acc, sems, start, chunk)
    next(steps)
    pheno = pheno_rows(pheno_ref)
    vectors = jnp.concatenate([sign_rows(signs_ref), pheno], axis=0)
    sums = dot_nt(jnp.ones((8, vectors.shape[1]), BF16), vectors)[:1]
    first = add_three(jnp.dot(pheno, first_ref[...], preferred_element_type=F32)[:8])
    next(steps)
    place_rows(side_ref[0], acc, sums, own_ref, other_ref, markers + LANES)
    half = own_ref.shape[0]
    last = sums[:, probes : probes + 1] + sums[:, probes + 1 : probes + 2] + sums[:, probes + 2 : probes + 3]
    row = jnp.concatenate([first, add_three(acc[probes : probes + 8, :])], axis=1)
    for ref in (own_ref, other_ref):
        ref[:1, markers + LANES + half : markers + LANES + half + 1] = last
        for t in range(row.shape[1] // LANES):
            ref[t : t + 1, markers : markers + LANES] = row[:, t * LANES : (t + 1) * LANES]


class Half:
    def __init__(self, mean_ref, scale_ref, bin_ref, geno_ref, start, norm):
        markers = geno_ref.shape[1]
        self.geno = geno_ref
        self.mean = mean_ref[:, start : start + markers]
        scale = scale_ref[:, start : start + markers]
        self.scale = scale * scale * norm
        self.member = (bin_ref[:, start : start + markers] == lax.broadcasted_iota(jnp.int32, (BINS, markers), 0)).astype(F32)

    def scores(self, sums, total):
        return (sums - self.mean * total) * self.scale

    def probe_scores(self, ref):
        markers = self.mean.shape[1]
        at = ref.shape[1] - LANES
        return [self.scores(ref[r : r + 1, :markers], ref[:1, at + r : at + r + 1]) for r in range(ref.shape[0])]

    def products(self, rows, weights):
        shifts = []
        count = len(rows) * BINS
        for r, row in enumerate(rows):
            weighted = self.member * row
            shifts.append(jnp.sum(weighted * self.mean, axis=1, keepdims=True))
            hi, lo = two_parts(weighted)
            weights[r * BINS : (r + 1) * BINS, :] = hi
            weights[count + r * BINS : count + (r + 1) * BINS, :] = lo
        both = dot_nt(weights[: 2 * count, :], self.geno[...])
        return both[:count] + both[count:] - jnp.concatenate(shifts, axis=0)


def square_of(products):
    count = products.shape[0]
    hi, lo = two_parts(products)
    both = dot_nt(jnp.concatenate([hi, lo], axis=0), hi)
    return both[:count] + (both[count:] + both[count:].T)


def gram_of(products, gram_norm):
    parts = []
    column = lax.broadcasted_iota(jnp.int32, (BINS, LANES), 1) // BINS
    for g in range(products.shape[0] // LANES):
        square = square_of(products[g * LANES : (g + 1) * LANES])
        total = square[:BINS]
        for r in range(1, GROUP):
            total = jnp.where(column == r, square[r * BINS : (r + 1) * BINS], total)
        parts.append(total * gram_norm)
    return jnp.concatenate(parts, axis=1)


def part_kernel(own_a, geno_a, mean_ref, scale_ref, bin_ref, part_ref, weights, *, norm):
    first = Half(mean_ref, scale_ref, bin_ref, geno_a, 0, norm)
    part_ref[...] = first.products(first.probe_scores(own_a), weights)


def own_kernel(side_ref, part_ref, other_a, own_b, geno_a, geno_b, mean_ref, scale_ref, bin_ref, out_ref, gram_ref, other_ref, weights, prod, sems, *, norm, gram_norm):
    half = own_b.shape[0]
    count = half * BINS
    markers = geno_a.shape[1]
    samples = geno_a.shape[0]
    first = Half(mean_ref, scale_ref, bin_ref, geno_a, 0, norm)
    second = Half(mean_ref, scale_ref, bin_ref, geno_b, markers, norm)
    tiles = markers // LANES
    pheno = [own_b[t : t + 1, markers : markers + LANES] for t in range(2 * tiles)]
    total = own_b[:1, markers + LANES + half : markers + LANES + half + 1]
    rows_b = second.probe_scores(own_b) + [second.scores(jnp.concatenate(pheno[tiles:], axis=1), total)]
    rows_a = first.probe_scores(other_a) + [first.scores(jnp.concatenate(pheno[:tiles], axis=1), total)]
    parts_b = second.products(rows_b, weights.at[0])
    mine = part_ref[...] + parts_b[:count]
    prod[:half] = mine.reshape(half, BINS, samples)
    copies = [pltpu.make_async_copy(prod.at[pl.ds(0, half)], out_ref.at[pl.ds(pl.multiple_of(side_ref[0] * half, half), half)], sems.at[0])]
    copies[0].start()
    gram_ref[:, : half * BINS] = gram_of(mine, gram_norm)
    parts_a = first.products(rows_a, weights.at[1])
    other_ref[...] = parts_a[:count]
    last = parts_a[count:] + parts_b[count:]
    prod[half : half + 1] = last.reshape(1, BINS, samples)
    copies.append(pltpu.make_async_copy(prod.at[pl.ds(half, 1)], out_ref.at[pl.ds(2 * half, 1)], sems.at[1]))
    copies[1].start()
    gram_ref[:, half * BINS : (half + 1) * BINS] = square_of(last) * gram_norm
    gram_ref[:, (half + 1) * BINS :] = jnp.zeros((BINS, LANES - BINS), F32)
    for copy in copies:
        copy.wait()


def other_kernel(side_ref, part_ref, other_b, geno_b, mean_ref, scale_ref, bin_ref, own_gram_ref, _, out_ref, gram_ref, weights, prod, sems, *, norm, gram_norm):
    half = other_b.shape[0]
    wide = half * BINS
    samples, markers = geno_b.shape
    side = side_ref[0]
    second = Half(mean_ref, scale_ref, bin_ref, geno_b, markers, norm)
    rows = second.probe_scores(other_b)
    products = part_ref[...] + second.products(rows, weights)
    prod[...] = products.reshape(half, BINS, samples)
    copy = pltpu.make_async_copy(prod, out_ref.at[pl.ds(pl.multiple_of((1 - side) * half, half), half)], sems.at[0])
    copy.start()
    gram_ref[:, pl.ds(pl.multiple_of((1 - side) * wide, wide), wide)] = gram_of(products, gram_norm)
    gram_ref[:, pl.ds(pl.multiple_of(side * wide, wide), wide)] = own_gram_ref[:, :wide]
    gram_ref[:, 2 * wide :] = own_gram_ref[:, wide:]
    copy.wait()


def parity(i):
    return bin(i).count("1") % 2


def exchange(x, even, odd=None):
    pairs = [(i, i ^ (even if odd is None or not parity(i) else odd)) for i in range(lax.axis_size("samp"))]
    return lax.ppermute(x, "samp", pairs)


def shards(genotypes, probe_signs, phenotype, marker_mean, marker_scale, marker_bin):
    samples, markers = genotypes.shape
    probes = probe_signs.shape[0]
    half = probes // 2
    devices = lax.axis_size("samp")
    total = samples * devices
    side = (lax.population_count(lax.axis_index("samp")) & 1).astype(jnp.int32).reshape(1)
    markers_info = [x.reshape(1, markers) for x in (marker_mean, marker_scale, marker_bin)]
    pheno = phenotype.reshape(1, samples)
    smem = pl.BlockSpec(memory_space=pltpu.SMEM)
    vmem = pl.BlockSpec(memory_space=pltpu.VMEM)
    hbm = pl.BlockSpec(memory_space=pl.ANY)

    width = markers // 2
    chunk = min(samples, 256)
    narrow = jax.ShapeDtypeStruct((samples, width), BF16)

    def sums(kernel, start, name, extra, rows, *operands):
        part = jax.ShapeDtypeStruct((half, width + extra), F32)
        return pl.pallas_call(
            functools.partial(kernel, start=start, chunk=chunk),
            out_shape=(part, part, narrow),
            in_specs=[smem, hbm] + [vmem] * (len(operands) - 2),
            out_specs=(vmem, vmem, vmem),
            scratch_shapes=[
                pltpu.VMEM((samples, width), jnp.int32),
                pltpu.VMEM((rows, width), F32),
                pltpu.SemaphoreType.DMA((samples // chunk,)),
            ],
            cost_estimate=pl.CostEstimate(flops=2 * rows * samples * width, bytes_accessed=6 * samples * width, transcendentals=0),
            compiler_params=pltpu.CompilerParams(vmem_limit_bytes=47 * MIB),
            name=name,
        )(*operands)

    flips = [1 << b for b in range(1, devices.bit_length() - 1)]
    own_a, other_a, narrow_a = sums(first_sums_kernel, 0, "sums_first", LANES, probes, side, genotypes, probe_signs)
    own_b, other_b, narrow_b = sums(
        second_sums_kernel, width, "sums_second", 2 * LANES, probes + 16, side, genotypes, probe_signs, pheno, narrow_a
    )
    own_a = own_a + exchange(other_a, 1)
    own_b = own_b + exchange(other_b, 1)
    received = None
    for s in range(len(flips)):
        even, odd = flips[s] | 1, flips[(s + 1) % len(flips)] | 1
        own_a = own_a + exchange(own_a, even, odd)
        if received is not None:
            own_b = own_b + received
        received = exchange(own_b, even, odd)

    norm = (total * (markers // BINS)) ** -0.5
    gram_norm = 1.0 / total
    rows = half * BINS

    def work(count):
        return pl.CostEstimate(flops=4 * count * samples * width, bytes_accessed=4 * rows * samples, transcendentals=0)

    params = pltpu.CompilerParams(vmem_limit_bytes=32 * MIB)
    part = jax.ShapeDtypeStruct((rows, samples), F32)
    weights = pltpu.VMEM((2 * rows, width), BF16)
    products = jax.ShapeDtypeStruct((probes + 1, BINS, samples), F32)

    other_a = exchange(own_a, 1)
    own_part = pl.pallas_call(
        functools.partial(part_kernel, norm=norm),
        out_shape=part,
        in_specs=[vmem] * 5,
        out_specs=vmem,
        scratch_shapes=[weights],
        cost_estimate=work(rows),
        compiler_params=params,
        name="products_part",
    )(own_a, narrow_a, *markers_info)
    own_b, received, own_part = lax.optimization_barrier((own_b, received, own_part))
    own_b = own_b + received
    other_b = exchange(own_b, 1)
    products, gram, other_part = pl.pallas_call(
        functools.partial(own_kernel, norm=norm, gram_norm=gram_norm),
        out_shape=(products, jax.ShapeDtypeStruct((BINS, rows + LANES), F32), part),
        in_specs=[smem] + [vmem] * 8,
        out_specs=(hbm, vmem, vmem),
        scratch_shapes=[
            pltpu.VMEM((2, 2 * (rows + BINS), width), BF16),
            pltpu.VMEM((half + 1, BINS, samples), F32),
            pltpu.SemaphoreType.DMA((2,)),
        ],
        cost_estimate=work(2 * rows),
        compiler_params=params,
        name="products_own",
    )(side, own_part, other_a, own_b, narrow_a, narrow_b, *markers_info)
    products, gram = pl.pallas_call(
        functools.partial(other_kernel, norm=norm, gram_norm=gram_norm),
        out_shape=(products, jax.ShapeDtypeStruct((BINS, 2 * rows + LANES), F32)),
        in_specs=[smem] + [vmem] * 7 + [hbm],
        out_specs=(hbm, vmem),
        scratch_shapes=[weights, pltpu.VMEM((half, BINS, samples), F32), pltpu.SemaphoreType.DMA((1,))],
        input_output_aliases={8: 0},
        cost_estimate=work(rows),
        compiler_params=params,
        name="products_other",
    )(side, other_part, other_b, narrow_b, *markers_info, gram, products)

    gram = gram + exchange(gram, 1)
    rest = flips
    while rest:
        if len(rest) > 1:
            near, far, both = (exchange(gram, f | 1) for f in (rest[0], rest[1], rest[0] | rest[1]))
            gram = (gram + near) + (far + both)
        else:
            gram = gram + exchange(gram, rest[0] | 1)
        rest = rest[2:]
    gram = gram[:, : (probes + 1) * BINS].reshape(BINS, probes + 1, BINS)
    return (products.transpose(1, 0, 2), gram.transpose(0, 2, 1))


def solution(mesh):
    in_specs = (
        P(("grp", "samp"), None),
        P(None, ("grp", "samp")),
        P(("grp", "samp")),
        P(),
        P(),
        P(),
    )
    out_specs = (P(None, None, ("grp", "samp")), P("grp", None, None))
    return jax.shard_map(shards, mesh=mesh, in_specs=in_specs, out_specs=out_specs, check_vma=False)
```

time: 235 us -> 44.1 us (0.19)
  blocking collectives: 81.7 us -> 0 us
  local copies, waits for them, and re-layouts: 59.5 us -> 1.88 us
  waiting for transfers between devices: 46.7 us -> 9.32 us
  matrix products: 26.7 us -> 0 us
  starting transfers between devices: 0.04 us -> 19.5 us
  between operations: 14.2 us -> 0.78 us
  Pallas kernels: 0 us -> 12.4 us
  other arithmetic: 5.82 us -> 0.11 us
    psum x1 -> x0, blocking collectives: 61 us -> none  [shards(): gram = lax.psum(local_gram, 'samp') / total]
    gather x4 -> x0, local copies, waits for them, and re-layouts: 48 us -> none  [the longest x2 24.4 us: shards(): picked = jnp.take(genotypes, order, axis=1).astype(jnp.float32)]
    reduce_scatter x1 -> x0, waiting for transfers between devices: 46.7 us -> none  [shards(): lax.psum_scatter(jnp.dot(standard.T, vectors.T, precision=lax.Precision.H...]
    dot_general x3 -> x0, matrix products: 26.7 us -> none  [the longest x1 12.3 us: shards(): jnp.dot(standard.T, vectors.T, precision=lax.Precision.HIGHEST, preferred...]
    all_gather x1 -> x0, blocking collectives: 20.7 us -> none  [shards(): scores = lax.all_gather(share, 'samp', axis=0, tiled=True)]
    ppermute x0 -> x15, starting transfers between devices: none -> 19.5 us  [exchange(): return lax.ppermute(x, 'samp', pairs)]
    pallas_call x0 -> x5, Pallas kernels: none -> 12.4 us  [the longest x2 4.96 us: sums(): pl.pallas_call(functools.partial(kernel, start=start, chunk=chunk), out_s...]
    unnamed x14 -> x11, local copies, waits for them, and re-layouts: 11.5 us -> 1.75 us
  transfers between devices with their start and end apart: 1 -> 15, of which waited for: 1 -> 8; matrix products, arithmetic and copies ran while one was open for 4% -> 0% of each run, Pallas kernels for 0% -> 17%
where the time goes in v3:
time: 44.1 us; the launch traced here: 43.9 us
  starting transfers between devices  19.5 us (44%)
  Pallas kernels  12.4 us (28%)
  waiting for transfers between devices  9.32 us (21%)
  local copies, waits for them, and re-layouts  1.88 us (4%)
  between operations  0.78 us (2%)
    ppermute x15, starting transfers between devices, exchange(): return lax.ppermute(x, 'samp', pairs)  19.5 us
    ppermute x15, waiting for transfers between devices, exchange(): return lax.ppermute(x, 'samp', pairs)  9.32 us
    pallas_call x2, Pallas kernels, sums(): pl.pallas_call(functools.partial(kernel, start=start, chunk=chunk), out_s...  4.96 us
    pallas_call x1, Pallas kernels, shards(): pl.pallas_call(functools.partial(own_kernel, norm=norm, gram_norm=gram_no...  3.62 us
    pallas_call x1, Pallas kernels, shards(): pl.pallas_call(functools.partial(other_kernel, norm=norm, gram_norm=gram_...  2.41 us
    unnamed x11, local copies, waits for them, and re-layouts  1.75 us
    pallas_call x1, Pallas kernels, shards(): pl.pallas_call(functools.partial(part_kernel, norm=norm), out_shape=part,...  1.38 us
  transfers between devices with their start and end apart: 15, of which 8 were waited for; matrix products, arithmetic and copies ran while one was open for 0% of the time, Pallas kernels for 17%

profile of v3, /device:TPU:0, one launch (start us, length us, event | category | flops | bytes accessed | tf_op | source)
XLA Modules:
  0.0 43.9 jit_solution(5266215164911523721)
XLA Ops:
  0.6 0.0 copy-start
  0.7 0.9 %copy-done = s32[32,1024]{1,0:T(8,128)S(1)} copy-done((s32[32,1024]{1,0:T(8,128)S(1)}, s32[32,1024]{1,0:T(8,128)}, u32[]{:S(2)}) %copy-start) | copy-done | bytes 131096
  1.5 0.0 copy-start.4
  1.5 2.4 %sums_first.1 = (f32[16,1152]{1,0:T(8,128)S(1)}, f32[16,1152]{1,0:T(8,128)S(1)}, bf16[1024,1024]{1,0:T(8,128)(2,1)S(1)}) custom-call(s32[1]{0:T(128)} %bitcast.side_ref, s32[1024,2048]{1,0:T(8,128)} %geno_hbm.3, s32[32,1024]{1,0:T(8,128)S(1)} %copy-done), custom_call_target="tpu_custom_call" | custom-call | flops 67108864 | bytes 6291456 | tf_op jit(solution)/shard_map/sums_first/pallas_call | solution.py:230
  4.0 0.5 %collective-permute-start.4 = (f32[16,1152]{1,0:T(8,128)S(1)}, f32[16,1152]{1,0:T(8,128)S(1)}, u32[]{:S(2)}, u32[]{:S(2)}) collective-permute-start(f32[16,1152]{1,0:T(8,128)S(1)} %get-tuple-element.20), channel_id=1, source_target_pairs={{0,1},{1,0},{2,3},{3,2},{4,5},{5,4},{6,7},{7,6},{8,9},{9,8},{10,11... | collective-permute-start | bytes 221192 | tf_op jit(solution)/shard_map/ppermute | solution.py:208
  4.5 0.0 copy-done.4
  4.5 0.0 copy-start.1
  4.5 0.0 copy-start.2
  4.5 0.0 copy-start.3
  4.5 2.5 %sums_second.1 = (f32[16,1280]{1,0:T(8,128)S(1)}, f32[16,1280]{1,0:T(8,128)S(1)}, bf16[1024,1024]{1,0:T(8,128)(2,1)S(1)}) custom-call(s32[1]{0:T(128)} %bitcast.side_ref, s32[1024,2048]{1,0:T(8,128)} %geno_hbm.3, s32[32,1024]{1,0:T(8,128)S(1)} %copy-done, f32[1,1024]{1,0:T(1,128)S(1)} %bitcast.16, bf16[1024,1024]{1,0:T(8,128)(2,1)S(1)} %get-tuple-element.16.first_ref.geno_a), custom_call_target="tpu_custom_call" | custom-call | flops 100663296 | bytes 6291456 | tf_op jit(solution)/shard_map/sums_second/pallas_call | solution.py:230
  7.1 0.1 collective-permute-start
  7.2 0.0 collective-permute-done.4
  7.2 2.7 %collective-permute-start.5 = (f32[16,1152]{1,0:T(8,128)S(1)}, f32[16,1152]{1,0:T(8,128)S(1)}, u32[]{:S(2)}, u32[]{:S(2)}) collective-permute-start(f32[16,1152]{1,0:T(8,128)S(1)} %add.42), channel_id=1, source_target_pairs={{0,3},{1,4},{2,7},{3,0},{4,1},{5,6},{6,5},{7,2},{8,13},{9,10},{10,... | collective-permute-start | bytes 221192 | tf_op jit(solution)/shard_map/ppermute | solution.py:208
  9.9 0.0 collective-permute-done
  9.9 1.2 %collective-permute-start.1 = (f32[16,1280]{1,0:T(8,128)S(1)}, f32[16,1280]{1,0:T(8,128)S(1)}, u32[]{:S(2)}, u32[]{:S(2)}) collective-permute-start(f32[16,1280]{1,0:T(8,128)S(1)} %add.39), channel_id=1, source_target_pairs={{0,3},{1,4},{2,7},{3,0},{4,1},{5,6},{6,5},{7,2},{8,13},{9,10},{10,... | collective-permute-start | bytes 245768 | tf_op jit(solution)/shard_map/ppermute | solution.py:208
  11.1 0.8 %collective-permute-done.5 = f32[16,1152]{1,0:T(8,128)S(1)} collective-permute-done((f32[16,1152]{1,0:T(8,128)S(1)}, f32[16,1152]{1,0:T(8,128)S(1)}, u32[]{:S(2)}, u32[]{:S(2)}) %collective-permute-start.5) | collective-permute-done | bytes 73760 | tf_op jit(solution)/shard_map/ppermute | solution.py:208
  11.9 2.2 %collective-permute-start.6 = (f32[16,1152]{1,0:T(8,128)S(1)}, f32[16,1152]{1,0:T(8,128)S(1)}, u32[]{:S(2)}, u32[]{:S(2)}) collective-permute-start(f32[16,1152]{1,0:T(8,128)S(1)} %add.43), channel_id=1, source_target_pairs={{0,5},{1,8},{2,11},{3,6},{4,13},{5,0},{6,3},{7,14},{8,1},{9,12},{1... | collective-permute-start | bytes 221192 | tf_op jit(solution)/shard_map/ppermute | solution.py:208
  14.1 0.0 collective-permute-done.1
  14.1 1.4 %collective-permute-start.2 = (f32[16,1280]{1,0:T(8,128)S(1)}, f32[16,1280]{1,0:T(8,128)S(1)}, u32[]{:S(2)}, u32[]{:S(2)}) collective-permute-start(f32[16,1280]{1,0:T(8,128)S(1)} %add.40), channel_id=1, source_target_pairs={{0,5},{1,8},{2,11},{3,6},{4,13},{5,0},{6,3},{7,14},{8,1},{9,12},{1... | collective-permute-start | bytes 245768 | tf_op jit(solution)/shard_map/ppermute | solution.py:208
  15.6 0.8 %collective-permute-done.6 = f32[16,1152]{1,0:T(8,128)S(1)} collective-permute-done((f32[16,1152]{1,0:T(8,128)S(1)}, f32[16,1152]{1,0:T(8,128)S(1)}, u32[]{:S(2)}, u32[]{:S(2)}) %collective-permute-start.6) | collective-permute-done | bytes 73760 | tf_op jit(solution)/shard_map/ppermute | solution.py:208
  16.3 3.1 %collective-permute-start.7 = (f32[16,1152]{1,0:T(8,128)S(1)}, f32[16,1152]{1,0:T(8,128)S(1)}, u32[]{:S(2)}, u32[]{:S(2)}) collective-permute-start(f32[16,1152]{1,0:T(8,128)S(1)} %add.44), channel_id=1, source_target_pairs={{0,9},{1,2},{2,1},{3,10},{4,7},{5,12},{6,15},{7,4},{8,11},{9,0},{1... | collective-permute-start | bytes 221192 | tf_op jit(solution)/shard_map/ppermute | solution.py:208
  19.4 0.0 collective-permute-done.2
  19.4 2.0 %collective-permute-start.3 = (f32[16,1280]{1,0:T(8,128)S(1)}, f32[16,1280]{1,0:T(8,128)S(1)}, u32[]{:S(2)}, u32[]{:S(2)}) collective-permute-start(f32[16,1280]{1,0:T(8,128)S(1)} %add.41), channel_id=1, source_target_pairs={{0,9},{1,2},{2,1},{3,10},{4,7},{5,12},{6,15},{7,4},{8,11},{9,0},{1... | collective-permute-start | bytes 245768 | tf_op jit(solution)/shard_map/ppermute | solution.py:208
  21.4 0.6 %collective-permute-done.7 = f32[16,1152]{1,0:T(8,128)S(1)} collective-permute-done((f32[16,1152]{1,0:T(8,128)S(1)}, f32[16,1152]{1,0:T(8,128)S(1)}, u32[]{:S(2)}, u32[]{:S(2)}) %collective-permute-start.7) | collective-permute-done | bytes 73760 | tf_op jit(solution)/shard_map/ppermute | solution.py:208
  22.0 0.1 collective-permute-start.8
  22.1 0.0 copy-done.1
  22.1 0.0 copy-done.2
  22.1 0.0 copy-done.3
  22.1 1.4 %products_part.1.part_ref = f32[256,1024]{1,0:T(8,128)S(1)} custom-call(f32[16,1152]{1,0:T(8,128)S(1)} %add.45.own_a, bf16[1024,1024]{1,0:T(8,128)(2,1)S(1)} %get-tuple-element.16.first_ref.geno_a, f32[1,2048]{1,0:T(1,128)S(1)} %bitcast.7, f32[1,2048]{1,0:T(1,128)S(1)} %bitcast.10, s32[1,2048]{1,0:T(1,128)S(1)} %bitcast.13), custom_call_target="tpu_custom_call" | custom-call | flops 1073741824 | bytes 1048576 | tf_op jit(solution)/shard_map/products_part/pallas_call | solution.py:273
  23.5 0.8 %collective-permute-done.3 = f32[16,1280]{1,0:T(8,128)S(1)} collective-permute-done((f32[16,1280]{1,0:T(8,128)S(1)}, f32[16,1280]{1,0:T(8,128)S(1)}, u32[]{:S(2)}, u32[]{:S(2)}) %collective-permute-start.3) | collective-permute-done | bytes 81952 | tf_op jit(solution)/shard_map/ppermute | solution.py:208
  24.3 0.6 %collective-permute-start.9 = (f32[16,1280]{1,0:T(8,128)S(1)}, f32[16,1280]{1,0:T(8,128)S(1)}, u32[]{:S(2)}, u32[]{:S(2)}) collective-permute-start(f32[16,1280]{1,0:T(8,128)S(1)} %add.46.own_b), channel_id=1, source_target_pairs={{0,1},{1,0},{2,3},{3,2},{4,5},{5,4},{6,7},{7,6},{8,9},{9,8},{10,11... | collective-permute-start | bytes 245768 | tf_op jit(solution)/shard_map/ppermute | solution.py:208
  24.9 0.0 collective-permute-done.8.other_a
  24.9 3.6 %products_own.1 = (f32[33,16,1024]{2,1,0:T(8,128)}, f32[16,384]{1,0:T(8,128)S(1)}, f32[256,1024]{1,0:T(8,128)S(1)}) custom-call(s32[1]{0:T(128)} %bitcast.side_ref, f32[256,1024]{1,0:T(8,128)S(1)} %products_part.1.part_ref, f32[16,1152]{1,0:T(8,128)S(1)} %collective-permute-done.8.other_a, f32[16,1280]{1,0:T(8,128)S(1)} %add.46.own_b, ...), custom_call_target="tpu_custom_call" | custom-call | flops 2147483648 | bytes 1048576 | tf_op jit(solution)/shard_map/products_own/pallas_call | solution.py:286
  28.5 0.0 collective-permute-done.9.other_b
  28.5 2.4 %products_other.1 = (f32[33,16,1024]{2,1,0:T(8,128)}, f32[16,640]{1,0:T(8,128)S(1)}) custom-call(s32[1]{0:T(128)} %bitcast.side_ref, f32[256,1024]{1,0:T(8,128)S(1)} %get-tuple-element.25.part_ref, f32[16,1280]{1,0:T(8,128)S(1)} %collective-permute-done.9.other_b, bf16[1024,1024]{1,0:T(8,128)(2,1)S(1)} %get-tuple-element.24.geno_b, ...), custom_call_target="tpu_custom_call", output_to_operand_aliasing={{0}: (8, {})} | custom-call | flops 1073741824 | bytes 1048576 | tf_op jit(solution)/shard_map/products_other/pallas_call | solution.py:300
  30.9 0.1 collective-permute-start.10
  31.0 1.2 %collective-permute-done.10 = f32[16,640]{1,0:T(8,128)S(1)} collective-permute-done((f32[16,640]{1,0:T(8,128)S(1)}, f32[16,640]{1,0:T(8,128)S(1)}, u32[]{:S(2)}, u32[]{:S(2)}) %collective-permute-start.10) | collective-permute-done | bytes 40992 | tf_op jit(solution)/shard_map/ppermute | solution.py:208
  32.2 2.7 %collective-permute-start.13 = (f32[16,640]{1,0:T(8,128)S(1)}, f32[16,640]{1,0:T(8,128)S(1)}, u32[]{:S(2)}, u32[]{:S(2)}) collective-permute-start(f32[16,640]{1,0:T(8,128)S(1)} %add.47), channel_id=1, source_target_pairs={{0,7},{1,6},{2,5},{3,4},{4,3},{5,2},{6,1},{7,0},{8,15},{9,14},{10,... | collective-permute-start | bytes 122888 | tf_op jit(solution)/shard_map/ppermute | solution.py:208
  34.9 0.0 collective-permute-start.12
  34.9 0.4 collective-permute-start.11
  35.3 1.5 %collective-permute-done.13 = f32[16,640]{1,0:T(8,128)S(1)} collective-permute-done((f32[16,640]{1,0:T(8,128)S(1)}, f32[16,640]{1,0:T(8,128)S(1)}, u32[]{:S(2)}, u32[]{:S(2)}) %collective-permute-start.13) | collective-permute-done | bytes 40992 | tf_op jit(solution)/shard_map/ppermute | solution.py:208
  36.8 1.6 %collective-permute-done.12 = f32[16,640]{1,0:T(8,128)S(1)} collective-permute-done((f32[16,640]{1,0:T(8,128)S(1)}, f32[16,640]{1,0:T(8,128)S(1)}, u32[]{:S(2)}, u32[]{:S(2)}) %collective-permute-start.12) | collective-permute-done | bytes 40992 | tf_op jit(solution)/shard_map/ppermute | solution.py:208
  38.5 0.0 collective-permute-done.11
  38.5 2.4 %collective-permute-start.14 = (f32[16,640]{1,0:T(8,128)S(1)}, f32[16,640]{1,0:T(8,128)S(1)}, u32[]{:S(2)}, u32[]{:S(2)}) collective-permute-start(f32[16,640]{1,0:T(8,128)S(1)} %add_add_fusion), channel_id=1, source_target_pairs={{0,9},{1,8},{2,11},{3,10},{4,13},{5,12},{6,15},{7,14},{8,1},{9,0},... | collective-permute-start | bytes 122888 | tf_op jit(solution)/shard_map/ppermute | solution.py:208
  40.9 2.1 %collective-permute-done.14 = f32[16,640]{1,0:T(8,128)S(1)} collective-permute-done((f32[16,640]{1,0:T(8,128)S(1)}, f32[16,640]{1,0:T(8,128)S(1)}, u32[]{:S(2)}, u32[]{:S(2)}) %collective-permute-start.14) | collective-permute-done | bytes 40992 | tf_op jit(solution)/shard_map/ppermute | solution.py:208
  43.0 0.1 reshape.27
  43.1 0.8 %copy.10 = f32[16,16,33]{2,1,0:T(8,128)} copy(f32[16,16,33]{1,2,0:T(8,128)S(1)} %bitcast.18) | data formatting | bytes 67584
  (11 shorter events, 0.1 us)
Async XLA Ops:
  0.6 0.9 %copy-start = (s32[32,1024]{1,0:T(8,128)S(1)}, s32[32,1024]{1,0:T(8,128)}, u32[]{:S(2)}) copy-start(s32[32,1024]{1,0:T(8,128)} %signs_ref.3) | copy-start | bytes 393220
  1.5 3.0 %copy-start.4 = (f32[1024]{0:T(1024)S(1)}, f32[1024]{0:T(1024)}, u32[]{:S(2)}) copy-start(f32[1024]{0:T(1024)} %param.8) | copy-start | bytes 12292
  4.0 3.2 %collective-permute-start.4 = (f32[16,1152]{1,0:T(8,128)S(1)}, f32[16,1152]{1,0:T(8,128)S(1)}, u32[]{:S(2)}, u32[]{:S(2)}) collective-permute-start(f32[16,1152]{1,0:T(8,128)S(1)} %get-tuple-element.20), channel_id=1, source_target_pairs={{0,1},{1,0},{2,3},{3,2},{4,5},{5,4},{6,7},{7,6},{8,9},{9,8},{10,11... | collective-permute-start | bytes 221192 | tf_op jit(solution)/shard_map/ppermute | solution.py:208
  4.5 17.6 %copy-start.1 = (f32[2048]{0:T(1024)S(1)}, f32[2048]{0:T(1024)}, u32[]{:S(2)}) copy-start(f32[2048]{0:T(1024)} %param.9) | copy-start | bytes 24580
  4.5 17.6 %copy-start.2 = (f32[2048]{0:T(1024)S(1)}, f32[2048]{0:T(1024)}, u32[]{:S(2)}) copy-start(f32[2048]{0:T(1024)} %param.10) | copy-start | bytes 24580
  4.5 17.6 %copy-start.3 = (s32[2048]{0:T(1024)S(1)}, s32[2048]{0:T(1024)}, u32[]{:S(2)}) copy-start(s32[2048]{0:T(1024)} %param.11) | copy-start | bytes 24580
  7.1 2.8 %collective-permute-start = (f32[16,1280]{1,0:T(8,128)S(1)}, f32[16,1280]{1,0:T(8,128)S(1)}, u32[]{:S(2)}, u32[]{:S(2)}) collective-permute-start(f32[16,1280]{1,0:T(8,128)S(1)} %get-tuple-element.18), channel_id=1, source_target_pairs={{0,1},{1,0},{2,3},{3,2},{4,5},{5,4},{6,7},{7,6},{8,9},{9,8},{10,11... | collective-permute-start | bytes 245768 | tf_op jit(solution)/shard_map/ppermute | solution.py:208
  7.2 4.7 %collective-permute-start.5 = (f32[16,1152]{1,0:T(8,128)S(1)}, f32[16,1152]{1,0:T(8,128)S(1)}, u32[]{:S(2)}, u32[]{:S(2)}) collective-permute-start(f32[16,1152]{1,0:T(8,128)S(1)} %add.42), channel_id=1, source_target_pairs={{0,3},{1,4},{2,7},{3,0},{4,1},{5,6},{6,5},{7,2},{8,13},{9,10},{10,... | collective-permute-start | bytes 221192 | tf_op jit(solution)/shard_map/ppermute | solution.py:208
  9.9 4.2 %collective-permute-start.1 = (f32[16,1280]{1,0:T(8,128)S(1)}, f32[16,1280]{1,0:T(8,128)S(1)}, u32[]{:S(2)}, u32[]{:S(2)}) collective-permute-start(f32[16,1280]{1,0:T(8,128)S(1)} %add.39), channel_id=1, source_target_pairs={{0,3},{1,4},{2,7},{3,0},{4,1},{5,6},{6,5},{7,2},{8,13},{9,10},{10,... | collective-permute-start | bytes 245768 | tf_op jit(solution)/shard_map/ppermute | solution.py:208
  11.9 4.4 %collective-permute-start.6 = (f32[16,1152]{1,0:T(8,128)S(1)}, f32[16,1152]{1,0:T(8,128)S(1)}, u32[]{:S(2)}, u32[]{:S(2)}) collective-permute-start(f32[16,1152]{1,0:T(8,128)S(1)} %add.43), channel_id=1, source_target_pairs={{0,5},{1,8},{2,11},{3,6},{4,13},{5,0},{6,3},{7,14},{8,1},{9,12},{1... | collective-permute-start | bytes 221192 | tf_op jit(solution)/shard_map/ppermute | solution.py:208
  14.1 5.3 %collective-permute-start.2 = (f32[16,1280]{1,0:T(8,128)S(1)}, f32[16,1280]{1,0:T(8,128)S(1)}, u32[]{:S(2)}, u32[]{:S(2)}) collective-permute-start(f32[16,1280]{1,0:T(8,128)S(1)} %add.40), channel_id=1, source_target_pairs={{0,5},{1,8},{2,11},{3,6},{4,13},{5,0},{6,3},{7,14},{8,1},{9,12},{1... | collective-permute-start | bytes 245768 | tf_op jit(solution)/shard_map/ppermute | solution.py:208
  16.3 5.6 %collective-permute-start.7 = (f32[16,1152]{1,0:T(8,128)S(1)}, f32[16,1152]{1,0:T(8,128)S(1)}, u32[]{:S(2)}, u32[]{:S(2)}) collective-permute-start(f32[16,1152]{1,0:T(8,128)S(1)} %add.44), channel_id=1, source_target_pairs={{0,9},{1,2},{2,1},{3,10},{4,7},{5,12},{6,15},{7,4},{8,11},{9,0},{1... | collective-permute-start | bytes 221192 | tf_op jit(solution)/shard_map/ppermute | solution.py:208
  19.4 4.8 %collective-permute-start.3 = (f32[16,1280]{1,0:T(8,128)S(1)}, f32[16,1280]{1,0:T(8,128)S(1)}, u32[]{:S(2)}, u32[]{:S(2)}) collective-permute-start(f32[16,1280]{1,0:T(8,128)S(1)} %add.41), channel_id=1, source_target_pairs={{0,9},{1,2},{2,1},{3,10},{4,7},{5,12},{6,15},{7,4},{8,11},{9,0},{1... | collective-permute-start | bytes 245768 | tf_op jit(solution)/shard_map/ppermute | solution.py:208
  22.0 2.9 %collective-permute-start.8 = (f32[16,1152]{1,0:T(8,128)S(1)}, f32[16,1152]{1,0:T(8,128)S(1)}, u32[]{:S(2)}, u32[]{:S(2)}) collective-permute-start(f32[16,1152]{1,0:T(8,128)S(1)} %add.45.own_a), channel_id=1, source_target_pairs={{0,1},{1,0},{2,3},{3,2},{4,5},{5,4},{6,7},{7,6},{8,9},{9,8},{10,11... | collective-permute-start | bytes 221192 | tf_op jit(solution)/shard_map/ppermute | solution.py:208
  24.3 4.2 %collective-permute-start.9 = (f32[16,1280]{1,0:T(8,128)S(1)}, f32[16,1280]{1,0:T(8,128)S(1)}, u32[]{:S(2)}, u32[]{:S(2)}) collective-permute-start(f32[16,1280]{1,0:T(8,128)S(1)} %add.46.own_b), channel_id=1, source_target_pairs={{0,1},{1,0},{2,3},{3,2},{4,5},{5,4},{6,7},{7,6},{8,9},{9,8},{10,11... | collective-permute-start | bytes 245768 | tf_op jit(solution)/shard_map/ppermute | solution.py:208
  30.9 1.3 %collective-permute-start.10 = (f32[16,640]{1,0:T(8,128)S(1)}, f32[16,640]{1,0:T(8,128)S(1)}, u32[]{:S(2)}, u32[]{:S(2)}) collective-permute-start(f32[16,640]{1,0:T(8,128)S(1)} %get-tuple-element.29), channel_id=1, source_target_pairs={{0,1},{1,0},{2,3},{3,2},{4,5},{5,4},{6,7},{7,6},{8,9},{9,8},{10,11... | collective-permute-start | bytes 122888 | tf_op jit(solution)/shard_map/ppermute | solution.py:208
  32.2 4.6 %collective-permute-start.13 = (f32[16,640]{1,0:T(8,128)S(1)}, f32[16,640]{1,0:T(8,128)S(1)}, u32[]{:S(2)}, u32[]{:S(2)}) collective-permute-start(f32[16,640]{1,0:T(8,128)S(1)} %add.47), channel_id=1, source_target_pairs={{0,7},{1,6},{2,5},{3,4},{4,3},{5,2},{6,1},{7,0},{8,15},{9,14},{10,... | collective-permute-start | bytes 122888 | tf_op jit(solution)/shard_map/ppermute | solution.py:208
  34.9 3.5 %collective-permute-start.12 = (f32[16,640]{1,0:T(8,128)S(1)}, f32[16,640]{1,0:T(8,128)S(1)}, u32[]{:S(2)}, u32[]{:S(2)}) collective-permute-start(f32[16,640]{1,0:T(8,128)S(1)} %add.47), channel_id=1, source_target_pairs={{0,5},{1,4},{2,7},{3,6},{4,1},{5,0},{6,3},{7,2},{8,13},{9,12},{10,... | collective-permute-start | bytes 122888 | tf_op jit(solution)/shard_map/ppermute | solution.py:208
  34.9 3.5 %collective-permute-start.11 = (f32[16,640]{1,0:T(8,128)S(1)}, f32[16,640]{1,0:T(8,128)S(1)}, u32[]{:S(2)}, u32[]{:S(2)}) collective-permute-start(f32[16,640]{1,0:T(8,128)S(1)} %add.47), channel_id=1, source_target_pairs={{0,3},{1,2},{2,1},{3,0},{4,7},{5,6},{6,5},{7,4},{8,11},{9,10},{10,... | collective-permute-start | bytes 122888 | tf_op jit(solution)/shard_map/ppermute | solution.py:208
  38.5 4.5 %collective-permute-start.14 = (f32[16,640]{1,0:T(8,128)S(1)}, f32[16,640]{1,0:T(8,128)S(1)}, u32[]{:S(2)}, u32[]{:S(2)}) collective-permute-start(f32[16,640]{1,0:T(8,128)S(1)} %add_add_fusion), channel_id=1, source_target_pairs={{0,9},{1,8},{2,11},{3,10},{4,13},{5,12},{6,15},{7,14},{8,1},{9,0},... | collective-permute-start | bytes 122888 | tf_op jit(solution)/shard_map/ppermute | solution.py:208

commit v4 on v3

--- a/solution.py
+++ b/solution.py
@@ -13,6 +13,7 @@
 F32 = jnp.float32
 BF16 = jnp.bfloat16
 MIB = 2**20
+PIECES = 2
 
 dot_nt = functools.partial(lax.dot_general, dimension_numbers=(((1,), (1,)), ((), ())), preferred_element_type=F32)
 
@@ -115,7 +116,7 @@
         at = ref.shape[1] - LANES
         return [self.scores(ref[r : r + 1, :markers], ref[:1, at + r : at + r + 1]) for r in range(ref.shape[0])]
 
-    def products(self, rows, weights):
+    def weigh(self, rows, weights):
         shifts = []
         count = len(rows) * BINS
         for r, row in enumerate(rows):
@@ -124,8 +125,16 @@
             hi, lo = two_parts(weighted)
             weights[r * BINS : (r + 1) * BINS, :] = hi
             weights[count + r * BINS : count + (r + 1) * BINS, :] = lo
-        both = dot_nt(weights[: 2 * count, :], self.geno[...])
-        return both[:count] + both[count:] - jnp.concatenate(shifts, axis=0)
+        return jnp.concatenate(shifts, axis=0)
+
+    def multiply(self, weights, span=slice(None)):
+        both = dot_nt(weights[...], self.geno[span, :])
+        count = both.shape[0] // 2
+        return both[:count] + both[count:]
+
+    def products(self, rows, weights):
+        shift = self.weigh(rows, weights)
+        return self.multiply(weights) - shift
 
 
 def square_of(products):
@@ -136,15 +145,42 @@
 
 
 def gram_of(products, gram_norm):
+    column = lax.broadcasted_iota(jnp.int32, (BINS, LANES), 1)
     parts = []
-    column = lax.broadcasted_iota(jnp.int32, (BINS, LANES), 1) // BINS
     for g in range(products.shape[0] // LANES):
         square = square_of(products[g * LANES : (g + 1) * LANES])
         total = square[:BINS]
         for r in range(1, GROUP):
-            total = jnp.where(column == r, square[r * BINS : (r + 1) * BINS], total)
+            total = jnp.where(column // BINS == r, square[r * BINS : (r + 1) * BINS], total)
         parts.append(total * gram_norm)
-    return jnp.concatenate(parts, axis=1)
+    h = BINS // 2
+    packed = []
+    for one, two in zip(parts[::2], parts[1::2]):
+        moved = pltpu.roll(two[h:], LANES - h, 1)
+        packed += [one[:h], two[:h], jnp.where(column[:h] % BINS >= h, one[h:], moved)]
+    return jnp.concatenate(packed, axis=1)
+
+
+def unpack_kernel(one_ref, two_ref, out_ref, upper, lower, *, pairs):
+    h = BINS // 2
+    count = upper.shape[0] // BINS
+    packed = one_ref[...] + two_ref[...]
+    tile = [packed[:, t * LANES : (t + 1) * LANES] for t in range(packed.shape[1] // LANES)]
+    for p in range(pairs):
+        one, two, low = tile[3 * p : 3 * p + 3]
+        for i, (a, b) in enumerate(((one, low), (two, pltpu.roll(low, h, 1)))):
+            at = (2 * p + i) * LANES
+            upper[at : at + LANES, :] = a.T
+            lower[at : at + LANES, :] = b.T
+    last = tile[3 * pairs].T
+    upper[2 * pairs * LANES :, :] = last[:BINS]
+    lower[2 * pairs * LANES :, :] = last[BINS : 2 * BINS]
+    for l in range(BINS):
+        row = upper[pl.ds(l, count, stride=BINS), :].T
+        out_ref[:h, l, :] = row
+        if l >= h:
+            out_ref[l, :h, :] = row
+            out_ref[h:, l, :] = lower[pl.ds(l, count, stride=BINS), :].T
 
 
 def part_kernel(own_a, geno_a, mean_ref, scale_ref, bin_ref, part_ref, weights, *, norm):
@@ -152,7 +188,7 @@
     part_ref[...] = first.products(first.probe_scores(own_a), weights)
 
 
-def own_kernel(side_ref, part_ref, other_a, own_b, geno_a, geno_b, mean_ref, scale_ref, bin_ref, out_ref, gram_ref, other_ref, weights, prod, sems, *, norm, gram_norm):
+def own_kernel(side_ref, part_ref, other_a, own_b, geno_a, geno_b, mean_ref, scale_ref, bin_ref, out_ref, gram_ref, other_ref, last_ref, weights, prod, sems, *, norm, gram_norm):
     half = own_b.shape[0]
     count = half * BINS
     markers = geno_a.shape[1]
@@ -166,37 +202,47 @@
     rows_a = first.probe_scores(other_a) + [first.scores(jnp.concatenate(pheno[:tiles], axis=1), total)]
     parts_b = second.products(rows_b, weights.at[0])
     mine = part_ref[...] + parts_b[:count]
-    prod[:half] = mine.reshape(half, BINS, samples)
-    copies = [pltpu.make_async_copy(prod.at[pl.ds(0, half)], out_ref.at[pl.ds(pl.multiple_of(side_ref[0] * half, half), half)], sems.at[0])]
-    copies[0].start()
-    gram_ref[:, : half * BINS] = gram_of(mine, gram_norm)
+    prod[...] = mine.reshape(half, BINS, samples)
+    copy = pltpu.make_async_copy(prod, out_ref.at[pl.ds(pl.multiple_of(side_ref[0] * half, half), half)], sems.at[0])
+    copy.start()
+    probe_gram = gram_of(mine, gram_norm)
+    gram_ref[:, : probe_gram.shape[1]] = probe_gram
     parts_a = first.products(rows_a, weights.at[1])
     other_ref[...] = parts_a[:count]
     last = parts_a[count:] + parts_b[count:]
-    prod[half : half + 1] = last.reshape(1, BINS, samples)
-    copies.append(pltpu.make_async_copy(prod.at[pl.ds(half, 1)], out_ref.at[pl.ds(2 * half, 1)], sems.at[1]))
-    copies[1].start()
-    gram_ref[:, half * BINS : (half + 1) * BINS] = square_of(last) * gram_norm
-    gram_ref[:, (half + 1) * BINS :] = jnp.zeros((BINS, LANES - BINS), F32)
-    for copy in copies:
-        copy.wait()
-
-
-def other_kernel(side_ref, part_ref, other_b, geno_b, mean_ref, scale_ref, bin_ref, own_gram_ref, _, out_ref, gram_ref, weights, prod, sems, *, norm, gram_norm):
+    last_ref[0] = last
+    square = square_of(last) * gram_norm
+    h = BINS // 2
+    rest = jnp.zeros((h, LANES - 2 * BINS), F32)
+    gram_ref[:, probe_gram.shape[1] :] = jnp.concatenate([square[:h], square[h:], rest], axis=1)
+    copy.wait()
+
+
+def other_kernel(side_ref, part_ref, last_ref, other_b, geno_b, mean_ref, scale_ref, bin_ref, own_gram_ref, _, out_ref, gram_ref, weights, prod, sems, *, norm, gram_norm):
     half = other_b.shape[0]
     wide = half * BINS
     samples, markers = geno_b.shape
     side = side_ref[0]
+    copies = [pltpu.make_async_copy(last_ref, out_ref.at[pl.ds(2 * half, 1)], sems.at[0])]
+    copies[0].start()
     second = Half(mean_ref, scale_ref, bin_ref, geno_b, markers, norm)
-    rows = second.probe_scores(other_b)
-    products = part_ref[...] + second.products(rows, weights)
-    prod[...] = products.reshape(half, BINS, samples)
-    copy = pltpu.make_async_copy(prod, out_ref.at[pl.ds(pl.multiple_of((1 - side) * half, half), half)], sems.at[0])
-    copy.start()
-    gram_ref[:, pl.ds(pl.multiple_of((1 - side) * wide, wide), wide)] = gram_of(products, gram_norm)
-    gram_ref[:, pl.ds(pl.multiple_of(side * wide, wide), wide)] = own_gram_ref[:, :wide]
-    gram_ref[:, 2 * wide :] = own_gram_ref[:, wide:]
-    copy.wait()
+    shift = second.weigh(second.probe_scores(other_b), weights)
+    pieces = sems.shape[0] - 1
+    width = samples // pieces
+    for p in range(pieces):
+        span = slice(p * width, (p + 1) * width)
+        products = part_ref[:, span] + (second.multiply(weights, span) - shift)
+        prod[:, :, span] = products.reshape(half, BINS, width)
+        to = out_ref.at[pl.ds(pl.multiple_of((1 - side) * half, half), half), :, span]
+        copies.append(pltpu.make_async_copy(prod.at[:, :, span], to, sems.at[p + 1]))
+        copies[-1].start()
+    gram = gram_of(prod[...].reshape(wide, samples), gram_norm)
+    packed = gram.shape[1]
+    gram_ref[:, pl.ds(pl.multiple_of((1 - side) * packed, packed), packed)] = gram
+    gram_ref[:, pl.ds(pl.multiple_of(side * packed, packed), packed)] = own_gram_ref[:, :packed]
+    gram_ref[:, 2 * packed :] = own_gram_ref[:, packed:]
+    for copy in copies:
+        copy.wait()
 
 
 def parity(i):
@@ -222,7 +268,7 @@
     hbm = pl.BlockSpec(memory_space=pl.ANY)
 
     width = markers // 2
-    chunk = min(samples, 256)
+    chunk = min(samples, 128)
     narrow = jax.ShapeDtypeStruct((samples, width), BF16)
 
     def sums(kernel, start, name, extra, rows, *operands):
@@ -249,17 +295,18 @@
     )
     own_a = own_a + exchange(other_a, 1)
     own_b = own_b + exchange(other_b, 1)
+    swapped = flips[1:2] + flips[:1] + flips[2:]
     received = None
-    for s in range(len(flips)):
-        even, odd = flips[s] | 1, flips[(s + 1) % len(flips)] | 1
-        own_a = own_a + exchange(own_a, even, odd)
+    for a_even, a_odd, b_even, b_odd in zip(flips, flips[1:] + flips[:1], swapped, flips[::-1]):
+        own_a = own_a + exchange(own_a, a_even | 1, a_odd | 1)
         if received is not None:
             own_b = own_b + received
-        received = exchange(own_b, even, odd)
+        received = exchange(own_b, b_even | 1, b_odd | 1)
 
     norm = (total * (markers // BINS)) ** -0.5
     gram_norm = 1.0 / total
     rows = half * BINS
+    packed = rows // LANES * 3 * LANES // 2
 
     def work(count):
         return pl.CostEstimate(flops=4 * count * samples * width, bytes_accessed=4 * rows * samples, transcendentals=0)
@@ -283,15 +330,15 @@
     own_b, received, own_part = lax.optimization_barrier((own_b, received, own_part))
     own_b = own_b + received
     other_b = exchange(own_b, 1)
-    products, gram, other_part = pl.pallas_call(
+    products, gram, other_part, last = pl.pallas_call(
         functools.partial(own_kernel, norm=norm, gram_norm=gram_norm),
-        out_shape=(products, jax.ShapeDtypeStruct((BINS, rows + LANES), F32), part),
+        out_shape=(products, jax.ShapeDtypeStruct((BINS // 2, packed + LANES), F32), part, jax.ShapeDtypeStruct((1, BINS, samples), F32)),
         in_specs=[smem] + [vmem] * 8,
-        out_specs=(hbm, vmem, vmem),
+        out_specs=(hbm, vmem, vmem, vmem),
         scratch_shapes=[
             pltpu.VMEM((2, 2 * (rows + BINS), width), BF16),
-            pltpu.VMEM((half + 1, BINS, samples), F32),
-            pltpu.SemaphoreType.DMA((2,)),
+            pltpu.VMEM((half, BINS, samples), F32),
+            pltpu.SemaphoreType.DMA((1,)),
         ],
         cost_estimate=work(2 * rows),
         compiler_params=params,
@@ -299,27 +346,34 @@
     )(side, own_part, other_a, own_b, narrow_a, narrow_b, *markers_info)
     products, gram = pl.pallas_call(
         functools.partial(other_kernel, norm=norm, gram_norm=gram_norm),
-        out_shape=(products, jax.ShapeDtypeStruct((BINS, 2 * rows + LANES), F32)),
-        in_specs=[smem] + [vmem] * 7 + [hbm],
+        out_shape=(products, jax.ShapeDtypeStruct((BINS // 2, 2 * packed + LANES), F32)),
+        in_specs=[smem] + [vmem] * 8 + [hbm],
         out_specs=(hbm, vmem),
-        scratch_shapes=[weights, pltpu.VMEM((half, BINS, samples), F32), pltpu.SemaphoreType.DMA((1,))],
-        input_output_aliases={8: 0},
+        scratch_shapes=[weights, pltpu.VMEM((half, BINS, samples), F32), pltpu.SemaphoreType.DMA((PIECES + 1,))],
+        input_output_aliases={9: 0},
         cost_estimate=work(rows),
         compiler_params=params,
         name="products_other",
-    )(side, other_part, other_b, narrow_b, *markers_info, gram, products)
+    )(side, other_part, last, other_b, narrow_b, *markers_info, gram, products)
 
     gram = gram + exchange(gram, 1)
     rest = flips
-    while rest:
-        if len(rest) > 1:
-            near, far, both = (exchange(gram, f | 1) for f in (rest[0], rest[1], rest[0] | rest[1]))
-            gram = (gram + near) + (far + both)
-        else:
-            gram = gram + exchange(gram, rest[0] | 1)
+    while len(rest) > 1:
+        near, far, both = (exchange(gram, f | 1) for f in (rest[0], rest[1], rest[0] | rest[1]))
+        gram = (gram + near) + (far + both)
         rest = rest[2:]
-    gram = gram[:, : (probes + 1) * BINS].reshape(BINS, probes + 1, BINS)
-    return (products.transpose(1, 0, 2), gram.transpose(0, 2, 1))
+    last = exchange(gram, rest[0] | 1) if rest else jnp.zeros_like(gram)
+    count = (probes + 1) * BINS
+    gram = pl.pallas_call(
+        functools.partial(unpack_kernel, pairs=2 * rows // (2 * LANES)),
+        out_shape=jax.ShapeDtypeStruct((BINS, BINS, probes + 1), F32),
+        in_specs=[vmem, vmem],
+        out_specs=vmem,
+        scratch_shapes=[pltpu.VMEM((count, BINS // 2), F32), pltpu.VMEM((count, BINS // 2), F32)],
+        compiler_params=pltpu.CompilerParams(vmem_limit_bytes=16 * MIB),
+        name="gram_unpack",
+    )(gram, last)
+    return (products.transpose(1, 0, 2), gram)
 
 
 def solution(mesh):

time: 44.1 us -> 42.9 us (0.973)
  local copies, waits for them, and re-layouts: 1.88 us -> 0.91 us
  waiting for transfers between devices: 9.32 us -> 8.69 us
  Pallas kernels: 12.4 us -> 13 us
    pallas_call x0 -> x1, Pallas kernels: none -> 1.12 us  [shards(): pl.pallas_call(functools.partial(unpack_kernel, pairs=2 * rows // (2 * LA...]
    unnamed x11 -> x10, local copies, waits for them, and re-layouts: 1.75 us -> 0.91 us
    ppermute x15, waiting for transfers between devices: 9.32 us -> 8.69 us  [exchange(): return lax.ppermute(x, 'samp', pairs)]
  transfers between devices with their start and end apart: 15 -> 15, of which waited for: 8 -> 9; matrix products, arithmetic and copies ran while one was open for 0% -> 0% of each run, Pallas kernels for 17% -> 17%
where the time goes in v4:
time: 42.9 us; the launch traced here: 42.7 us
  starting transfers between devices  19.3 us (45%)
  Pallas kernels  13 us (30%)
  waiting for transfers between devices  8.69 us (20%)
  local copies, waits for them, and re-layouts  0.91 us (2%)
  between operations  0.75 us (2%)
    ppermute x15, starting transfers between devices, exchange(): return lax.ppermute(x, 'samp', pairs)  19.3 us
    ppermute x15, waiting for transfers between devices, exchange(): return lax.ppermute(x, 'samp', pairs)  8.69 us
    pallas_call x2, Pallas kernels, sums(): pl.pallas_call(functools.partial(kernel, start=start, chunk=chunk), out_s...  4.96 us
    pallas_call x1, Pallas kernels, shards(): pl.pallas_call(functools.partial(own_kernel, norm=norm, gram_norm=gram_no...  3.28 us
    pallas_call x1, Pallas kernels, shards(): pl.pallas_call(functools.partial(other_kernel, norm=norm, gram_norm=gram_...  2.23 us
    pallas_call x1, Pallas kernels, shards(): pl.pallas_call(functools.partial(part_kernel, norm=norm), out_shape=part,...  1.39 us
    pallas_call x1, Pallas kernels, shards(): pl.pallas_call(functools.partial(unpack_kernel, pairs=2 * rows // (2 * LA...  1.12 us
    unnamed x10, local copies, waits for them, and re-layouts  0.91 us
  transfers between devices with their start and end apart: 15, of which 9 were waited for; matrix products, arithmetic and copies ran while one was open for 0% of the time, Pallas kernels for 17%

profile of v4, /device:TPU:0, one launch (start us, length us, event | category | flops | bytes accessed | tf_op | source)
XLA Modules:
  0.0 42.7 jit_solution(10880594600664232718)
XLA Ops:
  0.6 0.0 copy-start
  0.7 0.9 %copy-done = s32[32,1024]{1,0:T(8,128)S(1)} copy-done((s32[32,1024]{1,0:T(8,128)S(1)}, s32[32,1024]{1,0:T(8,128)}, u32[]{:S(2)}) %copy-start) | copy-done | bytes 131096
  1.5 0.0 copy-start.4
  1.5 2.4 %sums_first.1 = (f32[16,1152]{1,0:T(8,128)S(1)}, f32[16,1152]{1,0:T(8,128)S(1)}, bf16[1024,1024]{1,0:T(8,128)(2,1)S(1)}) custom-call(s32[1]{0:T(128)} %bitcast.side_ref, s32[1024,2048]{1,0:T(8,128)} %geno_hbm.3, s32[32,1024]{1,0:T(8,128)S(1)} %copy-done), custom_call_target="tpu_custom_call" | custom-call | flops 67108864 | bytes 6291456 | tf_op jit(solution)/shard_map/sums_first/pallas_call | solution.py:276
  4.0 0.5 %collective-permute-start.4 = (f32[16,1152]{1,0:T(8,128)S(1)}, f32[16,1152]{1,0:T(8,128)S(1)}, u32[]{:S(2)}, u32[]{:S(2)}) collective-permute-start(f32[16,1152]{1,0:T(8,128)S(1)} %get-tuple-element.21), channel_id=1, source_target_pairs={{0,1},{1,0},{2,3},{3,2},{4,5},{5,4},{6,7},{7,6},{8,9},{9,8},{10,11... | collective-permute-start | bytes 221192 | tf_op jit(solution)/shard_map/ppermute | solution.py:254
  4.5 0.0 copy-done.4
  4.5 0.0 copy-start.1
  4.5 0.0 copy-start.2
  4.5 0.0 copy-start.3
  4.5 2.5 %sums_second.1 = (f32[16,1280]{1,0:T(8,128)S(1)}, f32[16,1280]{1,0:T(8,128)S(1)}, bf16[1024,1024]{1,0:T(8,128)(2,1)S(1)}) custom-call(s32[1]{0:T(128)} %bitcast.side_ref, s32[1024,2048]{1,0:T(8,128)} %geno_hbm.3, s32[32,1024]{1,0:T(8,128)S(1)} %copy-done, f32[1,1024]{1,0:T(1,128)S(1)} %bitcast.15, bf16[1024,1024]{1,0:T(8,128)(2,1)S(1)} %get-tuple-element.17.first_ref.geno_a), custom_call_target="tpu_custom_call" | custom-call | flops 100663296 | bytes 6291456 | tf_op jit(solution)/shard_map/sums_second/pallas_call | solution.py:276
  7.1 0.1 collective-permute-start
  7.2 0.0 collective-permute-done.4
  7.2 2.7 %collective-permute-start.5 = (f32[16,1152]{1,0:T(8,128)S(1)}, f32[16,1152]{1,0:T(8,128)S(1)}, u32[]{:S(2)}, u32[]{:S(2)}) collective-permute-start(f32[16,1152]{1,0:T(8,128)S(1)} %add.39), channel_id=1, source_target_pairs={{0,3},{1,4},{2,7},{3,0},{4,1},{5,6},{6,5},{7,2},{8,13},{9,10},{10,... | collective-permute-start | bytes 221192 | tf_op jit(solution)/shard_map/ppermute | solution.py:254
  9.9 0.0 collective-permute-done
  9.9 1.7 %collective-permute-start.1 = (f32[16,1280]{1,0:T(8,128)S(1)}, f32[16,1280]{1,0:T(8,128)S(1)}, u32[]{:S(2)}, u32[]{:S(2)}) collective-permute-start(f32[16,1280]{1,0:T(8,128)S(1)} %add.36), channel_id=1, source_target_pairs={{0,5},{1,8},{2,11},{3,6},{4,13},{5,0},{6,3},{7,14},{8,1},{9,12},{1... | collective-permute-start | bytes 245768 | tf_op jit(solution)/shard_map/ppermute | solution.py:254
  11.6 0.3 collective-permute-done.5
  11.9 1.9 %collective-permute-start.6 = (f32[16,1152]{1,0:T(8,128)S(1)}, f32[16,1152]{1,0:T(8,128)S(1)}, u32[]{:S(2)}, u32[]{:S(2)}) collective-permute-start(f32[16,1152]{1,0:T(8,128)S(1)} %add.40), channel_id=1, source_target_pairs={{0,5},{1,8},{2,11},{3,6},{4,13},{5,0},{6,3},{7,14},{8,1},{9,12},{1... | collective-permute-start | bytes 221192 | tf_op jit(solution)/shard_map/ppermute | solution.py:254
  13.9 0.3 collective-permute-done.1
  14.1 1.3 %collective-permute-start.2 = (f32[16,1280]{1,0:T(8,128)S(1)}, f32[16,1280]{1,0:T(8,128)S(1)}, u32[]{:S(2)}, u32[]{:S(2)}) collective-permute-start(f32[16,1280]{1,0:T(8,128)S(1)} %add.37), channel_id=1, source_target_pairs={{0,3},{1,4},{2,7},{3,0},{4,1},{5,6},{6,5},{7,2},{8,13},{9,10},{10,... | collective-permute-start | bytes 245768 | tf_op jit(solution)/shard_map/ppermute | solution.py:254
  15.5 1.3 %collective-permute-done.6 = f32[16,1152]{1,0:T(8,128)S(1)} collective-permute-done((f32[16,1152]{1,0:T(8,128)S(1)}, f32[16,1152]{1,0:T(8,128)S(1)}, u32[]{:S(2)}, u32[]{:S(2)}) %collective-permute-start.6) | collective-permute-done | bytes 73760 | tf_op jit(solution)/shard_map/ppermute | solution.py:254
  16.7 2.7 %collective-permute-start.7 = (f32[16,1152]{1,0:T(8,128)S(1)}, f32[16,1152]{1,0:T(8,128)S(1)}, u32[]{:S(2)}, u32[]{:S(2)}) collective-permute-start(f32[16,1152]{1,0:T(8,128)S(1)} %add.41), channel_id=1, source_target_pairs={{0,9},{1,2},{2,1},{3,10},{4,7},{5,12},{6,15},{7,4},{8,11},{9,0},{1... | collective-permute-start | bytes 221192 | tf_op jit(solution)/shard_map/ppermute | solution.py:254
  19.4 0.0 collective-permute-done.2
  19.4 1.7 %collective-permute-start.3 = (f32[16,1280]{1,0:T(8,128)S(1)}, f32[16,1280]{1,0:T(8,128)S(1)}, u32[]{:S(2)}, u32[]{:S(2)}) collective-permute-start(f32[16,1280]{1,0:T(8,128)S(1)} %add.38), channel_id=1, source_target_pairs={{0,9},{1,2},{2,1},{3,10},{4,7},{5,12},{6,15},{7,4},{8,11},{9,0},{1... | collective-permute-start | bytes 245768 | tf_op jit(solution)/shard_map/ppermute | solution.py:254
  21.1 0.4 collective-permute-done.7
  21.5 0.4 collective-permute-start.8
  21.9 0.0 copy-done.1
  21.9 0.0 copy-done.2
  21.9 0.0 copy-done.3
  21.9 1.4 %products_part.1.part_ref = f32[256,1024]{1,0:T(8,128)S(1)} custom-call(f32[16,1152]{1,0:T(8,128)S(1)} %add.42.own_a, bf16[1024,1024]{1,0:T(8,128)(2,1)S(1)} %get-tuple-element.17.first_ref.geno_a, f32[1,2048]{1,0:T(1,128)S(1)} %bitcast.6, f32[1,2048]{1,0:T(1,128)S(1)} %bitcast.9, s32[1,2048]{1,0:T(1,128)S(1)} %bitcast.12), custom_call_target="tpu_custom_call" | custom-call | flops 1073741824 | bytes 1048576 | tf_op jit(solution)/shard_map/products_part/pallas_call | solution.py:320
  23.3 1.0 %collective-permute-done.3 = f32[16,1280]{1,0:T(8,128)S(1)} collective-permute-done((f32[16,1280]{1,0:T(8,128)S(1)}, f32[16,1280]{1,0:T(8,128)S(1)}, u32[]{:S(2)}, u32[]{:S(2)}) %collective-permute-start.3) | collective-permute-done | bytes 81952 | tf_op jit(solution)/shard_map/ppermute | solution.py:254
  24.3 0.2 collective-permute-start.9
  24.5 0.0 collective-permute-done.8.other_a
  24.5 3.3 %products_own.1 = (f32[33,16,1024]{2,1,0:T(8,128)}, f32[8,512]{1,0:T(8,128)S(1)}, f32[256,1024]{1,0:T(8,128)S(1)}, f32[1,16,1024]{2,1,0:T(8,128)S(1)}) custom-call(s32[1]{0:T(128)} %bitcast.side_ref, f32[256,1024]{1,0:T(8,128)S(1)} %products_part.1.part_ref, f32[16,1152]{1,0:T(8,128)S(1)} %collective-permute-done.8.other_a, f32[16,1280]{1,0:T(8,128)S(1)} %add.43.own_b, ...), custom_call_target="tpu_custom_call" | custom-call | flops 2147483648 | bytes 1048576 | tf_op jit(solution)/shard_map/products_own/pallas_call | solution.py:333
  27.7 0.0 collective-permute-done.9.other_b
  27.8 2.2 %products_other.1 = (f32[33,16,1024]{2,1,0:T(8,128)}, f32[8,896]{1,0:T(8,128)S(1)}) custom-call(s32[1]{0:T(128)} %bitcast.side_ref, f32[256,1024]{1,0:T(8,128)S(1)} %get-tuple-element.26.part_ref, f32[1,16,1024]{2,1,0:T(8,128)S(1)} %get-tuple-element.27.last_ref, f32[16,1280]{1,0:T(8,128)S(1)} %collective-permute-done.9.other_b, ...), custom_call_target="tpu_custom_call", output_to_operand_aliasing={{0}: (9, {})} | custom-call | flops 1073741824 | bytes 1048576 | tf_op jit(solution)/shard_map/products_other/pallas_call | solution.py:347
  30.0 0.5 %collective-permute-start.10 = (f32[8,896]{1,0:T(8,128)S(1)}, f32[8,896]{1,0:T(8,128)S(1)}, u32[]{:S(2)}, u32[]{:S(2)}) collective-permute-start(f32[8,896]{1,0:T(8,128)S(1)} %get-tuple-element.31), channel_id=1, source_target_pairs={{0,1},{1,0},{2,3},{3,2},{4,5},{5,4},{6,7},{7,6},{8,9},{9,8},{10,11... | collective-permute-start | bytes 86024 | tf_op jit(solution)/shard_map/ppermute | solution.py:254
  30.5 0.9 %collective-permute-done.10 = f32[8,896]{1,0:T(8,128)S(1)} collective-permute-done((f32[8,896]{1,0:T(8,128)S(1)}, f32[8,896]{1,0:T(8,128)S(1)}, u32[]{:S(2)}, u32[]{:S(2)}) %collective-permute-start.10) | collective-permute-done | bytes 28704 | tf_op jit(solution)/shard_map/ppermute | solution.py:254
  31.3 2.7 %collective-permute-start.13 = (f32[8,896]{1,0:T(8,128)S(1)}, f32[8,896]{1,0:T(8,128)S(1)}, u32[]{:S(2)}, u32[]{:S(2)}) collective-permute-start(f32[8,896]{1,0:T(8,128)S(1)} %add.44), channel_id=1, source_target_pairs={{0,7},{1,6},{2,5},{3,4},{4,3},{5,2},{6,1},{7,0},{8,15},{9,14},{10,... | collective-permute-start | bytes 86024 | tf_op jit(solution)/shard_map/ppermute | solution.py:254
  34.0 0.0 collective-permute-start.12
  34.0 0.4 %collective-permute-start.11 = (f32[8,896]{1,0:T(8,128)S(1)}, f32[8,896]{1,0:T(8,128)S(1)}, u32[]{:S(2)}, u32[]{:S(2)}) collective-permute-start(f32[8,896]{1,0:T(8,128)S(1)} %add.44), channel_id=1, source_target_pairs={{0,3},{1,2},{2,1},{3,0},{4,7},{5,6},{6,5},{7,4},{8,11},{9,10},{10,... | collective-permute-start | bytes 86024 | tf_op jit(solution)/shard_map/ppermute | solution.py:254
  34.5 1.1 %collective-permute-done.13 = f32[8,896]{1,0:T(8,128)S(1)} collective-permute-done((f32[8,896]{1,0:T(8,128)S(1)}, f32[8,896]{1,0:T(8,128)S(1)}, u32[]{:S(2)}, u32[]{:S(2)}) %collective-permute-start.13) | collective-permute-done | bytes 28704 | tf_op jit(solution)/shard_map/ppermute | solution.py:254
  35.6 1.7 %collective-permute-done.12 = f32[8,896]{1,0:T(8,128)S(1)} collective-permute-done((f32[8,896]{1,0:T(8,128)S(1)}, f32[8,896]{1,0:T(8,128)S(1)}, u32[]{:S(2)}, u32[]{:S(2)}) %collective-permute-start.12) | collective-permute-done | bytes 28704 | tf_op jit(solution)/shard_map/ppermute | solution.py:254
  37.3 0.0 collective-permute-done.11
  37.3 2.4 %collective-permute-start.14 = (f32[8,896]{1,0:T(8,128)S(1)}, f32[8,896]{1,0:T(8,128)S(1)}, u32[]{:S(2)}, u32[]{:S(2)}) collective-permute-start(f32[8,896]{1,0:T(8,128)S(1)} %add_add_fusion.one_ref), channel_id=1, source_target_pairs={{0,9},{1,8},{2,11},{3,10},{4,13},{5,12},{6,15},{7,14},{8,1},{9,0},... | collective-permute-start | bytes 86024 | tf_op jit(solution)/shard_map/ppermute | solution.py:254
  39.8 1.8 %collective-permute-done.14.two_ref = f32[8,896]{1,0:T(8,128)S(1)} collective-permute-done((f32[8,896]{1,0:T(8,128)S(1)}, f32[8,896]{1,0:T(8,128)S(1)}, u32[]{:S(2)}, u32[]{:S(2)}) %collective-permute-start.14) | collective-permute-done | bytes 28704 | tf_op jit(solution)/shard_map/ppermute | solution.py:254
  41.6 1.1 %gram_unpack.1 = f32[16,16,33]{2,1,0:T(8,128)} custom-call(f32[8,896]{1,0:T(8,128)S(1)} %add_add_fusion.one_ref, f32[8,896]{1,0:T(8,128)S(1)} %collective-permute-done.14.two_ref), custom_call_target="tpu_custom_call" | custom-call | tf_op jit(solution)/shard_map/gram_unpack/pallas_call | solution.py:367
  (10 shorter events, 0.1 us)
Async XLA Ops:
  0.6 0.9 %copy-start = (s32[32,1024]{1,0:T(8,128)S(1)}, s32[32,1024]{1,0:T(8,128)}, u32[]{:S(2)}) copy-start(s32[32,1024]{1,0:T(8,128)} %signs_ref.3) | copy-start | bytes 393220
  1.5 2.9 %copy-start.4 = (f32[1024]{0:T(1024)S(1)}, f32[1024]{0:T(1024)}, u32[]{:S(2)}) copy-start(f32[1024]{0:T(1024)} %param.8) | copy-start | bytes 12292
  4.0 3.2 %collective-permute-start.4 = (f32[16,1152]{1,0:T(8,128)S(1)}, f32[16,1152]{1,0:T(8,128)S(1)}, u32[]{:S(2)}, u32[]{:S(2)}) collective-permute-start(f32[16,1152]{1,0:T(8,128)S(1)} %get-tuple-element.21), channel_id=1, source_target_pairs={{0,1},{1,0},{2,3},{3,2},{4,5},{5,4},{6,7},{7,6},{8,9},{9,8},{10,11... | collective-permute-start | bytes 221192 | tf_op jit(solution)/shard_map/ppermute | solution.py:254
  4.5 17.4 %copy-start.1 = (f32[2048]{0:T(1024)S(1)}, f32[2048]{0:T(1024)}, u32[]{:S(2)}) copy-start(f32[2048]{0:T(1024)} %param.9) | copy-start | bytes 24580
  4.5 17.4 %copy-start.2 = (f32[2048]{0:T(1024)S(1)}, f32[2048]{0:T(1024)}, u32[]{:S(2)}) copy-start(f32[2048]{0:T(1024)} %param.10) | copy-start | bytes 24580
  4.5 17.4 %copy-start.3 = (s32[2048]{0:T(1024)S(1)}, s32[2048]{0:T(1024)}, u32[]{:S(2)}) copy-start(s32[2048]{0:T(1024)} %param.11) | copy-start | bytes 24580
  7.1 2.8 %collective-permute-start = (f32[16,1280]{1,0:T(8,128)S(1)}, f32[16,1280]{1,0:T(8,128)S(1)}, u32[]{:S(2)}, u32[]{:S(2)}) collective-permute-start(f32[16,1280]{1,0:T(8,128)S(1)} %get-tuple-element.19), channel_id=1, source_target_pairs={{0,1},{1,0},{2,3},{3,2},{4,5},{5,4},{6,7},{7,6},{8,9},{9,8},{10,11... | collective-permute-start | bytes 245768 | tf_op jit(solution)/shard_map/ppermute | solution.py:254
  7.2 4.7 %collective-permute-start.5 = (f32[16,1152]{1,0:T(8,128)S(1)}, f32[16,1152]{1,0:T(8,128)S(1)}, u32[]{:S(2)}, u32[]{:S(2)}) collective-permute-start(f32[16,1152]{1,0:T(8,128)S(1)} %add.39), channel_id=1, source_target_pairs={{0,3},{1,4},{2,7},{3,0},{4,1},{5,6},{6,5},{7,2},{8,13},{9,10},{10,... | collective-permute-start | bytes 221192 | tf_op jit(solution)/shard_map/ppermute | solution.py:254
  9.9 4.2 %collective-permute-start.1 = (f32[16,1280]{1,0:T(8,128)S(1)}, f32[16,1280]{1,0:T(8,128)S(1)}, u32[]{:S(2)}, u32[]{:S(2)}) collective-permute-start(f32[16,1280]{1,0:T(8,128)S(1)} %add.36), channel_id=1, source_target_pairs={{0,5},{1,8},{2,11},{3,6},{4,13},{5,0},{6,3},{7,14},{8,1},{9,12},{1... | collective-permute-start | bytes 245768 | tf_op jit(solution)/shard_map/ppermute | solution.py:254
  11.9 4.8 %collective-permute-start.6 = (f32[16,1152]{1,0:T(8,128)S(1)}, f32[16,1152]{1,0:T(8,128)S(1)}, u32[]{:S(2)}, u32[]{:S(2)}) collective-permute-start(f32[16,1152]{1,0:T(8,128)S(1)} %add.40), channel_id=1, source_target_pairs={{0,5},{1,8},{2,11},{3,6},{4,13},{5,0},{6,3},{7,14},{8,1},{9,12},{1... | collective-permute-start | bytes 221192 | tf_op jit(solution)/shard_map/ppermute | solution.py:254
  14.1 5.3 %collective-permute-start.2 = (f32[16,1280]{1,0:T(8,128)S(1)}, f32[16,1280]{1,0:T(8,128)S(1)}, u32[]{:S(2)}, u32[]{:S(2)}) collective-permute-start(f32[16,1280]{1,0:T(8,128)S(1)} %add.37), channel_id=1, source_target_pairs={{0,3},{1,4},{2,7},{3,0},{4,1},{5,6},{6,5},{7,2},{8,13},{9,10},{10,... | collective-permute-start | bytes 245768 | tf_op jit(solution)/shard_map/ppermute | solution.py:254
  16.7 4.7 %collective-permute-start.7 = (f32[16,1152]{1,0:T(8,128)S(1)}, f32[16,1152]{1,0:T(8,128)S(1)}, u32[]{:S(2)}, u32[]{:S(2)}) collective-permute-start(f32[16,1152]{1,0:T(8,128)S(1)} %add.41), channel_id=1, source_target_pairs={{0,9},{1,2},{2,1},{3,10},{4,7},{5,12},{6,15},{7,4},{8,11},{9,0},{1... | collective-permute-start | bytes 221192 | tf_op jit(solution)/shard_map/ppermute | solution.py:254
  19.4 4.8 %collective-permute-start.3 = (f32[16,1280]{1,0:T(8,128)S(1)}, f32[16,1280]{1,0:T(8,128)S(1)}, u32[]{:S(2)}, u32[]{:S(2)}) collective-permute-start(f32[16,1280]{1,0:T(8,128)S(1)} %add.38), channel_id=1, source_target_pairs={{0,9},{1,2},{2,1},{3,10},{4,7},{5,12},{6,15},{7,4},{8,11},{9,0},{1... | collective-permute-start | bytes 245768 | tf_op jit(solution)/shard_map/ppermute | solution.py:254
  21.5 3.0 %collective-permute-start.8 = (f32[16,1152]{1,0:T(8,128)S(1)}, f32[16,1152]{1,0:T(8,128)S(1)}, u32[]{:S(2)}, u32[]{:S(2)}) collective-permute-start(f32[16,1152]{1,0:T(8,128)S(1)} %add.42.own_a), channel_id=1, source_target_pairs={{0,1},{1,0},{2,3},{3,2},{4,5},{5,4},{6,7},{7,6},{8,9},{9,8},{10,11... | collective-permute-start | bytes 221192 | tf_op jit(solution)/shard_map/ppermute | solution.py:254
  24.3 3.5 %collective-permute-start.9 = (f32[16,1280]{1,0:T(8,128)S(1)}, f32[16,1280]{1,0:T(8,128)S(1)}, u32[]{:S(2)}, u32[]{:S(2)}) collective-permute-start(f32[16,1280]{1,0:T(8,128)S(1)} %add.43.own_b), channel_id=1, source_target_pairs={{0,1},{1,0},{2,3},{3,2},{4,5},{5,4},{6,7},{7,6},{8,9},{9,8},{10,11... | collective-permute-start | bytes 245768 | tf_op jit(solution)/shard_map/ppermute | solution.py:254
  30.0 1.3 %collective-permute-start.10 = (f32[8,896]{1,0:T(8,128)S(1)}, f32[8,896]{1,0:T(8,128)S(1)}, u32[]{:S(2)}, u32[]{:S(2)}) collective-permute-start(f32[8,896]{1,0:T(8,128)S(1)} %get-tuple-element.31), channel_id=1, source_target_pairs={{0,1},{1,0},{2,3},{3,2},{4,5},{5,4},{6,7},{7,6},{8,9},{9,8},{10,11... | collective-permute-start | bytes 86024 | tf_op jit(solution)/shard_map/ppermute | solution.py:254
  31.3 4.3 %collective-permute-start.13 = (f32[8,896]{1,0:T(8,128)S(1)}, f32[8,896]{1,0:T(8,128)S(1)}, u32[]{:S(2)}, u32[]{:S(2)}) collective-permute-start(f32[8,896]{1,0:T(8,128)S(1)} %add.44), channel_id=1, source_target_pairs={{0,7},{1,6},{2,5},{3,4},{4,3},{5,2},{6,1},{7,0},{8,15},{9,14},{10,... | collective-permute-start | bytes 86024 | tf_op jit(solution)/shard_map/ppermute | solution.py:254
  34.0 3.3 %collective-permute-start.12 = (f32[8,896]{1,0:T(8,128)S(1)}, f32[8,896]{1,0:T(8,128)S(1)}, u32[]{:S(2)}, u32[]{:S(2)}) collective-permute-start(f32[8,896]{1,0:T(8,128)S(1)} %add.44), channel_id=1, source_target_pairs={{0,5},{1,4},{2,7},{3,6},{4,1},{5,0},{6,3},{7,2},{8,13},{9,12},{10,... | collective-permute-start | bytes 86024 | tf_op jit(solution)/shard_map/ppermute | solution.py:254
  34.0 3.3 %collective-permute-start.11 = (f32[8,896]{1,0:T(8,128)S(1)}, f32[8,896]{1,0:T(8,128)S(1)}, u32[]{:S(2)}, u32[]{:S(2)}) collective-permute-start(f32[8,896]{1,0:T(8,128)S(1)} %add.44), channel_id=1, source_target_pairs={{0,3},{1,2},{2,1},{3,0},{4,7},{5,6},{6,5},{7,4},{8,11},{9,10},{10,... | collective-permute-start | bytes 86024 | tf_op jit(solution)/shard_map/ppermute | solution.py:254
  37.3 4.3 %collective-permute-start.14 = (f32[8,896]{1,0:T(8,128)S(1)}, f32[8,896]{1,0:T(8,128)S(1)}, u32[]{:S(2)}, u32[]{:S(2)}) collective-permute-start(f32[8,896]{1,0:T(8,128)S(1)} %add_add_fusion.one_ref), channel_id=1, source_target_pairs={{0,9},{1,8},{2,11},{3,10},{4,13},{5,12},{6,15},{7,14},{8,1},{9,0},... | collective-permute-start | bytes 86024 | tf_op jit(solution)/shard_map/ppermute | solution.py:254

commit v5 on v4

v5 whole, which is shorter than its diff:
```python
import functools

import jax
import jax.numpy as jnp
from jax import lax
from jax.experimental import pallas as pl
from jax.experimental.pallas import tpu as pltpu
from jax.sharding import PartitionSpec as P

BINS = 16
LANES = 128
GROUP = LANES // BINS
F32 = jnp.float32
BF16 = jnp.bfloat16
MIB = 2**20

dot_nt = functools.partial(lax.dot_general, dimension_numbers=(((1,), (1,)), ((), ())), preferred_element_type=F32)


def two_parts(x):
    hi = x.astype(BF16)
    return hi, (x - hi.astype(F32)).astype(BF16)


def sign_rows(signs_ref):
    return (2 * signs_ref[...] - 1).astype(F32).astype(BF16)


def pheno_rows(pheno_ref):
    pheno = pheno_ref[...]
    high = pheno.astype(BF16).astype(F32)
    rest = pheno - high
    middle = rest.astype(BF16).astype(F32)
    tail = jnp.zeros((13, pheno.shape[1]), F32)
    return jnp.concatenate([high, middle, rest - middle, tail], axis=0).astype(BF16)


def add_three(x):
    return x[:1] + x[1:2] + x[2:3]


def narrowed(geno_hbm, narrow_ref, raw, sems, start, chunk):
    samples, markers = raw.shape
    rows = [slice(c * chunk, (c + 1) * chunk) for c in range(samples // chunk)]
    copies = [pltpu.make_async_copy(geno_hbm.at[s, start : start + markers], raw.at[s], sems.at[c]) for c, s in enumerate(rows)]
    for copy in copies:
        copy.start()

    def finish():
        for copy, s in zip(copies, rows):
            copy.wait()
            narrow = raw[s].astype(F32).astype(BF16)
            narrow_ref[s] = narrow
            yield s, narrow

    return finish


def place_rows(side, vectors, acc, own_ref, other_ref):
    half = own_ref.shape[0]
    probes = 2 * half
    markers = acc.shape[1]
    tiles = markers // LANES
    sums = dot_nt(jnp.ones((8, vectors.shape[1]), BF16), vectors)[:1]
    last = sums[:, probes : probes + 1] + sums[:, probes + 1 : probes + 2] + sums[:, probes + 2 : probes + 3]
    pheno = add_three(acc[probes : probes + 8, :])
    for ref, which in ((own_ref, side), (other_ref, 1 - side)):
        ref[:, :markers] = acc[pl.ds(pl.multiple_of(which * half, half), half), :]
        ref[: half - tiles, markers:] = jnp.zeros((half - tiles, LANES), F32)
        ref[:1, markers : markers + half] = jnp.where(which == 0, sums[:, :half], sums[:, half:probes])
        ref[:1, markers + half : markers + half + 1] = last
        for t in range(tiles):
            ref[half - tiles + t : half - tiles + t + 1, markers:] = pheno[:, t * LANES : (t + 1) * LANES]


def vector_rows(signs_ref, pheno_ref):
    return jnp.concatenate([sign_rows(signs_ref), pheno_rows(pheno_ref)], axis=0)


def narrow_kernel(geno_hbm, narrow_ref, raw, sems, *, start, chunk):
    for _ in narrowed(geno_hbm, narrow_ref, raw, sems, start, chunk)():
        pass


def first_sums_kernel(side_ref, narrow_ref, signs_ref, pheno_ref, own_ref, other_ref, acc):
    vectors = vector_rows(signs_ref, pheno_ref)
    acc[...] = jnp.dot(vectors, narrow_ref[...], preferred_element_type=F32)
    place_rows(side_ref[0], vectors, acc, own_ref, other_ref)


def second_sums_kernel(side_ref, geno_hbm, signs_ref, pheno_ref, own_ref, other_ref, narrow_ref, raw, acc, sems, *, start, chunk):
    finish = narrowed(geno_hbm, narrow_ref, raw, sems, start, chunk)
    vectors = vector_rows(signs_ref, pheno_ref)
    for s, narrow in finish():
        part = jnp.dot(vectors[:, s], narrow, preferred_element_type=F32)
        if s.start == 0:
            acc[...] = part
        else:
            acc[...] += part
    place_rows(side_ref[0], vectors, acc, own_ref, other_ref)


class Half:
    def __init__(self, mean_ref, scale_ref, bin_ref, geno_ref, start, norm):
        markers = geno_ref.shape[1]
        self.geno = geno_ref
        self.mean = mean_ref[:, start : start + markers]
        scale = scale_ref[:, start : start + markers]
        self.scale = scale * scale * norm
        self.member = (bin_ref[:, start : start + markers] == lax.broadcasted_iota(jnp.int32, (BINS, markers), 0)).astype(F32)

    def scores(self, sums, total):
        return (sums - self.mean * total) * self.scale

    def probe_scores(self, ref):
        markers = self.mean.shape[1]
        return [self.scores(ref[r : r + 1, :markers], ref[:1, markers + r : markers + r + 1]) for r in range(ref.shape[0])]

    def pheno_scores(self, ref):
        half = ref.shape[0]
        markers = self.mean.shape[1]
        tiles = markers // LANES
        row = jnp.concatenate([ref[t : t + 1, markers:] for t in range(half - tiles, half)], axis=1)
        return self.scores(row, ref[:1, markers + half : markers + half + 1])

    def weigh(self, rows, weights):
        shifts = []
        count = len(rows) * BINS
        for r, row in enumerate(rows):
            weighted = self.member * row
            shifts.append(jnp.sum(weighted * self.mean, axis=1, keepdims=True))
            hi, lo = two_parts(weighted)
            weights[r * BINS : (r + 1) * BINS, :] = hi
            weights[count + r * BINS : count + (r + 1) * BINS, :] = lo
        return jnp.concatenate(shifts, axis=0)

    def multiply(self, weights, span=slice(None)):
        both = dot_nt(weights[...], self.geno[span, :])
        count = both.shape[0] // 2
        return both[:count] + both[count:]

    def products(self, rows, weights):
        shift = self.weigh(rows, weights)
        return self.multiply(weights) - shift


def square_of(products):
    count = products.shape[0]
    hi, lo = two_parts(products)
    both = dot_nt(jnp.concatenate([hi, lo], axis=0), hi)
    return both[:count] + (both[count:] + both[count:].T)


def gram_of(products, gram_norm):
    column = lax.broadcasted_iota(jnp.int32, (BINS, LANES), 1)
    parts = []
    for g in range(products.shape[0] // LANES):
        square = square_of(products[g * LANES : (g + 1) * LANES])
        total = square[:BINS]
        for r in range(1, GROUP):
            total = jnp.where(column // BINS == r, square[r * BINS : (r + 1) * BINS], total)
        parts.append(total * gram_norm)
    h = BINS // 2
    packed = []
    for one, two in zip(parts[::2], parts[1::2]):
        moved = pltpu.roll(two[h:], LANES - h, 1)
        packed += [one[:h], two[:h], jnp.where(column[:h] % BINS >= h, one[h:], moved)]
    return jnp.concatenate(packed, axis=1)


def unpack_kernel(one_ref, two_ref, out_ref, upper, lower, *, pairs):
    h = BINS // 2
    count = upper.shape[0] // BINS
    packed = one_ref[...] + two_ref[...]
    tile = [packed[:, t * LANES : (t + 1) * LANES] for t in range(packed.shape[1] // LANES)]
    for p in range(pairs):
        one, two, low = tile[3 * p : 3 * p + 3]
        for i, (a, b) in enumerate(((one, low), (two, pltpu.roll(low, h, 1)))):
            at = (2 * p + i) * LANES
            upper[at : at + LANES, :] = a.T
            lower[at : at + LANES, :] = b.T
    last = tile[3 * pairs].T
    upper[2 * pairs * LANES :, :] = last[:BINS]
    lower[2 * pairs * LANES :, :] = last[BINS : 2 * BINS]
    for l in range(BINS):
        row = upper[pl.ds(l, count, stride=BINS), :].T
        out_ref[:h, l, :] = row
        if l >= h:
            out_ref[l, :h, :] = row
            out_ref[h:, l, :] = lower[pl.ds(l, count, stride=BINS), :].T


def part_kernel(sums_a, geno_a, mean_ref, scale_ref, bin_ref, part_ref, weights, *, norm, pheno):
    first = Half(mean_ref, scale_ref, bin_ref, geno_a, 0, norm)
    rows = first.probe_scores(sums_a) + ([first.pheno_scores(sums_a)] if pheno else [])
    part_ref[...] = first.products(rows, weights)


def own_kernel(own_part, other_part, own_b, geno_b, mean_ref, scale_ref, bin_ref, mine_ref, last_ref, gram_ref, weights, *, norm, gram_norm):
    half = own_b.shape[0]
    count = half * BINS
    samples, markers = geno_b.shape
    second = Half(mean_ref, scale_ref, bin_ref, geno_b, markers, norm)
    parts = second.products(second.probe_scores(own_b) + [second.pheno_scores(own_b)], weights)
    mine = own_part[...] + parts[:count]
    mine_ref[...] = mine.reshape(half, BINS, samples)
    last = other_part[count:] + parts[count:]
    last_ref[0] = last
    probe_gram = gram_of(mine, gram_norm)
    gram_ref[:, : probe_gram.shape[1]] = probe_gram
    square = square_of(last) * gram_norm
    h = BINS // 2
    rest = jnp.zeros((h, LANES - 2 * BINS), F32)
    gram_ref[:, probe_gram.shape[1] :] = jnp.concatenate([square[:h], square[h:], rest], axis=1)


def other_kernel(side_ref, part_ref, other_b, geno_b, mean_ref, scale_ref, bin_ref, own_gram_ref, theirs_ref, gram_ref, weights, *, norm, gram_norm):
    half = other_b.shape[0]
    side = side_ref[0]
    samples, markers = geno_b.shape
    second = Half(mean_ref, scale_ref, bin_ref, geno_b, markers, norm)
    products = part_ref[: half * BINS] + second.products(second.probe_scores(other_b), weights)
    theirs_ref[...] = products.reshape(half, BINS, samples)
    gram = gram_of(products, gram_norm)
    packed = gram.shape[1]
    gram_ref[:, pl.ds(pl.multiple_of((1 - side) * packed, packed), packed)] = gram
    gram_ref[:, pl.ds(pl.multiple_of(side * packed, packed), packed)] = own_gram_ref[:, :packed]
    gram_ref[:, 2 * packed :] = own_gram_ref[:, packed:]


def store_kernel(side_ref, mine_ref, theirs_ref, last_ref, out_ref, sems):
    half = mine_ref.shape[0]
    copies = []
    for i, (ref, which) in enumerate(((mine_ref, side_ref[0]), (theirs_ref, 1 - side_ref[0]))):
        to = out_ref.at[pl.ds(pl.multiple_of(which * half, half), half)]
        copies.append(pltpu.make_async_copy(ref, to, sems.at[i]))
    copies.append(pltpu.make_async_copy(last_ref, out_ref.at[pl.ds(2 * half, 1)], sems.at[2]))
    for copy in copies:
        copy.start()
    for copy in copies:
        copy.wait()


def parity(i):
    return bin(i).count("1") % 2


def exchange(x, even, odd=None):
    pairs = [(i, i ^ (even if odd is None or not parity(i) else odd)) for i in range(lax.axis_size("samp"))]
    return lax.ppermute(x, "samp", pairs)


def shards(genotypes, probe_signs, phenotype, marker_mean, marker_scale, marker_bin):
    samples, markers = genotypes.shape
    probes = probe_signs.shape[0]
    half = probes // 2
    devices = lax.axis_size("samp")
    total = samples * devices
    side = (lax.population_count(lax.axis_index("samp")) & 1).astype(jnp.int32).reshape(1)
    markers_info = [x.reshape(1, markers) for x in (marker_mean, marker_scale, marker_bin)]
    pheno = phenotype.reshape(1, samples)
    smem = pl.BlockSpec(memory_space=pltpu.SMEM)
    vmem = pl.BlockSpec(memory_space=pltpu.VMEM)
    hbm = pl.BlockSpec(memory_space=pl.ANY)

    width = markers // 2
    chunk = min(samples, 128)
    narrow = jax.ShapeDtypeStruct((samples, width), BF16)

    part = jax.ShapeDtypeStruct((half, width + LANES), F32)
    raw = [pltpu.VMEM((samples, width), jnp.int32)]
    acc = [pltpu.VMEM((probes + 16, width), F32)]
    sems = [pltpu.SemaphoreType.DMA((samples // chunk,))]

    def local(kernel, name, out_shape, scratch, work, moved, mib, *operands, **options):
        spaces = {id(side): smem, id(genotypes): hbm}
        return pl.pallas_call(
            functools.partial(kernel, **options),
            out_shape=out_shape,
            in_specs=[spaces.get(id(x), vmem) for x in operands],
            out_specs=jax.tree.map(lambda _: vmem, out_shape),
            scratch_shapes=scratch,
            cost_estimate=pl.CostEstimate(flops=2 * work * samples * width, bytes_accessed=moved, transcendentals=0),
            compiler_params=pltpu.CompilerParams(vmem_limit_bytes=mib * MIB),
            name=name,
        )(*operands)

    flips = [1 << b for b in range(1, devices.bit_length() - 1)]
    large = 6 * samples * width
    narrow_a = local(narrow_kernel, "narrow_first", narrow, raw + sems, 0, large, 47, genotypes, start=0, chunk=chunk)
    own_a, other_a = local(
        first_sums_kernel, "sums_first", (part, part), acc, probes, 2 * samples * width, 32, side, narrow_a, probe_signs, pheno
    )
    own_b, other_b, narrow_b = local(
        second_sums_kernel,
        "sums_second",
        (part, part, narrow),
        raw + acc + sems,
        probes,
        large,
        47,
        side,
        genotypes,
        probe_signs,
        pheno,
        start=width,
        chunk=chunk,
    )
    own_a = own_a + exchange(other_a, 1)
    own_b = own_b + exchange(other_b, 1)
    swapped = flips[1:2] + flips[:1] + flips[2:]
    received = None
    for a_even, a_odd, b_even, b_odd in zip(flips, flips[1:] + flips[:1], swapped, flips[::-1]):
        own_a = own_a + exchange(own_a, a_even | 1, a_odd | 1)
        if received is not None:
            own_b = own_b + received
        received = exchange(own_b, b_even | 1, b_odd | 1)

    norm = (total * (markers // BINS)) ** -0.5
    gram_norm = 1.0 / total
    rows = half * BINS
    packed = rows // LANES * 3 * LANES // 2
    probe_rows = jax.ShapeDtypeStruct((half, BINS, samples), F32)

    def multiply(kernel, name, count, out_shape, *operands, **options):
        scratch = [pltpu.VMEM((2 * count, width), BF16)]
        return local(kernel, name, out_shape, scratch, 2 * count, 4 * count * samples, 32, *operands, norm=norm, **options)

    other_a = exchange(own_a, 1)
    own_part, other_part = (
        multiply(part_kernel, name, count, jax.ShapeDtypeStruct((count, samples), F32), x, narrow_a, *markers_info, pheno=count > rows)
        for name, count, x in (("products_part", rows, own_a), ("products_part_other", rows + BINS, other_a))
    )
    own_b, received, other_part = lax.optimization_barrier((own_b, received, other_part))
    own_b = own_b + received
    other_b = exchange(own_b, 1)
    out_shape = (
        probe_rows,
        jax.ShapeDtypeStruct((1, BINS, samples), F32),
        jax.ShapeDtypeStruct((BINS // 2, packed + LANES), F32),
    )
    mine, last, gram = multiply(
        own_kernel, "products_own", rows + BINS, out_shape, own_part, other_part, own_b, narrow_b, *markers_info, gram_norm=gram_norm
    )
    out_shape = (probe_rows, jax.ShapeDtypeStruct((BINS // 2, 2 * packed + LANES), F32))
    theirs, gram = multiply(
        other_kernel, "products_other", rows, out_shape, side, other_part, other_b, narrow_b, *markers_info, gram, gram_norm=gram_norm
    )
    products = pl.pallas_call(
        store_kernel,
        out_shape=jax.ShapeDtypeStruct((probes + 1, BINS, samples), F32),
        in_specs=[smem, vmem, vmem, vmem],
        out_specs=hbm,
        scratch_shapes=[pltpu.SemaphoreType.DMA((3,))],
        cost_estimate=pl.CostEstimate(flops=0, bytes_accessed=4 * (probes + 1) * BINS * samples, transcendentals=0),
        compiler_params=pltpu.CompilerParams(vmem_limit_bytes=16 * MIB),
        name="products_store",
    )(side, mine, theirs, last)

    gram = gram + exchange(gram, 1)
    rest = flips
    while len(rest) > 1:
        near, far, both = (exchange(gram, f | 1) for f in (rest[0], rest[1], rest[0] | rest[1]))
        gram = (gram + near) + (far + both)
        rest = rest[2:]
    last = exchange(gram, rest[0] | 1) if rest else jnp.zeros_like(gram)
    count = (probes + 1) * BINS
    gram = pl.pallas_call(
        functools.partial(unpack_kernel, pairs=2 * rows // (2 * LANES)),
        out_shape=jax.ShapeDtypeStruct((BINS, BINS, probes + 1), F32),
        in_specs=[vmem, vmem],
        out_specs=vmem,
        scratch_shapes=[pltpu.VMEM((count, BINS // 2), F32), pltpu.VMEM((count, BINS // 2), F32)],
        compiler_params=pltpu.CompilerParams(vmem_limit_bytes=16 * MIB),
        name="gram_unpack",
    )(gram, last)
    return (products.transpose(1, 0, 2), gram)


def solution(mesh):
    in_specs = (
        P(("grp", "samp"), None),
        P(None, ("grp", "samp")),
        P(("grp", "samp")),
        P(),
        P(),
        P(),
    )
    out_specs = (P(None, None, ("grp", "samp")), P("grp", None, None))
    return jax.shard_map(shards, mesh=mesh, in_specs=in_specs, out_specs=out_specs, check_vma=False)
```

time: 42.9 us -> 41.8 us (0.974)
  waiting for transfers between devices: 8.69 us -> 5.85 us
  Pallas kernels: 13 us -> 14.5 us
  starting transfers between devices: 19.3 us -> 20.3 us
  local copies, waits for them, and re-layouts: 0.91 us -> 0.02 us
    ppermute x15, waiting for transfers between devices: 8.69 us -> 5.85 us  [exchange(): return lax.ppermute(x, 'samp', pairs)]
    pallas_call x5 -> x8, Pallas kernels: 11.9 us -> 13.4 us  [the longest x7 12.1 us: local(): pl.pallas_call(functools.partial(kernel, **options), out_shape=out_shape,...]
    ppermute x15, starting transfers between devices: 19.3 us -> 20.3 us  [exchange(): return lax.ppermute(x, 'samp', pairs)]
    unnamed x10, local copies, waits for them, and re-layouts: 0.91 us -> 0.02 us
  transfers between devices with their start and end apart: 15 -> 15, of which waited for: 9 -> 8; matrix products, arithmetic and copies ran while one was open for 0% -> 0% of each run, Pallas kernels for 17% -> 21%
where the time goes in v5:
time: 41.8 us; the launch traced here: 41.6 us
  starting transfers between devices  20.3 us (49%)
  Pallas kernels  14.5 us (35%)
  waiting for transfers between devices  5.85 us (14%)
  between operations  0.78 us (2%)
    ppermute x15, starting transfers between devices, exchange(): return lax.ppermute(x, 'samp', pairs)  20.3 us
    pallas_call x7, Pallas kernels, local(): pl.pallas_call(functools.partial(kernel, **options), out_shape=out_shape,...  12.1 us
    ppermute x15, waiting for transfers between devices, exchange(): return lax.ppermute(x, 'samp', pairs)  5.85 us
    pallas_call x1, Pallas kernels, shards(): pl.pallas_call(store_kernel, out_shape=jax.ShapeDtypeStruct((probes + 1,...  1.34 us
    pallas_call x1, Pallas kernels, shards(): pl.pallas_call(functools.partial(unpack_kernel, pairs=2 * rows // (2 * LA...  1.12 us
  transfers between devices with their start and end apart: 15, of which 8 were waited for; matrix products, arithmetic and copies ran while one was open for 0% of the time, Pallas kernels for 21%

profile of v5, /device:TPU:0, one launch (start us, length us, event | category | flops | bytes accessed | tf_op | source)
XLA Modules:
  0.0 41.6 jit_solution(17739130638489488652)
XLA Ops:
  0.6 0.0 copy-start
  0.7 0.0 copy-start.1
  0.7 2.3 %narrow_first.1.narrow_ref.geno_a = bf16[1024,1024]{1,0:T(8,128)(2,1)S(1)} custom-call(s32[1024,2048]{1,0:T(8,128)} %geno_hbm.3), custom_call_target="tpu_custom_call" | custom-call | bytes 6291456 | tf_op jit(solution)/shard_map/narrow_first/pallas_call | solution.py:277
  3.0 0.0 copy-done
  3.0 0.0 copy-done.1
  3.0 0.6 %sums_first.1 = (f32[16,1152]{1,0:T(8,128)S(1)}, f32[16,1152]{1,0:T(8,128)S(1)}) custom-call(s32[1]{0:T(128)} %bitcast.side_ref, bf16[1024,1024]{1,0:T(8,128)(2,1)S(1)} %narrow_first.1.narrow_ref.geno_a, s32[32,1024]{1,0:T(8,128)S(1)} %copy-done, f32[1,1024]{1,0:T(1,128)S(1)} %bitcast.6), custom_call_target="tpu_custom_call" | custom-call | flops 67108864 | bytes 2097152 | tf_op jit(solution)/shard_map/sums_first/pallas_call | solution.py:277
  3.6 0.0 copy-start.2
  3.6 0.0 copy-start.3
  3.6 0.5 %collective-permute-start = (f32[16,1152]{1,0:T(8,128)S(1)}, f32[16,1152]{1,0:T(8,128)S(1)}, u32[]{:S(2)}, u32[]{:S(2)}) collective-permute-start(f32[16,1152]{1,0:T(8,128)S(1)} %get-tuple-element.16), channel_id=1, source_target_pairs={{0,1},{1,0},{2,3},{3,2},{4,5},{5,4},{6,7},{7,6},{8,9},{9,8},{10,11... | collective-permute-start | bytes 221192 | tf_op jit(solution)/shard_map/ppermute | solution.py:250
  4.1 2.6 %sums_second.1 = (f32[16,1152]{1,0:T(8,128)S(1)}, f32[16,1152]{1,0:T(8,128)S(1)}, bf16[1024,1024]{1,0:T(8,128)(2,1)S(1)}) custom-call(s32[1]{0:T(128)} %bitcast.side_ref, s32[1024,2048]{1,0:T(8,128)} %geno_hbm.3, s32[32,1024]{1,0:T(8,128)S(1)} %copy-done, f32[1,1024]{1,0:T(1,128)S(1)} %bitcast.7), custom_call_target="tpu_custom_call" | custom-call | flops 67108864 | bytes 6291456 | tf_op jit(solution)/shard_map/sums_second/pallas_call | solution.py:277
  6.6 0.1 collective-permute-start.4
  6.8 0.0 collective-permute-done
  6.8 2.7 %collective-permute-start.1 = (f32[16,1152]{1,0:T(8,128)S(1)}, f32[16,1152]{1,0:T(8,128)S(1)}, u32[]{:S(2)}, u32[]{:S(2)}) collective-permute-start(f32[16,1152]{1,0:T(8,128)S(1)} %add.36), channel_id=1, source_target_pairs={{0,3},{1,4},{2,7},{3,0},{4,1},{5,6},{6,5},{7,2},{8,13},{9,10},{10,... | collective-permute-start | bytes 221192 | tf_op jit(solution)/shard_map/ppermute | solution.py:250
  9.5 0.0 collective-permute-done.4
  9.5 1.7 %collective-permute-start.5 = (f32[16,1152]{1,0:T(8,128)S(1)}, f32[16,1152]{1,0:T(8,128)S(1)}, u32[]{:S(2)}, u32[]{:S(2)}) collective-permute-start(f32[16,1152]{1,0:T(8,128)S(1)} %add.40), channel_id=1, source_target_pairs={{0,5},{1,8},{2,11},{3,6},{4,13},{5,0},{6,3},{7,14},{8,1},{9,12},{1... | collective-permute-start | bytes 221192 | tf_op jit(solution)/shard_map/ppermute | solution.py:250
  11.2 0.3 collective-permute-done.1
  11.5 1.9 %collective-permute-start.2 = (f32[16,1152]{1,0:T(8,128)S(1)}, f32[16,1152]{1,0:T(8,128)S(1)}, u32[]{:S(2)}, u32[]{:S(2)}) collective-permute-start(f32[16,1152]{1,0:T(8,128)S(1)} %add.37), channel_id=1, source_target_pairs={{0,5},{1,8},{2,11},{3,6},{4,13},{5,0},{6,3},{7,14},{8,1},{9,12},{1... | collective-permute-start | bytes 221192 | tf_op jit(solution)/shard_map/ppermute | solution.py:250
  13.5 0.1 collective-permute-done.5
  13.5 1.5 %collective-permute-start.6 = (f32[16,1152]{1,0:T(8,128)S(1)}, f32[16,1152]{1,0:T(8,128)S(1)}, u32[]{:S(2)}, u32[]{:S(2)}) collective-permute-start(f32[16,1152]{1,0:T(8,128)S(1)} %add.41), channel_id=1, source_target_pairs={{0,3},{1,4},{2,7},{3,0},{4,1},{5,6},{6,5},{7,2},{8,13},{9,10},{10,... | collective-permute-start | bytes 221192 | tf_op jit(solution)/shard_map/ppermute | solution.py:250
  15.1 1.2 %collective-permute-done.2 = f32[16,1152]{1,0:T(8,128)S(1)} collective-permute-done((f32[16,1152]{1,0:T(8,128)S(1)}, f32[16,1152]{1,0:T(8,128)S(1)}, u32[]{:S(2)}, u32[]{:S(2)}) %collective-permute-start.2) | collective-permute-done | bytes 73760 | tf_op jit(solution)/shard_map/ppermute | solution.py:250
  16.2 2.8 %collective-permute-start.3 = (f32[16,1152]{1,0:T(8,128)S(1)}, f32[16,1152]{1,0:T(8,128)S(1)}, u32[]{:S(2)}, u32[]{:S(2)}) collective-permute-start(f32[16,1152]{1,0:T(8,128)S(1)} %add.38), channel_id=1, source_target_pairs={{0,9},{1,2},{2,1},{3,10},{4,7},{5,12},{6,15},{7,4},{8,11},{9,0},{1... | collective-permute-start | bytes 221192 | tf_op jit(solution)/shard_map/ppermute | solution.py:250
  19.0 0.0 collective-permute-done.6
  19.0 1.5 %collective-permute-start.7 = (f32[16,1152]{1,0:T(8,128)S(1)}, f32[16,1152]{1,0:T(8,128)S(1)}, u32[]{:S(2)}, u32[]{:S(2)}) collective-permute-start(f32[16,1152]{1,0:T(8,128)S(1)} %add.42), channel_id=1, source_target_pairs={{0,9},{1,2},{2,1},{3,10},{4,7},{5,12},{6,15},{7,4},{8,11},{9,0},{1... | collective-permute-start | bytes 221192 | tf_op jit(solution)/shard_map/ppermute | solution.py:250
  20.5 0.5 %collective-permute-done.3 = f32[16,1152]{1,0:T(8,128)S(1)} collective-permute-done((f32[16,1152]{1,0:T(8,128)S(1)}, f32[16,1152]{1,0:T(8,128)S(1)}, u32[]{:S(2)}, u32[]{:S(2)}) %collective-permute-start.3) | collective-permute-done | bytes 73760 | tf_op jit(solution)/shard_map/ppermute | solution.py:250
  21.1 0.5 %collective-permute-start.8 = (f32[16,1152]{1,0:T(8,128)S(1)}, f32[16,1152]{1,0:T(8,128)S(1)}, u32[]{:S(2)}, u32[]{:S(2)}) collective-permute-start(f32[16,1152]{1,0:T(8,128)S(1)} %add.39.sums_a), channel_id=1, source_target_pairs={{0,1},{1,0},{2,3},{3,2},{4,5},{5,4},{6,7},{7,6},{8,9},{9,8},{10,11... | collective-permute-start | bytes 221192 | tf_op jit(solution)/shard_map/ppermute | solution.py:250
  21.5 0.0 copy-done.2
  21.5 0.0 copy-done.3
  21.5 0.0 copy-done.4
  21.5 1.4 %products_part.1.own_part = f32[256,1024]{1,0:T(8,128)S(1)} custom-call(f32[16,1152]{1,0:T(8,128)S(1)} %add.39.sums_a, bf16[1024,1024]{1,0:T(8,128)(2,1)S(1)} %narrow_first.1.narrow_ref.geno_a, f32[1,2048]{1,0:T(1,128)S(1)} %bitcast.8, f32[1,2048]{1,0:T(1,128)S(1)} %bitcast.12, s32[1,2048]{1,0:T(1,128)S(1)} %bitcast.16), custom_call_target="tpu_custom_call" | custom-call | flops 1073741824 | bytes 1048576 | tf_op jit(solution)/shard_map/products_part/pallas_call | solution.py:277
  22.9 0.0 collective-permute-done.8.sums_a
  22.9 1.5 %products_part_other.1.other_part.part_ref = f32[272,1024]{1,0:T(8,128)S(1)} custom-call(f32[16,1152]{1,0:T(8,128)S(1)} %collective-permute-done.8.sums_a, bf16[1024,1024]{1,0:T(8,128)(2,1)S(1)} %narrow_first.1.narrow_ref.geno_a, f32[1,2048]{1,0:T(1,128)S(1)} %bitcast.9, f32[1,2048]{1,0:T(1,128)S(1)} %bitcast.13, s32[1,2048]{1,0:T(1,128)S(1)} %bitcast.17), custom_call_target="tpu_custom_call" | custom-call | flops 1140850688 | bytes 1114112 | tf_op jit(solution)/shard_map/products_part_other/pallas_call | solution.py:277
  24.4 0.0 collective-permute-done.7
  24.4 0.2 collective-permute-start.9
  24.6 1.9 %products_own.1 = (f32[16,16,1024]{2,1,0:T(8,128)S(1)}, f32[1,16,1024]{2,1,0:T(8,128)S(1)}, f32[8,512]{1,0:T(8,128)S(1)}) custom-call(f32[256,1024]{1,0:T(8,128)S(1)} %products_part.1.own_part, f32[272,1024]{1,0:T(8,128)S(1)} %products_part_other.1.other_part.part_ref, f32[16,1152]{1,0:T(8,128)S(1)} %add.43.own_b, ...), custom_call_target="tpu_custom_call" | custom-call | flops 1140850688 | bytes 1114112 | tf_op jit(solution)/shard_map/products_own/pallas_call | solution.py:277
  26.5 0.0 collective-permute-done.9.other_b
  26.5 1.8 %products_other.1 = (f32[16,16,1024]{2,1,0:T(8,128)S(1)}, f32[8,896]{1,0:T(8,128)S(1)}) custom-call(s32[1]{0:T(128)} %bitcast.side_ref, f32[272,1024]{1,0:T(8,128)S(1)} %products_part_other.1.other_part.part_ref, f32[16,1152]{1,0:T(8,128)S(1)} %collective-permute-done.9.other_b, bf16[1024,1024]{1,0:T(8,128)(2,1)S(1)} %get-tuple-element.22.geno_b, ...), custom_call_target="tpu_custom_call" | custom-call | flops 1073741824 | bytes 1048576 | tf_op jit(solution)/shard_map/products_other/pallas_call | solution.py:277
  28.3 0.4 %collective-permute-start.10 = (f32[8,896]{1,0:T(8,128)S(1)}, f32[8,896]{1,0:T(8,128)S(1)}, u32[]{:S(2)}, u32[]{:S(2)}) collective-permute-start(f32[8,896]{1,0:T(8,128)S(1)} %get-tuple-element.27), channel_id=1, source_target_pairs={{0,1},{1,0},{2,3},{3,2},{4,5},{5,4},{6,7},{7,6},{8,9},{9,8},{10,11... | collective-permute-start | bytes 86024 | tf_op jit(solution)/shard_map/ppermute | solution.py:250
  28.7 0.9 %collective-permute-done.10 = f32[8,896]{1,0:T(8,128)S(1)} collective-permute-done((f32[8,896]{1,0:T(8,128)S(1)}, f32[8,896]{1,0:T(8,128)S(1)}, u32[]{:S(2)}, u32[]{:S(2)}) %collective-permute-start.10) | collective-permute-done | bytes 28704 | tf_op jit(solution)/shard_map/ppermute | solution.py:250
  29.6 3.1 %collective-permute-start.13 = (f32[8,896]{1,0:T(8,128)S(1)}, f32[8,896]{1,0:T(8,128)S(1)}, u32[]{:S(2)}, u32[]{:S(2)}) collective-permute-start(f32[8,896]{1,0:T(8,128)S(1)} %add.44), channel_id=1, source_target_pairs={{0,7},{1,6},{2,5},{3,4},{4,3},{5,2},{6,1},{7,0},{8,15},{9,14},{10,... | collective-permute-start | bytes 86024 | tf_op jit(solution)/shard_map/ppermute | solution.py:250
  32.7 0.0 collective-permute-start.12
  32.7 0.6 %collective-permute-start.11 = (f32[8,896]{1,0:T(8,128)S(1)}, f32[8,896]{1,0:T(8,128)S(1)}, u32[]{:S(2)}, u32[]{:S(2)}) collective-permute-start(f32[8,896]{1,0:T(8,128)S(1)} %add.44), channel_id=1, source_target_pairs={{0,3},{1,2},{2,1},{3,0},{4,7},{5,6},{6,5},{7,4},{8,11},{9,10},{10,... | collective-permute-start | bytes 86024 | tf_op jit(solution)/shard_map/ppermute | solution.py:250
  33.3 1.1 %collective-permute-done.13 = f32[8,896]{1,0:T(8,128)S(1)} collective-permute-done((f32[8,896]{1,0:T(8,128)S(1)}, f32[8,896]{1,0:T(8,128)S(1)}, u32[]{:S(2)}, u32[]{:S(2)}) %collective-permute-start.13) | collective-permute-done | bytes 28704 | tf_op jit(solution)/shard_map/ppermute | solution.py:250
  34.4 1.6 %collective-permute-done.12 = f32[8,896]{1,0:T(8,128)S(1)} collective-permute-done((f32[8,896]{1,0:T(8,128)S(1)}, f32[8,896]{1,0:T(8,128)S(1)}, u32[]{:S(2)}, u32[]{:S(2)}) %collective-permute-start.12) | collective-permute-done | bytes 28704 | tf_op jit(solution)/shard_map/ppermute | solution.py:250
  36.0 0.0 collective-permute-done.11
  36.1 2.9 %collective-permute-start.14 = (f32[8,896]{1,0:T(8,128)S(1)}, f32[8,896]{1,0:T(8,128)S(1)}, u32[]{:S(2)}, u32[]{:S(2)}) collective-permute-start(f32[8,896]{1,0:T(8,128)S(1)} %add_add_fusion.one_ref), channel_id=1, source_target_pairs={{0,9},{1,8},{2,11},{3,10},{4,13},{5,12},{6,15},{7,14},{8,1},{9,0},... | collective-permute-start | bytes 86024 | tf_op jit(solution)/shard_map/ppermute | solution.py:250
  38.9 1.3 %products_store.1 = f32[33,16,1024]{2,1,0:T(8,128)} custom-call(s32[1]{0:T(128)} %bitcast.side_ref, f32[16,16,1024]{2,1,0:T(8,128)S(1)} %get-tuple-element.23.mine_ref, f32[16,16,1024]{2,1,0:T(8,128)S(1)} %get-tuple-element.25.theirs_ref, f32[1,16,1024]{2,1,0:T(8,128)S(1)} %get-tuple-element.26.last_ref), custom_call_target="tpu_custom_call" | custom-call | bytes 2162688 | tf_op jit(solution)/shard_map/products_store/pallas_call | solution.py:349
  40.3 0.2 collective-permute-done.14.two_ref
  40.5 1.1 %gram_unpack.1 = f32[16,16,33]{2,1,0:T(8,128)} custom-call(f32[8,896]{1,0:T(8,128)S(1)} %add_add_fusion.one_ref, f32[8,896]{1,0:T(8,128)S(1)} %collective-permute-done.14.two_ref), custom_call_target="tpu_custom_call" | custom-call | tf_op jit(solution)/shard_map/gram_unpack/pallas_call | solution.py:368
  (11 shorter events, 0.1 us)
Async XLA Ops:
  0.6 2.3 %copy-start = (s32[32,1024]{1,0:T(8,128)S(1)}, s32[32,1024]{1,0:T(8,128)}, u32[]{:S(2)}) copy-start(s32[32,1024]{1,0:T(8,128)} %signs_ref.3) | copy-start | bytes 393220
  0.7 2.3 %copy-start.1 = (f32[1024]{0:T(1024)S(1)}, f32[1024]{0:T(1024)}, u32[]{:S(2)}) copy-start(f32[1024]{0:T(1024)} %param.8) | copy-start | bytes 12292
  3.6 17.9 %copy-start.2 = (f32[2048]{0:T(1024)S(1)}, f32[2048]{0:T(1024)}, u32[]{:S(2)}) copy-start(f32[2048]{0:T(1024)} %param.9) | copy-start | bytes 24580
  3.6 17.9 %copy-start.3 = (f32[2048]{0:T(1024)S(1)}, f32[2048]{0:T(1024)}, u32[]{:S(2)}) copy-start(f32[2048]{0:T(1024)} %param.10) | copy-start | bytes 24580
  3.6 17.9 %copy-start.4 = (s32[2048]{0:T(1024)S(1)}, s32[2048]{0:T(1024)}, u32[]{:S(2)}) copy-start(s32[2048]{0:T(1024)} %param.11) | copy-start | bytes 24580
  3.6 3.2 %collective-permute-start = (f32[16,1152]{1,0:T(8,128)S(1)}, f32[16,1152]{1,0:T(8,128)S(1)}, u32[]{:S(2)}, u32[]{:S(2)}) collective-permute-start(f32[16,1152]{1,0:T(8,128)S(1)} %get-tuple-element.16), channel_id=1, source_target_pairs={{0,1},{1,0},{2,3},{3,2},{4,5},{5,4},{6,7},{7,6},{8,9},{9,8},{10,11... | collective-permute-start | bytes 221192 | tf_op jit(solution)/shard_map/ppermute | solution.py:250
  6.6 2.8 %collective-permute-start.4 = (f32[16,1152]{1,0:T(8,128)S(1)}, f32[16,1152]{1,0:T(8,128)S(1)}, u32[]{:S(2)}, u32[]{:S(2)}) collective-permute-start(f32[16,1152]{1,0:T(8,128)S(1)} %get-tuple-element.18), channel_id=1, source_target_pairs={{0,1},{1,0},{2,3},{3,2},{4,5},{5,4},{6,7},{7,6},{8,9},{9,8},{10,11... | collective-permute-start | bytes 221192 | tf_op jit(solution)/shard_map/ppermute | solution.py:250
  6.8 4.7 %collective-permute-start.1 = (f32[16,1152]{1,0:T(8,128)S(1)}, f32[16,1152]{1,0:T(8,128)S(1)}, u32[]{:S(2)}, u32[]{:S(2)}) collective-permute-start(f32[16,1152]{1,0:T(8,128)S(1)} %add.36), channel_id=1, source_target_pairs={{0,3},{1,4},{2,7},{3,0},{4,1},{5,6},{6,5},{7,2},{8,13},{9,10},{10,... | collective-permute-start | bytes 221192 | tf_op jit(solution)/shard_map/ppermute | solution.py:250
  9.5 4.0 %collective-permute-start.5 = (f32[16,1152]{1,0:T(8,128)S(1)}, f32[16,1152]{1,0:T(8,128)S(1)}, u32[]{:S(2)}, u32[]{:S(2)}) collective-permute-start(f32[16,1152]{1,0:T(8,128)S(1)} %add.40), channel_id=1, source_target_pairs={{0,5},{1,8},{2,11},{3,6},{4,13},{5,0},{6,3},{7,14},{8,1},{9,12},{1... | collective-permute-start | bytes 221192 | tf_op jit(solution)/shard_map/ppermute | solution.py:250
  11.5 4.7 %collective-permute-start.2 = (f32[16,1152]{1,0:T(8,128)S(1)}, f32[16,1152]{1,0:T(8,128)S(1)}, u32[]{:S(2)}, u32[]{:S(2)}) collective-permute-start(f32[16,1152]{1,0:T(8,128)S(1)} %add.37), channel_id=1, source_target_pairs={{0,5},{1,8},{2,11},{3,6},{4,13},{5,0},{6,3},{7,14},{8,1},{9,12},{1... | collective-permute-start | bytes 221192 | tf_op jit(solution)/shard_map/ppermute | solution.py:250
  13.5 5.5 %collective-permute-start.6 = (f32[16,1152]{1,0:T(8,128)S(1)}, f32[16,1152]{1,0:T(8,128)S(1)}, u32[]{:S(2)}, u32[]{:S(2)}) collective-permute-start(f32[16,1152]{1,0:T(8,128)S(1)} %add.41), channel_id=1, source_target_pairs={{0,3},{1,4},{2,7},{3,0},{4,1},{5,6},{6,5},{7,2},{8,13},{9,10},{10,... | collective-permute-start | bytes 221192 | tf_op jit(solution)/shard_map/ppermute | solution.py:250
  16.2 4.8 %collective-permute-start.3 = (f32[16,1152]{1,0:T(8,128)S(1)}, f32[16,1152]{1,0:T(8,128)S(1)}, u32[]{:S(2)}, u32[]{:S(2)}) collective-permute-start(f32[16,1152]{1,0:T(8,128)S(1)} %add.38), channel_id=1, source_target_pairs={{0,9},{1,2},{2,1},{3,10},{4,7},{5,12},{6,15},{7,4},{8,11},{9,0},{1... | collective-permute-start | bytes 221192 | tf_op jit(solution)/shard_map/ppermute | solution.py:250
  19.0 5.4 %collective-permute-start.7 = (f32[16,1152]{1,0:T(8,128)S(1)}, f32[16,1152]{1,0:T(8,128)S(1)}, u32[]{:S(2)}, u32[]{:S(2)}) collective-permute-start(f32[16,1152]{1,0:T(8,128)S(1)} %add.42), channel_id=1, source_target_pairs={{0,9},{1,2},{2,1},{3,10},{4,7},{5,12},{6,15},{7,4},{8,11},{9,0},{1... | collective-permute-start | bytes 221192 | tf_op jit(solution)/shard_map/ppermute | solution.py:250
  21.1 1.8 %collective-permute-start.8 = (f32[16,1152]{1,0:T(8,128)S(1)}, f32[16,1152]{1,0:T(8,128)S(1)}, u32[]{:S(2)}, u32[]{:S(2)}) collective-permute-start(f32[16,1152]{1,0:T(8,128)S(1)} %add.39.sums_a), channel_id=1, source_target_pairs={{0,1},{1,0},{2,3},{3,2},{4,5},{5,4},{6,7},{7,6},{8,9},{9,8},{10,11... | collective-permute-start | bytes 221192 | tf_op jit(solution)/shard_map/ppermute | solution.py:250
  24.4 2.1 %collective-permute-start.9 = (f32[16,1152]{1,0:T(8,128)S(1)}, f32[16,1152]{1,0:T(8,128)S(1)}, u32[]{:S(2)}, u32[]{:S(2)}) collective-permute-start(f32[16,1152]{1,0:T(8,128)S(1)} %add.43.own_b), channel_id=1, source_target_pairs={{0,1},{1,0},{2,3},{3,2},{4,5},{5,4},{6,7},{7,6},{8,9},{9,8},{10,11... | collective-permute-start | bytes 221192 | tf_op jit(solution)/shard_map/ppermute | solution.py:250
  28.3 1.3 %collective-permute-start.10 = (f32[8,896]{1,0:T(8,128)S(1)}, f32[8,896]{1,0:T(8,128)S(1)}, u32[]{:S(2)}, u32[]{:S(2)}) collective-permute-start(f32[8,896]{1,0:T(8,128)S(1)} %get-tuple-element.27), channel_id=1, source_target_pairs={{0,1},{1,0},{2,3},{3,2},{4,5},{5,4},{6,7},{7,6},{8,9},{9,8},{10,11... | collective-permute-start | bytes 86024 | tf_op jit(solution)/shard_map/ppermute | solution.py:250
  29.6 4.8 %collective-permute-start.13 = (f32[8,896]{1,0:T(8,128)S(1)}, f32[8,896]{1,0:T(8,128)S(1)}, u32[]{:S(2)}, u32[]{:S(2)}) collective-permute-start(f32[8,896]{1,0:T(8,128)S(1)} %add.44), channel_id=1, source_target_pairs={{0,7},{1,6},{2,5},{3,4},{4,3},{5,2},{6,1},{7,0},{8,15},{9,14},{10,... | collective-permute-start | bytes 86024 | tf_op jit(solution)/shard_map/ppermute | solution.py:250
  32.7 3.3 %collective-permute-start.12 = (f32[8,896]{1,0:T(8,128)S(1)}, f32[8,896]{1,0:T(8,128)S(1)}, u32[]{:S(2)}, u32[]{:S(2)}) collective-permute-start(f32[8,896]{1,0:T(8,128)S(1)} %add.44), channel_id=1, source_target_pairs={{0,5},{1,4},{2,7},{3,6},{4,1},{5,0},{6,3},{7,2},{8,13},{9,12},{10,... | collective-permute-start | bytes 86024 | tf_op jit(solution)/shard_map/ppermute | solution.py:250
  32.7 3.3 %collective-permute-start.11 = (f32[8,896]{1,0:T(8,128)S(1)}, f32[8,896]{1,0:T(8,128)S(1)}, u32[]{:S(2)}, u32[]{:S(2)}) collective-permute-start(f32[8,896]{1,0:T(8,128)S(1)} %add.44), channel_id=1, source_target_pairs={{0,3},{1,2},{2,1},{3,0},{4,7},{5,6},{6,5},{7,4},{8,11},{9,10},{10,... | collective-permute-start | bytes 86024 | tf_op jit(solution)/shard_map/ppermute | solution.py:250
  36.1 4.4 %collective-permute-start.14 = (f32[8,896]{1,0:T(8,128)S(1)}, f32[8,896]{1,0:T(8,128)S(1)}, u32[]{:S(2)}, u32[]{:S(2)}) collective-permute-start(f32[8,896]{1,0:T(8,128)S(1)} %add_add_fusion.one_ref), channel_id=1, source_target_pairs={{0,9},{1,8},{2,11},{3,10},{4,13},{5,12},{6,15},{7,14},{8,1},{9,0},... | collective-permute-start | bytes 86024 | tf_op jit(solution)/shard_map/ppermute | solution.py:250

commit v6 on v5

--- a/solution.py
+++ b/solution.py
@@ -308,9 +308,9 @@
     )
     own_a = own_a + exchange(other_a, 1)
     own_b = own_b + exchange(other_b, 1)
-    swapped = flips[1:2] + flips[:1] + flips[2:]
+    turned, back = flips[1:] + flips[:1], flips[-1:] + flips[:-1]
     received = None
-    for a_even, a_odd, b_even, b_odd in zip(flips, flips[1:] + flips[:1], swapped, flips[::-1]):
+    for a_even, a_odd, b_even, b_odd in zip(turned, flips, back, flips):
         own_a = own_a + exchange(own_a, a_even | 1, a_odd | 1)
         if received is not None:
             own_b = own_b + received

time: 41.8 us -> 41.4 us (level)
  waiting for transfers between devices: 5.85 us -> 4.35 us
  starting transfers between devices: 20.3 us -> 21.4 us
    ppermute x15, waiting for transfers between devices: 5.85 us -> 4.35 us  [exchange(): return lax.ppermute(x, 'samp', pairs)]
    ppermute x15, starting transfers between devices: 20.3 us -> 21.4 us  [exchange(): return lax.ppermute(x, 'samp', pairs)]
  transfers between devices with their start and end apart: 15 -> 15, of which waited for: 8 -> 7; matrix products, arithmetic and copies ran while one was open for 0% -> 0% of each run, Pallas kernels for 21% -> 21%
where the time goes in v6:
time: 41.4 us; the launch traced here: 41.2 us
  starting transfers between devices  21.4 us (52%)
  Pallas kernels  14.5 us (35%)
  waiting for transfers between devices  4.35 us (11%)
  between operations  0.78 us (2%)
    ppermute x15, starting transfers between devices, exchange(): return lax.ppermute(x, 'samp', pairs)  21.4 us
    pallas_call x7, Pallas kernels, local(): pl.pallas_call(functools.partial(kernel, **options), out_shape=out_shape,...  12.1 us
    ppermute x15, waiting for transfers between devices, exchange(): return lax.ppermute(x, 'samp', pairs)  4.35 us
    pallas_call x1, Pallas kernels, shards(): pl.pallas_call(store_kernel, out_shape=jax.ShapeDtypeStruct((probes + 1,...  1.34 us
    pallas_call x1, Pallas kernels, shards(): pl.pallas_call(functools.partial(unpack_kernel, pairs=2 * rows // (2 * LA...  1.12 us
  transfers between devices with their start and end apart: 15, of which 7 were waited for; matrix products, arithmetic and copies ran while one was open for 0% of the time, Pallas kernels for 21%

profile of v6, /device:TPU:0, one launch (start us, length us, event | category | flops | bytes accessed | tf_op | source)
XLA Modules:
  0.0 41.2 jit_solution(14193628249808577494)
XLA Ops:
  0.6 0.0 copy-start
  0.7 0.0 copy-start.1
  0.7 2.3 %narrow_first.1.narrow_ref.geno_a = bf16[1024,1024]{1,0:T(8,128)(2,1)S(1)} custom-call(s32[1024,2048]{1,0:T(8,128)} %geno_hbm.3), custom_call_target="tpu_custom_call" | custom-call | bytes 6291456 | tf_op jit(solution)/shard_map/narrow_first/pallas_call | solution.py:277
  3.0 0.0 copy-done
  3.0 0.0 copy-done.1
  3.0 0.6 %sums_first.1 = (f32[16,1152]{1,0:T(8,128)S(1)}, f32[16,1152]{1,0:T(8,128)S(1)}) custom-call(s32[1]{0:T(128)} %bitcast.side_ref, bf16[1024,1024]{1,0:T(8,128)(2,1)S(1)} %narrow_first.1.narrow_ref.geno_a, s32[32,1024]{1,0:T(8,128)S(1)} %copy-done, f32[1,1024]{1,0:T(1,128)S(1)} %bitcast.6), custom_call_target="tpu_custom_call" | custom-call | flops 67108864 | bytes 2097152 | tf_op jit(solution)/shard_map/sums_first/pallas_call | solution.py:277
  3.6 0.0 copy-start.2
  3.6 0.0 copy-start.3
  3.6 0.5 %collective-permute-start = (f32[16,1152]{1,0:T(8,128)S(1)}, f32[16,1152]{1,0:T(8,128)S(1)}, u32[]{:S(2)}, u32[]{:S(2)}) collective-permute-start(f32[16,1152]{1,0:T(8,128)S(1)} %get-tuple-element.16), channel_id=1, source_target_pairs={{0,1},{1,0},{2,3},{3,2},{4,5},{5,4},{6,7},{7,6},{8,9},{9,8},{10,11... | collective-permute-start | bytes 221192 | tf_op jit(solution)/shard_map/ppermute | solution.py:250
  4.1 2.6 %sums_second.1 = (f32[16,1152]{1,0:T(8,128)S(1)}, f32[16,1152]{1,0:T(8,128)S(1)}, bf16[1024,1024]{1,0:T(8,128)(2,1)S(1)}) custom-call(s32[1]{0:T(128)} %bitcast.side_ref, s32[1024,2048]{1,0:T(8,128)} %geno_hbm.3, s32[32,1024]{1,0:T(8,128)S(1)} %copy-done, f32[1,1024]{1,0:T(1,128)S(1)} %bitcast.7), custom_call_target="tpu_custom_call" | custom-call | flops 67108864 | bytes 6291456 | tf_op jit(solution)/shard_map/sums_second/pallas_call | solution.py:277
  6.6 0.1 collective-permute-start.4
  6.8 0.0 collective-permute-done
  6.8 2.7 %collective-permute-start.1 = (f32[16,1152]{1,0:T(8,128)S(1)}, f32[16,1152]{1,0:T(8,128)S(1)}, u32[]{:S(2)}, u32[]{:S(2)}) collective-permute-start(f32[16,1152]{1,0:T(8,128)S(1)} %add.36), channel_id=1, source_target_pairs={{0,5},{1,2},{2,1},{3,6},{4,7},{5,0},{6,3},{7,4},{8,11},{9,12},{10,... | collective-permute-start | bytes 221192 | tf_op jit(solution)/shard_map/ppermute | solution.py:250
  9.5 0.0 collective-permute-done.4
  9.5 2.7 %collective-permute-start.5 = (f32[16,1152]{1,0:T(8,128)S(1)}, f32[16,1152]{1,0:T(8,128)S(1)}, u32[]{:S(2)}, u32[]{:S(2)}) collective-permute-start(f32[16,1152]{1,0:T(8,128)S(1)} %add.40), channel_id=1, source_target_pairs={{0,9},{1,2},{2,1},{3,10},{4,7},{5,12},{6,15},{7,4},{8,11},{9,0},{1... | collective-permute-start | bytes 221192 | tf_op jit(solution)/shard_map/ppermute | solution.py:250
  12.3 0.0 collective-permute-done.1
  12.3 2.2 %collective-permute-start.2 = (f32[16,1152]{1,0:T(8,128)S(1)}, f32[16,1152]{1,0:T(8,128)S(1)}, u32[]{:S(2)}, u32[]{:S(2)}) collective-permute-start(f32[16,1152]{1,0:T(8,128)S(1)} %add.37), channel_id=1, source_target_pairs={{0,9},{1,4},{2,7},{3,10},{4,1},{5,12},{6,15},{7,2},{8,13},{9,0},{1... | collective-permute-start | bytes 221192 | tf_op jit(solution)/shard_map/ppermute | solution.py:250
  14.5 0.0 collective-permute-done.5
  14.5 2.3 %collective-permute-start.6 = (f32[16,1152]{1,0:T(8,128)S(1)}, f32[16,1152]{1,0:T(8,128)S(1)}, u32[]{:S(2)}, u32[]{:S(2)}) collective-permute-start(f32[16,1152]{1,0:T(8,128)S(1)} %add.41), channel_id=1, source_target_pairs={{0,3},{1,4},{2,7},{3,0},{4,1},{5,6},{6,5},{7,2},{8,13},{9,10},{10,... | collective-permute-start | bytes 221192 | tf_op jit(solution)/shard_map/ppermute | solution.py:250
  16.8 0.3 collective-permute-done.2
  17.1 1.9 %collective-permute-start.3 = (f32[16,1152]{1,0:T(8,128)S(1)}, f32[16,1152]{1,0:T(8,128)S(1)}, u32[]{:S(2)}, u32[]{:S(2)}) collective-permute-start(f32[16,1152]{1,0:T(8,128)S(1)} %add.38), channel_id=1, source_target_pairs={{0,3},{1,8},{2,11},{3,0},{4,13},{5,6},{6,5},{7,14},{8,1},{9,10},{1... | collective-permute-start | bytes 221192 | tf_op jit(solution)/shard_map/ppermute | solution.py:250
  19.0 0.0 collective-permute-done.6
  19.0 1.3 %collective-permute-start.7 = (f32[16,1152]{1,0:T(8,128)S(1)}, f32[16,1152]{1,0:T(8,128)S(1)}, u32[]{:S(2)}, u32[]{:S(2)}) collective-permute-start(f32[16,1152]{1,0:T(8,128)S(1)} %add.42), channel_id=1, source_target_pairs={{0,5},{1,8},{2,11},{3,6},{4,13},{5,0},{6,3},{7,14},{8,1},{9,12},{1... | collective-permute-start | bytes 221192 | tf_op jit(solution)/shard_map/ppermute | solution.py:250
  20.3 0.7 %collective-permute-done.3 = f32[16,1152]{1,0:T(8,128)S(1)} collective-permute-done((f32[16,1152]{1,0:T(8,128)S(1)}, f32[16,1152]{1,0:T(8,128)S(1)}, u32[]{:S(2)}, u32[]{:S(2)}) %collective-permute-start.3) | collective-permute-done | bytes 73760 | tf_op jit(solution)/shard_map/ppermute | solution.py:250
  21.0 1.3 %collective-permute-start.8 = (f32[16,1152]{1,0:T(8,128)S(1)}, f32[16,1152]{1,0:T(8,128)S(1)}, u32[]{:S(2)}, u32[]{:S(2)}) collective-permute-start(f32[16,1152]{1,0:T(8,128)S(1)} %add.39.sums_a), channel_id=1, source_target_pairs={{0,1},{1,0},{2,3},{3,2},{4,5},{5,4},{6,7},{7,6},{8,9},{9,8},{10,11... | collective-permute-start | bytes 221192 | tf_op jit(solution)/shard_map/ppermute | solution.py:250
  22.3 0.0 copy-done.2
  22.4 0.0 copy-done.3
  22.4 0.0 copy-done.4
  22.4 1.4 %products_part.1.own_part = f32[256,1024]{1,0:T(8,128)S(1)} custom-call(f32[16,1152]{1,0:T(8,128)S(1)} %add.39.sums_a, bf16[1024,1024]{1,0:T(8,128)(2,1)S(1)} %narrow_first.1.narrow_ref.geno_a, f32[1,2048]{1,0:T(1,128)S(1)} %bitcast.8, f32[1,2048]{1,0:T(1,128)S(1)} %bitcast.12, s32[1,2048]{1,0:T(1,128)S(1)} %bitcast.16), custom_call_target="tpu_custom_call" | custom-call | flops 1073741824 | bytes 1048576 | tf_op jit(solution)/shard_map/products_part/pallas_call | solution.py:277
  23.7 0.0 collective-permute-done.8.sums_a
  23.8 1.4 %products_part_other.1.other_part.part_ref = f32[272,1024]{1,0:T(8,128)S(1)} custom-call(f32[16,1152]{1,0:T(8,128)S(1)} %collective-permute-done.8.sums_a, bf16[1024,1024]{1,0:T(8,128)(2,1)S(1)} %narrow_first.1.narrow_ref.geno_a, f32[1,2048]{1,0:T(1,128)S(1)} %bitcast.9, f32[1,2048]{1,0:T(1,128)S(1)} %bitcast.13, s32[1,2048]{1,0:T(1,128)S(1)} %bitcast.17), custom_call_target="tpu_custom_call" | custom-call | flops 1140850688 | bytes 1114112 | tf_op jit(solution)/shard_map/products_part_other/pallas_call | solution.py:277
  25.2 0.0 collective-permute-done.7
  25.2 0.1 collective-permute-start.9
  25.3 1.9 %products_own.1 = (f32[16,16,1024]{2,1,0:T(8,128)S(1)}, f32[1,16,1024]{2,1,0:T(8,128)S(1)}, f32[8,512]{1,0:T(8,128)S(1)}) custom-call(f32[256,1024]{1,0:T(8,128)S(1)} %products_part.1.own_part, f32[272,1024]{1,0:T(8,128)S(1)} %products_part_other.1.other_part.part_ref, f32[16,1152]{1,0:T(8,128)S(1)} %add.43.own_b, ...), custom_call_target="tpu_custom_call" | custom-call | flops 1140850688 | bytes 1114112 | tf_op jit(solution)/shard_map/products_own/pallas_call | solution.py:277
  27.3 0.0 collective-permute-done.9.other_b
  27.3 1.8 %products_other.1 = (f32[16,16,1024]{2,1,0:T(8,128)S(1)}, f32[8,896]{1,0:T(8,128)S(1)}) custom-call(s32[1]{0:T(128)} %bitcast.side_ref, f32[272,1024]{1,0:T(8,128)S(1)} %products_part_other.1.other_part.part_ref, f32[16,1152]{1,0:T(8,128)S(1)} %collective-permute-done.9.other_b, bf16[1024,1024]{1,0:T(8,128)(2,1)S(1)} %get-tuple-element.22.geno_b, ...), custom_call_target="tpu_custom_call" | custom-call | flops 1073741824 | bytes 1048576 | tf_op jit(solution)/shard_map/products_other/pallas_call | solution.py:277
  29.1 0.5 %collective-permute-start.10 = (f32[8,896]{1,0:T(8,128)S(1)}, f32[8,896]{1,0:T(8,128)S(1)}, u32[]{:S(2)}, u32[]{:S(2)}) collective-permute-start(f32[8,896]{1,0:T(8,128)S(1)} %get-tuple-element.27), channel_id=1, source_target_pairs={{0,1},{1,0},{2,3},{3,2},{4,5},{5,4},{6,7},{7,6},{8,9},{9,8},{10,11... | collective-permute-start | bytes 86024 | tf_op jit(solution)/shard_map/ppermute | solution.py:250
  29.6 0.9 %collective-permute-done.10 = f32[8,896]{1,0:T(8,128)S(1)} collective-permute-done((f32[8,896]{1,0:T(8,128)S(1)}, f32[8,896]{1,0:T(8,128)S(1)}, u32[]{:S(2)}, u32[]{:S(2)}) %collective-permute-start.10) | collective-permute-done | bytes 28704 | tf_op jit(solution)/shard_map/ppermute | solution.py:250
  30.4 1.5 %collective-permute-start.13 = (f32[8,896]{1,0:T(8,128)S(1)}, f32[8,896]{1,0:T(8,128)S(1)}, u32[]{:S(2)}, u32[]{:S(2)}) collective-permute-start(f32[8,896]{1,0:T(8,128)S(1)} %add.44), channel_id=1, source_target_pairs={{0,7},{1,6},{2,5},{3,4},{4,3},{5,2},{6,1},{7,0},{8,15},{9,14},{10,... | collective-permute-start | bytes 86024 | tf_op jit(solution)/shard_map/ppermute | solution.py:250
  32.0 0.5 %collective-permute-start.12 = (f32[8,896]{1,0:T(8,128)S(1)}, f32[8,896]{1,0:T(8,128)S(1)}, u32[]{:S(2)}, u32[]{:S(2)}) collective-permute-start(f32[8,896]{1,0:T(8,128)S(1)} %add.44), channel_id=1, source_target_pairs={{0,5},{1,4},{2,7},{3,6},{4,1},{5,0},{6,3},{7,2},{8,13},{9,12},{10,... | collective-permute-start | bytes 86024 | tf_op jit(solution)/shard_map/ppermute | solution.py:250
  32.5 1.1 %collective-permute-start.11 = (f32[8,896]{1,0:T(8,128)S(1)}, f32[8,896]{1,0:T(8,128)S(1)}, u32[]{:S(2)}, u32[]{:S(2)}) collective-permute-start(f32[8,896]{1,0:T(8,128)S(1)} %add.44), channel_id=1, source_target_pairs={{0,3},{1,2},{2,1},{3,0},{4,7},{5,6},{6,5},{7,4},{8,11},{9,10},{10,... | collective-permute-start | bytes 86024 | tf_op jit(solution)/shard_map/ppermute | solution.py:250
  33.6 1.0 %collective-permute-done.13 = f32[8,896]{1,0:T(8,128)S(1)} collective-permute-done((f32[8,896]{1,0:T(8,128)S(1)}, f32[8,896]{1,0:T(8,128)S(1)}, u32[]{:S(2)}, u32[]{:S(2)}) %collective-permute-start.13) | collective-permute-done | bytes 28704 | tf_op jit(solution)/shard_map/ppermute | solution.py:250
  34.6 0.6 %collective-permute-done.12 = f32[8,896]{1,0:T(8,128)S(1)} collective-permute-done((f32[8,896]{1,0:T(8,128)S(1)}, f32[8,896]{1,0:T(8,128)S(1)}, u32[]{:S(2)}, u32[]{:S(2)}) %collective-permute-start.12) | collective-permute-done | bytes 28704 | tf_op jit(solution)/shard_map/ppermute | solution.py:250
  35.3 0.5 %collective-permute-done.11 = f32[8,896]{1,0:T(8,128)S(1)} collective-permute-done((f32[8,896]{1,0:T(8,128)S(1)}, f32[8,896]{1,0:T(8,128)S(1)}, u32[]{:S(2)}, u32[]{:S(2)}) %collective-permute-start.11) | collective-permute-done | bytes 28704 | tf_op jit(solution)/shard_map/ppermute | solution.py:250
  35.8 2.7 %collective-permute-start.14 = (f32[8,896]{1,0:T(8,128)S(1)}, f32[8,896]{1,0:T(8,128)S(1)}, u32[]{:S(2)}, u32[]{:S(2)}) collective-permute-start(f32[8,896]{1,0:T(8,128)S(1)} %add_add_fusion.one_ref), channel_id=1, source_target_pairs={{0,9},{1,8},{2,11},{3,10},{4,13},{5,12},{6,15},{7,14},{8,1},{9,0},... | collective-permute-start | bytes 86024 | tf_op jit(solution)/shard_map/ppermute | solution.py:250
  38.5 1.3 %products_store.1 = f32[33,16,1024]{2,1,0:T(8,128)} custom-call(s32[1]{0:T(128)} %bitcast.side_ref, f32[16,16,1024]{2,1,0:T(8,128)S(1)} %get-tuple-element.23.mine_ref, f32[16,16,1024]{2,1,0:T(8,128)S(1)} %get-tuple-element.25.theirs_ref, f32[1,16,1024]{2,1,0:T(8,128)S(1)} %get-tuple-element.26.last_ref), custom_call_target="tpu_custom_call" | custom-call | bytes 2162688 | tf_op jit(solution)/shard_map/products_store/pallas_call | solution.py:349
  39.8 0.2 collective-permute-done.14.two_ref
  40.1 1.1 %gram_unpack.1 = f32[16,16,33]{2,1,0:T(8,128)} custom-call(f32[8,896]{1,0:T(8,128)S(1)} %add_add_fusion.one_ref, f32[8,896]{1,0:T(8,128)S(1)} %collective-permute-done.14.two_ref), custom_call_target="tpu_custom_call" | custom-call | tf_op jit(solution)/shard_map/gram_unpack/pallas_call | solution.py:368
  (11 shorter events, 0.1 us)
Async XLA Ops:
  0.6 2.3 %copy-start = (s32[32,1024]{1,0:T(8,128)S(1)}, s32[32,1024]{1,0:T(8,128)}, u32[]{:S(2)}) copy-start(s32[32,1024]{1,0:T(8,128)} %signs_ref.3) | copy-start | bytes 393220
  0.7 2.3 %copy-start.1 = (f32[1024]{0:T(1024)S(1)}, f32[1024]{0:T(1024)}, u32[]{:S(2)}) copy-start(f32[1024]{0:T(1024)} %param.8) | copy-start | bytes 12292
  3.6 18.7 %copy-start.2 = (f32[2048]{0:T(1024)S(1)}, f32[2048]{0:T(1024)}, u32[]{:S(2)}) copy-start(f32[2048]{0:T(1024)} %param.9) | copy-start | bytes 24580
  3.6 18.7 %copy-start.3 = (f32[2048]{0:T(1024)S(1)}, f32[2048]{0:T(1024)}, u32[]{:S(2)}) copy-start(f32[2048]{0:T(1024)} %param.10) | copy-start | bytes 24580
  3.6 18.7 %copy-start.4 = (s32[2048]{0:T(1024)S(1)}, s32[2048]{0:T(1024)}, u32[]{:S(2)}) copy-start(s32[2048]{0:T(1024)} %param.11) | copy-start | bytes 24580
  3.6 3.2 %collective-permute-start = (f32[16,1152]{1,0:T(8,128)S(1)}, f32[16,1152]{1,0:T(8,128)S(1)}, u32[]{:S(2)}, u32[]{:S(2)}) collective-permute-start(f32[16,1152]{1,0:T(8,128)S(1)} %get-tuple-element.16), channel_id=1, source_target_pairs={{0,1},{1,0},{2,3},{3,2},{4,5},{5,4},{6,7},{7,6},{8,9},{9,8},{10,11... | collective-permute-start | bytes 221192 | tf_op jit(solution)/shard_map/ppermute | solution.py:250
  6.6 2.9 %collective-permute-start.4 = (f32[16,1152]{1,0:T(8,128)S(1)}, f32[16,1152]{1,0:T(8,128)S(1)}, u32[]{:S(2)}, u32[]{:S(2)}) collective-permute-start(f32[16,1152]{1,0:T(8,128)S(1)} %get-tuple-element.18), channel_id=1, source_target_pairs={{0,1},{1,0},{2,3},{3,2},{4,5},{5,4},{6,7},{7,6},{8,9},{9,8},{10,11... | collective-permute-start | bytes 221192 | tf_op jit(solution)/shard_map/ppermute | solution.py:250
  6.8 5.5 %collective-permute-start.1 = (f32[16,1152]{1,0:T(8,128)S(1)}, f32[16,1152]{1,0:T(8,128)S(1)}, u32[]{:S(2)}, u32[]{:S(2)}) collective-permute-start(f32[16,1152]{1,0:T(8,128)S(1)} %add.36), channel_id=1, source_target_pairs={{0,5},{1,2},{2,1},{3,6},{4,7},{5,0},{6,3},{7,4},{8,11},{9,12},{10,... | collective-permute-start | bytes 221192 | tf_op jit(solution)/shard_map/ppermute | solution.py:250
  9.5 4.9 %collective-permute-start.5 = (f32[16,1152]{1,0:T(8,128)S(1)}, f32[16,1152]{1,0:T(8,128)S(1)}, u32[]{:S(2)}, u32[]{:S(2)}) collective-permute-start(f32[16,1152]{1,0:T(8,128)S(1)} %add.40), channel_id=1, source_target_pairs={{0,9},{1,2},{2,1},{3,10},{4,7},{5,12},{6,15},{7,4},{8,11},{9,0},{1... | collective-permute-start | bytes 221192 | tf_op jit(solution)/shard_map/ppermute | solution.py:250
  12.3 4.8 %collective-permute-start.2 = (f32[16,1152]{1,0:T(8,128)S(1)}, f32[16,1152]{1,0:T(8,128)S(1)}, u32[]{:S(2)}, u32[]{:S(2)}) collective-permute-start(f32[16,1152]{1,0:T(8,128)S(1)} %add.37), channel_id=1, source_target_pairs={{0,9},{1,4},{2,7},{3,10},{4,1},{5,12},{6,15},{7,2},{8,13},{9,0},{1... | collective-permute-start | bytes 221192 | tf_op jit(solution)/shard_map/ppermute | solution.py:250
  14.5 4.5 %collective-permute-start.6 = (f32[16,1152]{1,0:T(8,128)S(1)}, f32[16,1152]{1,0:T(8,128)S(1)}, u32[]{:S(2)}, u32[]{:S(2)}) collective-permute-start(f32[16,1152]{1,0:T(8,128)S(1)} %add.41), channel_id=1, source_target_pairs={{0,3},{1,4},{2,7},{3,0},{4,1},{5,6},{6,5},{7,2},{8,13},{9,10},{10,... | collective-permute-start | bytes 221192 | tf_op jit(solution)/shard_map/ppermute | solution.py:250
  17.1 3.9 %collective-permute-start.3 = (f32[16,1152]{1,0:T(8,128)S(1)}, f32[16,1152]{1,0:T(8,128)S(1)}, u32[]{:S(2)}, u32[]{:S(2)}) collective-permute-start(f32[16,1152]{1,0:T(8,128)S(1)} %add.38), channel_id=1, source_target_pairs={{0,3},{1,8},{2,11},{3,0},{4,13},{5,6},{6,5},{7,14},{8,1},{9,10},{1... | collective-permute-start | bytes 221192 | tf_op jit(solution)/shard_map/ppermute | solution.py:250
  19.0 6.2 %collective-permute-start.7 = (f32[16,1152]{1,0:T(8,128)S(1)}, f32[16,1152]{1,0:T(8,128)S(1)}, u32[]{:S(2)}, u32[]{:S(2)}) collective-permute-start(f32[16,1152]{1,0:T(8,128)S(1)} %add.42), channel_id=1, source_target_pairs={{0,5},{1,8},{2,11},{3,6},{4,13},{5,0},{6,3},{7,14},{8,1},{9,12},{1... | collective-permute-start | bytes 221192 | tf_op jit(solution)/shard_map/ppermute | solution.py:250
  21.0 2.7 %collective-permute-start.8 = (f32[16,1152]{1,0:T(8,128)S(1)}, f32[16,1152]{1,0:T(8,128)S(1)}, u32[]{:S(2)}, u32[]{:S(2)}) collective-permute-start(f32[16,1152]{1,0:T(8,128)S(1)} %add.39.sums_a), channel_id=1, source_target_pairs={{0,1},{1,0},{2,3},{3,2},{4,5},{5,4},{6,7},{7,6},{8,9},{9,8},{10,11... | collective-permute-start | bytes 221192 | tf_op jit(solution)/shard_map/ppermute | solution.py:250
  25.2 2.1 %collective-permute-start.9 = (f32[16,1152]{1,0:T(8,128)S(1)}, f32[16,1152]{1,0:T(8,128)S(1)}, u32[]{:S(2)}, u32[]{:S(2)}) collective-permute-start(f32[16,1152]{1,0:T(8,128)S(1)} %add.43.own_b), channel_id=1, source_target_pairs={{0,1},{1,0},{2,3},{3,2},{4,5},{5,4},{6,7},{7,6},{8,9},{9,8},{10,11... | collective-permute-start | bytes 221192 | tf_op jit(solution)/shard_map/ppermute | solution.py:250
  29.1 1.3 %collective-permute-start.10 = (f32[8,896]{1,0:T(8,128)S(1)}, f32[8,896]{1,0:T(8,128)S(1)}, u32[]{:S(2)}, u32[]{:S(2)}) collective-permute-start(f32[8,896]{1,0:T(8,128)S(1)} %get-tuple-element.27), channel_id=1, source_target_pairs={{0,1},{1,0},{2,3},{3,2},{4,5},{5,4},{6,7},{7,6},{8,9},{9,8},{10,11... | collective-permute-start | bytes 86024 | tf_op jit(solution)/shard_map/ppermute | solution.py:250
  30.4 4.2 %collective-permute-start.13 = (f32[8,896]{1,0:T(8,128)S(1)}, f32[8,896]{1,0:T(8,128)S(1)}, u32[]{:S(2)}, u32[]{:S(2)}) collective-permute-start(f32[8,896]{1,0:T(8,128)S(1)} %add.44), channel_id=1, source_target_pairs={{0,7},{1,6},{2,5},{3,4},{4,3},{5,2},{6,1},{7,0},{8,15},{9,14},{10,... | collective-permute-start | bytes 86024 | tf_op jit(solution)/shard_map/ppermute | solution.py:250
  32.0 3.3 %collective-permute-start.12 = (f32[8,896]{1,0:T(8,128)S(1)}, f32[8,896]{1,0:T(8,128)S(1)}, u32[]{:S(2)}, u32[]{:S(2)}) collective-permute-start(f32[8,896]{1,0:T(8,128)S(1)} %add.44), channel_id=1, source_target_pairs={{0,5},{1,4},{2,7},{3,6},{4,1},{5,0},{6,3},{7,2},{8,13},{9,12},{10,... | collective-permute-start | bytes 86024 | tf_op jit(solution)/shard_map/ppermute | solution.py:250
  32.5 3.3 %collective-permute-start.11 = (f32[8,896]{1,0:T(8,128)S(1)}, f32[8,896]{1,0:T(8,128)S(1)}, u32[]{:S(2)}, u32[]{:S(2)}) collective-permute-start(f32[8,896]{1,0:T(8,128)S(1)} %add.44), channel_id=1, source_target_pairs={{0,3},{1,2},{2,1},{3,0},{4,7},{5,6},{6,5},{7,4},{8,11},{9,10},{10,... | collective-permute-start | bytes 86024 | tf_op jit(solution)/shard_map/ppermute | solution.py:250
  35.8 4.3 %collective-permute-start.14 = (f32[8,896]{1,0:T(8,128)S(1)}, f32[8,896]{1,0:T(8,128)S(1)}, u32[]{:S(2)}, u32[]{:S(2)}) collective-permute-start(f32[8,896]{1,0:T(8,128)S(1)} %add_add_fusion.one_ref), channel_id=1, source_target_pairs={{0,9},{1,8},{2,11},{3,10},{4,13},{5,12},{6,15},{7,14},{8,1},{9,0},... | collective-permute-start | bytes 86024 | tf_op jit(solution)/shard_map/ppermute | solution.py:250

commit v7 on v6

--- a/solution.py
+++ b/solution.py
@@ -168,26 +168,25 @@
     return jnp.concatenate(packed, axis=1)
 
 
-def unpack_kernel(one_ref, two_ref, out_ref, upper, lower, *, pairs):
+def unpack_kernel(one_ref, two_ref, out_ref, rows, *, pairs):
     h = BINS // 2
-    count = upper.shape[0] // BINS
+    count = rows.shape[0] // BINS
     packed = one_ref[...] + two_ref[...]
     tile = [packed[:, t * LANES : (t + 1) * LANES] for t in range(packed.shape[1] // LANES)]
     for p in range(pairs):
         one, two, low = tile[3 * p : 3 * p + 3]
         for i, (a, b) in enumerate(((one, low), (two, pltpu.roll(low, h, 1)))):
             at = (2 * p + i) * LANES
-            upper[at : at + LANES, :] = a.T
-            lower[at : at + LANES, :] = b.T
-    last = tile[3 * pairs].T
-    upper[2 * pairs * LANES :, :] = last[:BINS]
-    lower[2 * pairs * LANES :, :] = last[BINS : 2 * BINS]
+            rows[at : at + LANES, :] = jnp.concatenate([a, b], axis=0).T
+    last = jnp.concatenate([tile[3 * pairs], pltpu.roll(tile[3 * pairs], LANES - BINS, 1)], axis=0).T
+    rows[2 * pairs * LANES :, :] = last[:BINS]
     for l in range(BINS):
-        row = upper[pl.ds(l, count, stride=BINS), :].T
-        out_ref[:h, l, :] = row
-        if l >= h:
-            out_ref[l, :h, :] = row
-            out_ref[h:, l, :] = lower[pl.ds(l, count, stride=BINS), :].T
+        plane = rows[pl.ds(l, count, stride=BINS), :].T
+        if l < h:
+            out_ref[:h, l, :] = plane[:h]
+        else:
+            out_ref[:, l, :] = plane
+            out_ref[l, :h, :] = plane[:h]
 
 
 def part_kernel(sums_a, geno_a, mean_ref, scale_ref, bin_ref, part_ref, weights, *, norm, pheno):
@@ -370,7 +369,7 @@
         out_shape=jax.ShapeDtypeStruct((BINS, BINS, probes + 1), F32),
         in_specs=[vmem, vmem],
         out_specs=vmem,
-        scratch_shapes=[pltpu.VMEM((count, BINS // 2), F32), pltpu.VMEM((count, BINS // 2), F32)],
+        scratch_shapes=[pltpu.VMEM((count, BINS), F32)],
         compiler_params=pltpu.CompilerParams(vmem_limit_bytes=16 * MIB),
         name="gram_unpack",
     )(gram, last)

time: 41.4 us -> 41.3 us (level)
  no operation moved by 1% of the time
where the time goes in v7:
time: 41.3 us; the launch traced here: 41.1 us
  starting transfers between devices  21.4 us (52%)
  Pallas kernels  14.4 us (35%)
  waiting for transfers between devices  4.35 us (11%)
  between operations  0.78 us (2%)
    ppermute x15, starting transfers between devices, exchange(): return lax.ppermute(x, 'samp', pairs)  21.4 us
    pallas_call x7, Pallas kernels, local(): pl.pallas_call(functools.partial(kernel, **options), out_shape=out_shape,...  12.1 us
    ppermute x15, waiting for transfers between devices, exchange(): return lax.ppermute(x, 'samp', pairs)  4.35 us
    pallas_call x1, Pallas kernels, shards(): pl.pallas_call(store_kernel, out_shape=jax.ShapeDtypeStruct((probes + 1,...  1.34 us
    pallas_call x1, Pallas kernels, shards(): pl.pallas_call(functools.partial(unpack_kernel, pairs=2 * rows // (2 * LA...  1.04 us
  transfers between devices with their start and end apart: 15, of which 7 were waited for; matrix products, arithmetic and copies ran while one was open for 0% of the time, Pallas kernels for 21%

profile of v7, /device:TPU:0, one launch (start us, length us, event | category | flops | bytes accessed | tf_op | source)
XLA Modules:
  0.0 41.1 jit_solution(5783339722431824248)
XLA Ops:
  0.6 0.0 copy-start
  0.7 0.0 copy-start.1
  0.7 2.3 %narrow_first.1.narrow_ref.geno_a = bf16[1024,1024]{1,0:T(8,128)(2,1)S(1)} custom-call(s32[1024,2048]{1,0:T(8,128)} %geno_hbm.3), custom_call_target="tpu_custom_call" | custom-call | bytes 6291456 | tf_op jit(solution)/shard_map/narrow_first/pallas_call | solution.py:276
  3.0 0.0 copy-done
  3.0 0.0 copy-done.1
  3.0 0.6 %sums_first.1 = (f32[16,1152]{1,0:T(8,128)S(1)}, f32[16,1152]{1,0:T(8,128)S(1)}) custom-call(s32[1]{0:T(128)} %bitcast.side_ref, bf16[1024,1024]{1,0:T(8,128)(2,1)S(1)} %narrow_first.1.narrow_ref.geno_a, s32[32,1024]{1,0:T(8,128)S(1)} %copy-done, f32[1,1024]{1,0:T(1,128)S(1)} %bitcast.6), custom_call_target="tpu_custom_call" | custom-call | flops 67108864 | bytes 2097152 | tf_op jit(solution)/shard_map/sums_first/pallas_call | solution.py:276
  3.6 0.0 copy-start.2
  3.6 0.0 copy-start.3
  3.6 0.5 %collective-permute-start = (f32[16,1152]{1,0:T(8,128)S(1)}, f32[16,1152]{1,0:T(8,128)S(1)}, u32[]{:S(2)}, u32[]{:S(2)}) collective-permute-start(f32[16,1152]{1,0:T(8,128)S(1)} %get-tuple-element.16), channel_id=1, source_target_pairs={{0,1},{1,0},{2,3},{3,2},{4,5},{5,4},{6,7},{7,6},{8,9},{9,8},{10,11... | collective-permute-start | bytes 221192 | tf_op jit(solution)/shard_map/ppermute | solution.py:249
  4.1 2.6 %sums_second.1 = (f32[16,1152]{1,0:T(8,128)S(1)}, f32[16,1152]{1,0:T(8,128)S(1)}, bf16[1024,1024]{1,0:T(8,128)(2,1)S(1)}) custom-call(s32[1]{0:T(128)} %bitcast.side_ref, s32[1024,2048]{1,0:T(8,128)} %geno_hbm.3, s32[32,1024]{1,0:T(8,128)S(1)} %copy-done, f32[1,1024]{1,0:T(1,128)S(1)} %bitcast.7), custom_call_target="tpu_custom_call" | custom-call | flops 67108864 | bytes 6291456 | tf_op jit(solution)/shard_map/sums_second/pallas_call | solution.py:276
  6.6 0.1 collective-permute-start.4
  6.8 0.0 collective-permute-done
  6.8 2.7 %collective-permute-start.1 = (f32[16,1152]{1,0:T(8,128)S(1)}, f32[16,1152]{1,0:T(8,128)S(1)}, u32[]{:S(2)}, u32[]{:S(2)}) collective-permute-start(f32[16,1152]{1,0:T(8,128)S(1)} %add.36), channel_id=1, source_target_pairs={{0,5},{1,2},{2,1},{3,6},{4,7},{5,0},{6,3},{7,4},{8,11},{9,12},{10,... | collective-permute-start | bytes 221192 | tf_op jit(solution)/shard_map/ppermute | solution.py:249
  9.5 0.0 collective-permute-done.4
  9.5 2.7 %collective-permute-start.5 = (f32[16,1152]{1,0:T(8,128)S(1)}, f32[16,1152]{1,0:T(8,128)S(1)}, u32[]{:S(2)}, u32[]{:S(2)}) collective-permute-start(f32[16,1152]{1,0:T(8,128)S(1)} %add.40), channel_id=1, source_target_pairs={{0,9},{1,2},{2,1},{3,10},{4,7},{5,12},{6,15},{7,4},{8,11},{9,0},{1... | collective-permute-start | bytes 221192 | tf_op jit(solution)/shard_map/ppermute | solution.py:249
  12.3 0.0 collective-permute-done.1
  12.3 2.2 %collective-permute-start.2 = (f32[16,1152]{1,0:T(8,128)S(1)}, f32[16,1152]{1,0:T(8,128)S(1)}, u32[]{:S(2)}, u32[]{:S(2)}) collective-permute-start(f32[16,1152]{1,0:T(8,128)S(1)} %add.37), channel_id=1, source_target_pairs={{0,9},{1,4},{2,7},{3,10},{4,1},{5,12},{6,15},{7,2},{8,13},{9,0},{1... | collective-permute-start | bytes 221192 | tf_op jit(solution)/shard_map/ppermute | solution.py:249
  14.5 0.0 collective-permute-done.5
  14.5 2.3 %collective-permute-start.6 = (f32[16,1152]{1,0:T(8,128)S(1)}, f32[16,1152]{1,0:T(8,128)S(1)}, u32[]{:S(2)}, u32[]{:S(2)}) collective-permute-start(f32[16,1152]{1,0:T(8,128)S(1)} %add.41), channel_id=1, source_target_pairs={{0,3},{1,4},{2,7},{3,0},{4,1},{5,6},{6,5},{7,2},{8,13},{9,10},{10,... | collective-permute-start | bytes 221192 | tf_op jit(solution)/shard_map/ppermute | solution.py:249
  16.8 0.3 collective-permute-done.2
  17.1 1.9 %collective-permute-start.3 = (f32[16,1152]{1,0:T(8,128)S(1)}, f32[16,1152]{1,0:T(8,128)S(1)}, u32[]{:S(2)}, u32[]{:S(2)}) collective-permute-start(f32[16,1152]{1,0:T(8,128)S(1)} %add.38), channel_id=1, source_target_pairs={{0,3},{1,8},{2,11},{3,0},{4,13},{5,6},{6,5},{7,14},{8,1},{9,10},{1... | collective-permute-start | bytes 221192 | tf_op jit(solution)/shard_map/ppermute | solution.py:249
  19.0 0.0 collective-permute-done.6
  19.0 1.3 %collective-permute-start.7 = (f32[16,1152]{1,0:T(8,128)S(1)}, f32[16,1152]{1,0:T(8,128)S(1)}, u32[]{:S(2)}, u32[]{:S(2)}) collective-permute-start(f32[16,1152]{1,0:T(8,128)S(1)} %add.42), channel_id=1, source_target_pairs={{0,5},{1,8},{2,11},{3,6},{4,13},{5,0},{6,3},{7,14},{8,1},{9,12},{1... | collective-permute-start | bytes 221192 | tf_op jit(solution)/shard_map/ppermute | solution.py:249
  20.3 0.7 %collective-permute-done.3 = f32[16,1152]{1,0:T(8,128)S(1)} collective-permute-done((f32[16,1152]{1,0:T(8,128)S(1)}, f32[16,1152]{1,0:T(8,128)S(1)}, u32[]{:S(2)}, u32[]{:S(2)}) %collective-permute-start.3) | collective-permute-done | bytes 73760 | tf_op jit(solution)/shard_map/ppermute | solution.py:249
  21.0 1.3 %collective-permute-start.8 = (f32[16,1152]{1,0:T(8,128)S(1)}, f32[16,1152]{1,0:T(8,128)S(1)}, u32[]{:S(2)}, u32[]{:S(2)}) collective-permute-start(f32[16,1152]{1,0:T(8,128)S(1)} %add.39.sums_a), channel_id=1, source_target_pairs={{0,1},{1,0},{2,3},{3,2},{4,5},{5,4},{6,7},{7,6},{8,9},{9,8},{10,11... | collective-permute-start | bytes 221192 | tf_op jit(solution)/shard_map/ppermute | solution.py:249
  22.3 0.0 copy-done.2
  22.4 0.0 copy-done.3
  22.4 0.0 copy-done.4
  22.4 1.4 %products_part.1.own_part = f32[256,1024]{1,0:T(8,128)S(1)} custom-call(f32[16,1152]{1,0:T(8,128)S(1)} %add.39.sums_a, bf16[1024,1024]{1,0:T(8,128)(2,1)S(1)} %narrow_first.1.narrow_ref.geno_a, f32[1,2048]{1,0:T(1,128)S(1)} %bitcast.8, f32[1,2048]{1,0:T(1,128)S(1)} %bitcast.12, s32[1,2048]{1,0:T(1,128)S(1)} %bitcast.16), custom_call_target="tpu_custom_call" | custom-call | flops 1073741824 | bytes 1048576 | tf_op jit(solution)/shard_map/products_part/pallas_call | solution.py:276
  23.7 0.0 collective-permute-done.8.sums_a
  23.8 1.4 %products_part_other.1.other_part.part_ref = f32[272,1024]{1,0:T(8,128)S(1)} custom-call(f32[16,1152]{1,0:T(8,128)S(1)} %collective-permute-done.8.sums_a, bf16[1024,1024]{1,0:T(8,128)(2,1)S(1)} %narrow_first.1.narrow_ref.geno_a, f32[1,2048]{1,0:T(1,128)S(1)} %bitcast.9, f32[1,2048]{1,0:T(1,128)S(1)} %bitcast.13, s32[1,2048]{1,0:T(1,128)S(1)} %bitcast.17), custom_call_target="tpu_custom_call" | custom-call | flops 1140850688 | bytes 1114112 | tf_op jit(solution)/shard_map/products_part_other/pallas_call | solution.py:276
  25.2 0.0 collective-permute-done.7
  25.2 0.1 collective-permute-start.9
  25.3 1.9 %products_own.1 = (f32[16,16,1024]{2,1,0:T(8,128)S(1)}, f32[1,16,1024]{2,1,0:T(8,128)S(1)}, f32[8,512]{1,0:T(8,128)S(1)}) custom-call(f32[256,1024]{1,0:T(8,128)S(1)} %products_part.1.own_part, f32[272,1024]{1,0:T(8,128)S(1)} %products_part_other.1.other_part.part_ref, f32[16,1152]{1,0:T(8,128)S(1)} %add.43.own_b, ...), custom_call_target="tpu_custom_call" | custom-call | flops 1140850688 | bytes 1114112 | tf_op jit(solution)/shard_map/products_own/pallas_call | solution.py:276
  27.3 0.0 collective-permute-done.9.other_b
  27.3 1.8 %products_other.1 = (f32[16,16,1024]{2,1,0:T(8,128)S(1)}, f32[8,896]{1,0:T(8,128)S(1)}) custom-call(s32[1]{0:T(128)} %bitcast.side_ref, f32[272,1024]{1,0:T(8,128)S(1)} %products_part_other.1.other_part.part_ref, f32[16,1152]{1,0:T(8,128)S(1)} %collective-permute-done.9.other_b, bf16[1024,1024]{1,0:T(8,128)(2,1)S(1)} %get-tuple-element.22.geno_b, ...), custom_call_target="tpu_custom_call" | custom-call | flops 1073741824 | bytes 1048576 | tf_op jit(solution)/shard_map/products_other/pallas_call | solution.py:276
  29.1 0.5 %collective-permute-start.10 = (f32[8,896]{1,0:T(8,128)S(1)}, f32[8,896]{1,0:T(8,128)S(1)}, u32[]{:S(2)}, u32[]{:S(2)}) collective-permute-start(f32[8,896]{1,0:T(8,128)S(1)} %get-tuple-element.27), channel_id=1, source_target_pairs={{0,1},{1,0},{2,3},{3,2},{4,5},{5,4},{6,7},{7,6},{8,9},{9,8},{10,11... | collective-permute-start | bytes 86024 | tf_op jit(solution)/shard_map/ppermute | solution.py:249
  29.6 0.9 %collective-permute-done.10 = f32[8,896]{1,0:T(8,128)S(1)} collective-permute-done((f32[8,896]{1,0:T(8,128)S(1)}, f32[8,896]{1,0:T(8,128)S(1)}, u32[]{:S(2)}, u32[]{:S(2)}) %collective-permute-start.10) | collective-permute-done | bytes 28704 | tf_op jit(solution)/shard_map/ppermute | solution.py:249
  30.4 1.5 %collective-permute-start.13 = (f32[8,896]{1,0:T(8,128)S(1)}, f32[8,896]{1,0:T(8,128)S(1)}, u32[]{:S(2)}, u32[]{:S(2)}) collective-permute-start(f32[8,896]{1,0:T(8,128)S(1)} %add.44), channel_id=1, source_target_pairs={{0,7},{1,6},{2,5},{3,4},{4,3},{5,2},{6,1},{7,0},{8,15},{9,14},{10,... | collective-permute-start | bytes 86024 | tf_op jit(solution)/shard_map/ppermute | solution.py:249
  32.0 0.5 %collective-permute-start.12 = (f32[8,896]{1,0:T(8,128)S(1)}, f32[8,896]{1,0:T(8,128)S(1)}, u32[]{:S(2)}, u32[]{:S(2)}) collective-permute-start(f32[8,896]{1,0:T(8,128)S(1)} %add.44), channel_id=1, source_target_pairs={{0,5},{1,4},{2,7},{3,6},{4,1},{5,0},{6,3},{7,2},{8,13},{9,12},{10,... | collective-permute-start | bytes 86024 | tf_op jit(solution)/shard_map/ppermute | solution.py:249
  32.5 1.1 %collective-permute-start.11 = (f32[8,896]{1,0:T(8,128)S(1)}, f32[8,896]{1,0:T(8,128)S(1)}, u32[]{:S(2)}, u32[]{:S(2)}) collective-permute-start(f32[8,896]{1,0:T(8,128)S(1)} %add.44), channel_id=1, source_target_pairs={{0,3},{1,2},{2,1},{3,0},{4,7},{5,6},{6,5},{7,4},{8,11},{9,10},{10,... | collective-permute-start | bytes 86024 | tf_op jit(solution)/shard_map/ppermute | solution.py:249
  33.6 1.0 %collective-permute-done.13 = f32[8,896]{1,0:T(8,128)S(1)} collective-permute-done((f32[8,896]{1,0:T(8,128)S(1)}, f32[8,896]{1,0:T(8,128)S(1)}, u32[]{:S(2)}, u32[]{:S(2)}) %collective-permute-start.13) | collective-permute-done | bytes 28704 | tf_op jit(solution)/shard_map/ppermute | solution.py:249
  34.6 0.6 %collective-permute-done.12 = f32[8,896]{1,0:T(8,128)S(1)} collective-permute-done((f32[8,896]{1,0:T(8,128)S(1)}, f32[8,896]{1,0:T(8,128)S(1)}, u32[]{:S(2)}, u32[]{:S(2)}) %collective-permute-start.12) | collective-permute-done | bytes 28704 | tf_op jit(solution)/shard_map/ppermute | solution.py:249
  35.3 0.5 %collective-permute-done.11 = f32[8,896]{1,0:T(8,128)S(1)} collective-permute-done((f32[8,896]{1,0:T(8,128)S(1)}, f32[8,896]{1,0:T(8,128)S(1)}, u32[]{:S(2)}, u32[]{:S(2)}) %collective-permute-start.11) | collective-permute-done | bytes 28704 | tf_op jit(solution)/shard_map/ppermute | solution.py:249
  35.8 2.7 %collective-permute-start.14 = (f32[8,896]{1,0:T(8,128)S(1)}, f32[8,896]{1,0:T(8,128)S(1)}, u32[]{:S(2)}, u32[]{:S(2)}) collective-permute-start(f32[8,896]{1,0:T(8,128)S(1)} %add_add_fusion.one_ref), channel_id=1, source_target_pairs={{0,9},{1,8},{2,11},{3,10},{4,13},{5,12},{6,15},{7,14},{8,1},{9,0},... | collective-permute-start | bytes 86024 | tf_op jit(solution)/shard_map/ppermute | solution.py:249
  38.5 1.3 %products_store.1 = f32[33,16,1024]{2,1,0:T(8,128)} custom-call(s32[1]{0:T(128)} %bitcast.side_ref, f32[16,16,1024]{2,1,0:T(8,128)S(1)} %get-tuple-element.23.mine_ref, f32[16,16,1024]{2,1,0:T(8,128)S(1)} %get-tuple-element.25.theirs_ref, f32[1,16,1024]{2,1,0:T(8,128)S(1)} %get-tuple-element.26.last_ref), custom_call_target="tpu_custom_call" | custom-call | bytes 2162688 | tf_op jit(solution)/shard_map/products_store/pallas_call | solution.py:348
  39.8 0.2 collective-permute-done.14.two_ref
  40.1 1.0 %gram_unpack.1 = f32[16,16,33]{2,1,0:T(8,128)} custom-call(f32[8,896]{1,0:T(8,128)S(1)} %add_add_fusion.one_ref, f32[8,896]{1,0:T(8,128)S(1)} %collective-permute-done.14.two_ref), custom_call_target="tpu_custom_call" | custom-call | tf_op jit(solution)/shard_map/gram_unpack/pallas_call | solution.py:367
  (11 shorter events, 0.1 us)
Async XLA Ops:
  0.6 2.3 %copy-start = (s32[32,1024]{1,0:T(8,128)S(1)}, s32[32,1024]{1,0:T(8,128)}, u32[]{:S(2)}) copy-start(s32[32,1024]{1,0:T(8,128)} %signs_ref.3) | copy-start | bytes 393220
  0.7 2.3 %copy-start.1 = (f32[1024]{0:T(1024)S(1)}, f32[1024]{0:T(1024)}, u32[]{:S(2)}) copy-start(f32[1024]{0:T(1024)} %param.8) | copy-start | bytes 12292
  3.6 18.7 %copy-start.2 = (f32[2048]{0:T(1024)S(1)}, f32[2048]{0:T(1024)}, u32[]{:S(2)}) copy-start(f32[2048]{0:T(1024)} %param.9) | copy-start | bytes 24580
  3.6 18.7 %copy-start.3 = (f32[2048]{0:T(1024)S(1)}, f32[2048]{0:T(1024)}, u32[]{:S(2)}) copy-start(f32[2048]{0:T(1024)} %param.10) | copy-start | bytes 24580
  3.6 18.7 %copy-start.4 = (s32[2048]{0:T(1024)S(1)}, s32[2048]{0:T(1024)}, u32[]{:S(2)}) copy-start(s32[2048]{0:T(1024)} %param.11) | copy-start | bytes 24580
  3.6 3.2 %collective-permute-start = (f32[16,1152]{1,0:T(8,128)S(1)}, f32[16,1152]{1,0:T(8,128)S(1)}, u32[]{:S(2)}, u32[]{:S(2)}) collective-permute-start(f32[16,1152]{1,0:T(8,128)S(1)} %get-tuple-element.16), channel_id=1, source_target_pairs={{0,1},{1,0},{2,3},{3,2},{4,5},{5,4},{6,7},{7,6},{8,9},{9,8},{10,11... | collective-permute-start | bytes 221192 | tf_op jit(solution)/shard_map/ppermute | solution.py:249
  6.6 2.9 %collective-permute-start.4 = (f32[16,1152]{1,0:T(8,128)S(1)}, f32[16,1152]{1,0:T(8,128)S(1)}, u32[]{:S(2)}, u32[]{:S(2)}) collective-permute-start(f32[16,1152]{1,0:T(8,128)S(1)} %get-tuple-element.18), channel_id=1, source_target_pairs={{0,1},{1,0},{2,3},{3,2},{4,5},{5,4},{6,7},{7,6},{8,9},{9,8},{10,11... | collective-permute-start | bytes 221192 | tf_op jit(solution)/shard_map/ppermute | solution.py:249
  6.8 5.5 %collective-permute-start.1 = (f32[16,1152]{1,0:T(8,128)S(1)}, f32[16,1152]{1,0:T(8,128)S(1)}, u32[]{:S(2)}, u32[]{:S(2)}) collective-permute-start(f32[16,1152]{1,0:T(8,128)S(1)} %add.36), channel_id=1, source_target_pairs={{0,5},{1,2},{2,1},{3,6},{4,7},{5,0},{6,3},{7,4},{8,11},{9,12},{10,... | collective-permute-start | bytes 221192 | tf_op jit(solution)/shard_map/ppermute | solution.py:249
  9.5 4.9 %collective-permute-start.5 = (f32[16,1152]{1,0:T(8,128)S(1)}, f32[16,1152]{1,0:T(8,128)S(1)}, u32[]{:S(2)}, u32[]{:S(2)}) collective-permute-start(f32[16,1152]{1,0:T(8,128)S(1)} %add.40), channel_id=1, source_target_pairs={{0,9},{1,2},{2,1},{3,10},{4,7},{5,12},{6,15},{7,4},{8,11},{9,0},{1... | collective-permute-start | bytes 221192 | tf_op jit(solution)/shard_map/ppermute | solution.py:249
  12.3 4.8 %collective-permute-start.2 = (f32[16,1152]{1,0:T(8,128)S(1)}, f32[16,1152]{1,0:T(8,128)S(1)}, u32[]{:S(2)}, u32[]{:S(2)}) collective-permute-start(f32[16,1152]{1,0:T(8,128)S(1)} %add.37), channel_id=1, source_target_pairs={{0,9},{1,4},{2,7},{3,10},{4,1},{5,12},{6,15},{7,2},{8,13},{9,0},{1... | collective-permute-start | bytes 221192 | tf_op jit(solution)/shard_map/ppermute | solution.py:249
  14.5 4.5 %collective-permute-start.6 = (f32[16,1152]{1,0:T(8,128)S(1)}, f32[16,1152]{1,0:T(8,128)S(1)}, u32[]{:S(2)}, u32[]{:S(2)}) collective-permute-start(f32[16,1152]{1,0:T(8,128)S(1)} %add.41), channel_id=1, source_target_pairs={{0,3},{1,4},{2,7},{3,0},{4,1},{5,6},{6,5},{7,2},{8,13},{9,10},{10,... | collective-permute-start | bytes 221192 | tf_op jit(solution)/shard_map/ppermute | solution.py:249
  17.1 3.9 %collective-permute-start.3 = (f32[16,1152]{1,0:T(8,128)S(1)}, f32[16,1152]{1,0:T(8,128)S(1)}, u32[]{:S(2)}, u32[]{:S(2)}) collective-permute-start(f32[16,1152]{1,0:T(8,128)S(1)} %add.38), channel_id=1, source_target_pairs={{0,3},{1,8},{2,11},{3,0},{4,13},{5,6},{6,5},{7,14},{8,1},{9,10},{1... | collective-permute-start | bytes 221192 | tf_op jit(solution)/shard_map/ppermute | solution.py:249
  19.0 6.2 %collective-permute-start.7 = (f32[16,1152]{1,0:T(8,128)S(1)}, f32[16,1152]{1,0:T(8,128)S(1)}, u32[]{:S(2)}, u32[]{:S(2)}) collective-permute-start(f32[16,1152]{1,0:T(8,128)S(1)} %add.42), channel_id=1, source_target_pairs={{0,5},{1,8},{2,11},{3,6},{4,13},{5,0},{6,3},{7,14},{8,1},{9,12},{1... | collective-permute-start | bytes 221192 | tf_op jit(solution)/shard_map/ppermute | solution.py:249
  21.0 2.7 %collective-permute-start.8 = (f32[16,1152]{1,0:T(8,128)S(1)}, f32[16,1152]{1,0:T(8,128)S(1)}, u32[]{:S(2)}, u32[]{:S(2)}) collective-permute-start(f32[16,1152]{1,0:T(8,128)S(1)} %add.39.sums_a), channel_id=1, source_target_pairs={{0,1},{1,0},{2,3},{3,2},{4,5},{5,4},{6,7},{7,6},{8,9},{9,8},{10,11... | collective-permute-start | bytes 221192 | tf_op jit(solution)/shard_map/ppermute | solution.py:249
  25.2 2.1 %collective-permute-start.9 = (f32[16,1152]{1,0:T(8,128)S(1)}, f32[16,1152]{1,0:T(8,128)S(1)}, u32[]{:S(2)}, u32[]{:S(2)}) collective-permute-start(f32[16,1152]{1,0:T(8,128)S(1)} %add.43.own_b), channel_id=1, source_target_pairs={{0,1},{1,0},{2,3},{3,2},{4,5},{5,4},{6,7},{7,6},{8,9},{9,8},{10,11... | collective-permute-start | bytes 221192 | tf_op jit(solution)/shard_map/ppermute | solution.py:249
  29.1 1.3 %collective-permute-start.10 = (f32[8,896]{1,0:T(8,128)S(1)}, f32[8,896]{1,0:T(8,128)S(1)}, u32[]{:S(2)}, u32[]{:S(2)}) collective-permute-start(f32[8,896]{1,0:T(8,128)S(1)} %get-tuple-element.27), channel_id=1, source_target_pairs={{0,1},{1,0},{2,3},{3,2},{4,5},{5,4},{6,7},{7,6},{8,9},{9,8},{10,11... | collective-permute-start | bytes 86024 | tf_op jit(solution)/shard_map/ppermute | solution.py:249
  30.4 4.2 %collective-permute-start.13 = (f32[8,896]{1,0:T(8,128)S(1)}, f32[8,896]{1,0:T(8,128)S(1)}, u32[]{:S(2)}, u32[]{:S(2)}) collective-permute-start(f32[8,896]{1,0:T(8,128)S(1)} %add.44), channel_id=1, source_target_pairs={{0,7},{1,6},{2,5},{3,4},{4,3},{5,2},{6,1},{7,0},{8,15},{9,14},{10,... | collective-permute-start | bytes 86024 | tf_op jit(solution)/shard_map/ppermute | solution.py:249
  32.0 3.3 %collective-permute-start.12 = (f32[8,896]{1,0:T(8,128)S(1)}, f32[8,896]{1,0:T(8,128)S(1)}, u32[]{:S(2)}, u32[]{:S(2)}) collective-permute-start(f32[8,896]{1,0:T(8,128)S(1)} %add.44), channel_id=1, source_target_pairs={{0,5},{1,4},{2,7},{3,6},{4,1},{5,0},{6,3},{7,2},{8,13},{9,12},{10,... | collective-permute-start | bytes 86024 | tf_op jit(solution)/shard_map/ppermute | solution.py:249
  32.5 3.3 %collective-permute-start.11 = (f32[8,896]{1,0:T(8,128)S(1)}, f32[8,896]{1,0:T(8,128)S(1)}, u32[]{:S(2)}, u32[]{:S(2)}) collective-permute-start(f32[8,896]{1,0:T(8,128)S(1)} %add.44), channel_id=1, source_target_pairs={{0,3},{1,2},{2,1},{3,0},{4,7},{5,6},{6,5},{7,4},{8,11},{9,10},{10,... | collective-permute-start | bytes 86024 | tf_op jit(solution)/shard_map/ppermute | solution.py:249
  35.8 4.3 %collective-permute-start.14 = (f32[8,896]{1,0:T(8,128)S(1)}, f32[8,896]{1,0:T(8,128)S(1)}, u32[]{:S(2)}, u32[]{:S(2)}) collective-permute-start(f32[8,896]{1,0:T(8,128)S(1)} %add_add_fusion.one_ref), channel_id=1, source_target_pairs={{0,9},{1,8},{2,11},{3,10},{4,13},{5,12},{6,15},{7,14},{8,1},{9,0},... | collective-permute-start | bytes 86024 | tf_op jit(solution)/shard_map/ppermute | solution.py:249

commit v8 on v7

--- a/solution.py
+++ b/solution.py
@@ -330,7 +330,7 @@
         multiply(part_kernel, name, count, jax.ShapeDtypeStruct((count, samples), F32), x, narrow_a, *markers_info, pheno=count > rows)
         for name, count, x in (("products_part", rows, own_a), ("products_part_other", rows + BINS, other_a))
     )
-    own_b, received, other_part = lax.optimization_barrier((own_b, received, other_part))
+    received, own_part, other_part = lax.optimization_barrier((received, own_part, other_part))
     own_b = own_b + received
     other_b = exchange(own_b, 1)
     out_shape = (

time: 41.3 us -> 41.3 us (level)
  no operation moved by 1% of the time
where the time goes in v8:
time: 41.3 us; the launch traced here: 41.1 us
  starting transfers between devices  21.4 us (52%)
  Pallas kernels  14.4 us (35%)
  waiting for transfers between devices  4.35 us (11%)
  between operations  0.78 us (2%)
    ppermute x15, starting transfers between devices, exchange(): return lax.ppermute(x, 'samp', pairs)  21.4 us
    pallas_call x7, Pallas kernels, local(): pl.pallas_call(functools.partial(kernel, **options), out_shape=out_shape,...  12.1 us
    ppermute x15, waiting for transfers between devices, exchange(): return lax.ppermute(x, 'samp', pairs)  4.35 us
    pallas_call x1, Pallas kernels, shards(): pl.pallas_call(store_kernel, out_shape=jax.ShapeDtypeStruct((probes + 1,...  1.34 us
    pallas_call x1, Pallas kernels, shards(): pl.pallas_call(functools.partial(unpack_kernel, pairs=2 * rows // (2 * LA...  1.04 us
  transfers between devices with their start and end apart: 15, of which 7 were waited for; matrix products, arithmetic and copies ran while one was open for 0% of the time, Pallas kernels for 21%

profile of v8, /device:TPU:0, one launch (start us, length us, event | category | flops | bytes accessed | tf_op | source)
XLA Modules:
  0.0 41.1 jit_solution(17703582069406061230)
XLA Ops:
  0.6 0.0 copy-start
  0.7 0.0 copy-start.1
  0.7 2.3 %narrow_first.1.narrow_ref.geno_a = bf16[1024,1024]{1,0:T(8,128)(2,1)S(1)} custom-call(s32[1024,2048]{1,0:T(8,128)} %geno_hbm.3), custom_call_target="tpu_custom_call" | custom-call | bytes 6291456 | tf_op jit(solution)/shard_map/narrow_first/pallas_call | solution.py:276
  3.0 0.0 copy-done
  3.0 0.0 copy-done.1
  3.0 0.6 %sums_first.1 = (f32[16,1152]{1,0:T(8,128)S(1)}, f32[16,1152]{1,0:T(8,128)S(1)}) custom-call(s32[1]{0:T(128)} %bitcast.side_ref, bf16[1024,1024]{1,0:T(8,128)(2,1)S(1)} %narrow_first.1.narrow_ref.geno_a, s32[32,1024]{1,0:T(8,128)S(1)} %copy-done, f32[1,1024]{1,0:T(1,128)S(1)} %bitcast.6), custom_call_target="tpu_custom_call" | custom-call | flops 67108864 | bytes 2097152 | tf_op jit(solution)/shard_map/sums_first/pallas_call | solution.py:276
  3.6 0.0 copy-start.2
  3.6 0.0 copy-start.3
  3.6 0.5 %collective-permute-start.4 = (f32[16,1152]{1,0:T(8,128)S(1)}, f32[16,1152]{1,0:T(8,128)S(1)}, u32[]{:S(2)}, u32[]{:S(2)}) collective-permute-start(f32[16,1152]{1,0:T(8,128)S(1)} %get-tuple-element.18), channel_id=1, source_target_pairs={{0,1},{1,0},{2,3},{3,2},{4,5},{5,4},{6,7},{7,6},{8,9},{9,8},{10,11... | collective-permute-start | bytes 221192 | tf_op jit(solution)/shard_map/ppermute | solution.py:249
  4.1 2.6 %sums_second.1 = (f32[16,1152]{1,0:T(8,128)S(1)}, f32[16,1152]{1,0:T(8,128)S(1)}, bf16[1024,1024]{1,0:T(8,128)(2,1)S(1)}) custom-call(s32[1]{0:T(128)} %bitcast.side_ref, s32[1024,2048]{1,0:T(8,128)} %geno_hbm.3, s32[32,1024]{1,0:T(8,128)S(1)} %copy-done, f32[1,1024]{1,0:T(1,128)S(1)} %bitcast.7), custom_call_target="tpu_custom_call" | custom-call | flops 67108864 | bytes 6291456 | tf_op jit(solution)/shard_map/sums_second/pallas_call | solution.py:276
  6.6 0.1 collective-permute-start
  6.8 0.0 collective-permute-done.4
  6.8 2.7 %collective-permute-start.5 = (f32[16,1152]{1,0:T(8,128)S(1)}, f32[16,1152]{1,0:T(8,128)S(1)}, u32[]{:S(2)}, u32[]{:S(2)}) collective-permute-start(f32[16,1152]{1,0:T(8,128)S(1)} %add.39), channel_id=1, source_target_pairs={{0,5},{1,2},{2,1},{3,6},{4,7},{5,0},{6,3},{7,4},{8,11},{9,12},{10,... | collective-permute-start | bytes 221192 | tf_op jit(solution)/shard_map/ppermute | solution.py:249
  9.5 0.0 collective-permute-done
  9.5 2.7 %collective-permute-start.1 = (f32[16,1152]{1,0:T(8,128)S(1)}, f32[16,1152]{1,0:T(8,128)S(1)}, u32[]{:S(2)}, u32[]{:S(2)}) collective-permute-start(f32[16,1152]{1,0:T(8,128)S(1)} %add.36), channel_id=1, source_target_pairs={{0,9},{1,2},{2,1},{3,10},{4,7},{5,12},{6,15},{7,4},{8,11},{9,0},{1... | collective-permute-start | bytes 221192 | tf_op jit(solution)/shard_map/ppermute | solution.py:249
  12.3 0.0 collective-permute-done.5
  12.3 2.2 %collective-permute-start.6 = (f32[16,1152]{1,0:T(8,128)S(1)}, f32[16,1152]{1,0:T(8,128)S(1)}, u32[]{:S(2)}, u32[]{:S(2)}) collective-permute-start(f32[16,1152]{1,0:T(8,128)S(1)} %add.40), channel_id=1, source_target_pairs={{0,9},{1,4},{2,7},{3,10},{4,1},{5,12},{6,15},{7,2},{8,13},{9,0},{1... | collective-permute-start | bytes 221192 | tf_op jit(solution)/shard_map/ppermute | solution.py:249
  14.5 0.0 collective-permute-done.1
  14.5 2.3 %collective-permute-start.2 = (f32[16,1152]{1,0:T(8,128)S(1)}, f32[16,1152]{1,0:T(8,128)S(1)}, u32[]{:S(2)}, u32[]{:S(2)}) collective-permute-start(f32[16,1152]{1,0:T(8,128)S(1)} %add.37), channel_id=1, source_target_pairs={{0,3},{1,4},{2,7},{3,0},{4,1},{5,6},{6,5},{7,2},{8,13},{9,10},{10,... | collective-permute-start | bytes 221192 | tf_op jit(solution)/shard_map/ppermute | solution.py:249
  16.8 0.3 collective-permute-done.6
  17.1 1.9 %collective-permute-start.7 = (f32[16,1152]{1,0:T(8,128)S(1)}, f32[16,1152]{1,0:T(8,128)S(1)}, u32[]{:S(2)}, u32[]{:S(2)}) collective-permute-start(f32[16,1152]{1,0:T(8,128)S(1)} %add.41), channel_id=1, source_target_pairs={{0,3},{1,8},{2,11},{3,0},{4,13},{5,6},{6,5},{7,14},{8,1},{9,10},{1... | collective-permute-start | bytes 221192 | tf_op jit(solution)/shard_map/ppermute | solution.py:249
  19.0 0.0 collective-permute-done.2
  19.0 1.3 %collective-permute-start.3 = (f32[16,1152]{1,0:T(8,128)S(1)}, f32[16,1152]{1,0:T(8,128)S(1)}, u32[]{:S(2)}, u32[]{:S(2)}) collective-permute-start(f32[16,1152]{1,0:T(8,128)S(1)} %add.38), channel_id=1, source_target_pairs={{0,5},{1,8},{2,11},{3,6},{4,13},{5,0},{6,3},{7,14},{8,1},{9,12},{1... | collective-permute-start | bytes 221192 | tf_op jit(solution)/shard_map/ppermute | solution.py:249
  20.3 0.7 %collective-permute-done.7 = f32[16,1152]{1,0:T(8,128)S(1)} collective-permute-done((f32[16,1152]{1,0:T(8,128)S(1)}, f32[16,1152]{1,0:T(8,128)S(1)}, u32[]{:S(2)}, u32[]{:S(2)}) %collective-permute-start.7) | collective-permute-done | bytes 73760 | tf_op jit(solution)/shard_map/ppermute | solution.py:249
  21.0 1.3 %collective-permute-start.8 = (f32[16,1152]{1,0:T(8,128)S(1)}, f32[16,1152]{1,0:T(8,128)S(1)}, u32[]{:S(2)}, u32[]{:S(2)}) collective-permute-start(f32[16,1152]{1,0:T(8,128)S(1)} %add.42.sums_a), channel_id=1, source_target_pairs={{0,1},{1,0},{2,3},{3,2},{4,5},{5,4},{6,7},{7,6},{8,9},{9,8},{10,11... | collective-permute-start | bytes 221192 | tf_op jit(solution)/shard_map/ppermute | solution.py:249
  22.3 0.0 copy-done.2
  22.4 0.0 copy-done.3
  22.4 0.0 copy-done.4
  22.4 1.4 %products_part.1.own_part = f32[256,1024]{1,0:T(8,128)S(1)} custom-call(f32[16,1152]{1,0:T(8,128)S(1)} %add.42.sums_a, bf16[1024,1024]{1,0:T(8,128)(2,1)S(1)} %narrow_first.1.narrow_ref.geno_a, f32[1,2048]{1,0:T(1,128)S(1)} %bitcast.8, f32[1,2048]{1,0:T(1,128)S(1)} %bitcast.12, s32[1,2048]{1,0:T(1,128)S(1)} %bitcast.16), custom_call_target="tpu_custom_call" | custom-call | flops 1073741824 | bytes 1048576 | tf_op jit(solution)/shard_map/products_part/pallas_call | solution.py:276
  23.7 0.0 collective-permute-done.8.sums_a
  23.8 1.4 %products_part_other.1.other_part.part_ref = f32[272,1024]{1,0:T(8,128)S(1)} custom-call(f32[16,1152]{1,0:T(8,128)S(1)} %collective-permute-done.8.sums_a, bf16[1024,1024]{1,0:T(8,128)(2,1)S(1)} %narrow_first.1.narrow_ref.geno_a, f32[1,2048]{1,0:T(1,128)S(1)} %bitcast.9, f32[1,2048]{1,0:T(1,128)S(1)} %bitcast.13, s32[1,2048]{1,0:T(1,128)S(1)} %bitcast.17), custom_call_target="tpu_custom_call" | custom-call | flops 1140850688 | bytes 1114112 | tf_op jit(solution)/shard_map/products_part_other/pallas_call | solution.py:276
  25.2 0.0 collective-permute-done.3
  25.2 0.1 collective-permute-start.9
  25.3 1.9 %products_own.1 = (f32[16,16,1024]{2,1,0:T(8,128)S(1)}, f32[1,16,1024]{2,1,0:T(8,128)S(1)}, f32[8,512]{1,0:T(8,128)S(1)}) custom-call(f32[256,1024]{1,0:T(8,128)S(1)} %products_part.1.own_part, f32[272,1024]{1,0:T(8,128)S(1)} %products_part_other.1.other_part.part_ref, f32[16,1152]{1,0:T(8,128)S(1)} %add.43.own_b, ...), custom_call_target="tpu_custom_call" | custom-call | flops 1140850688 | bytes 1114112 | tf_op jit(solution)/shard_map/products_own/pallas_call | solution.py:276
  27.3 0.0 collective-permute-done.9.other_b
  27.3 1.8 %products_other.1 = (f32[16,16,1024]{2,1,0:T(8,128)S(1)}, f32[8,896]{1,0:T(8,128)S(1)}) custom-call(s32[1]{0:T(128)} %bitcast.side_ref, f32[272,1024]{1,0:T(8,128)S(1)} %products_part_other.1.other_part.part_ref, f32[16,1152]{1,0:T(8,128)S(1)} %collective-permute-done.9.other_b, bf16[1024,1024]{1,0:T(8,128)(2,1)S(1)} %get-tuple-element.22.geno_b, ...), custom_call_target="tpu_custom_call" | custom-call | flops 1073741824 | bytes 1048576 | tf_op jit(solution)/shard_map/products_other/pallas_call | solution.py:276
  29.1 0.5 %collective-permute-start.10 = (f32[8,896]{1,0:T(8,128)S(1)}, f32[8,896]{1,0:T(8,128)S(1)}, u32[]{:S(2)}, u32[]{:S(2)}) collective-permute-start(f32[8,896]{1,0:T(8,128)S(1)} %get-tuple-element.27), channel_id=1, source_target_pairs={{0,1},{1,0},{2,3},{3,2},{4,5},{5,4},{6,7},{7,6},{8,9},{9,8},{10,11... | collective-permute-start | bytes 86024 | tf_op jit(solution)/shard_map/ppermute | solution.py:249
  29.6 0.9 %collective-permute-done.10 = f32[8,896]{1,0:T(8,128)S(1)} collective-permute-done((f32[8,896]{1,0:T(8,128)S(1)}, f32[8,896]{1,0:T(8,128)S(1)}, u32[]{:S(2)}, u32[]{:S(2)}) %collective-permute-start.10) | collective-permute-done | bytes 28704 | tf_op jit(solution)/shard_map/ppermute | solution.py:249
  30.4 1.5 %collective-permute-start.13 = (f32[8,896]{1,0:T(8,128)S(1)}, f32[8,896]{1,0:T(8,128)S(1)}, u32[]{:S(2)}, u32[]{:S(2)}) collective-permute-start(f32[8,896]{1,0:T(8,128)S(1)} %add.44), channel_id=1, source_target_pairs={{0,7},{1,6},{2,5},{3,4},{4,3},{5,2},{6,1},{7,0},{8,15},{9,14},{10,... | collective-permute-start | bytes 86024 | tf_op jit(solution)/shard_map/ppermute | solution.py:249
  32.0 0.5 %collective-permute-start.12 = (f32[8,896]{1,0:T(8,128)S(1)}, f32[8,896]{1,0:T(8,128)S(1)}, u32[]{:S(2)}, u32[]{:S(2)}) collective-permute-start(f32[8,896]{1,0:T(8,128)S(1)} %add.44), channel_id=1, source_target_pairs={{0,5},{1,4},{2,7},{3,6},{4,1},{5,0},{6,3},{7,2},{8,13},{9,12},{10,... | collective-permute-start | bytes 86024 | tf_op jit(solution)/shard_map/ppermute | solution.py:249
  32.5 1.1 %collective-permute-start.11 = (f32[8,896]{1,0:T(8,128)S(1)}, f32[8,896]{1,0:T(8,128)S(1)}, u32[]{:S(2)}, u32[]{:S(2)}) collective-permute-start(f32[8,896]{1,0:T(8,128)S(1)} %add.44), channel_id=1, source_target_pairs={{0,3},{1,2},{2,1},{3,0},{4,7},{5,6},{6,5},{7,4},{8,11},{9,10},{10,... | collective-permute-start | bytes 86024 | tf_op jit(solution)/shard_map/ppermute | solution.py:249
  33.6 1.0 %collective-permute-done.13 = f32[8,896]{1,0:T(8,128)S(1)} collective-permute-done((f32[8,896]{1,0:T(8,128)S(1)}, f32[8,896]{1,0:T(8,128)S(1)}, u32[]{:S(2)}, u32[]{:S(2)}) %collective-permute-start.13) | collective-permute-done | bytes 28704 | tf_op jit(solution)/shard_map/ppermute | solution.py:249
  34.6 0.6 %collective-permute-done.12 = f32[8,896]{1,0:T(8,128)S(1)} collective-permute-done((f32[8,896]{1,0:T(8,128)S(1)}, f32[8,896]{1,0:T(8,128)S(1)}, u32[]{:S(2)}, u32[]{:S(2)}) %collective-permute-start.12) | collective-permute-done | bytes 28704 | tf_op jit(solution)/shard_map/ppermute | solution.py:249
  35.3 0.5 %collective-permute-done.11 = f32[8,896]{1,0:T(8,128)S(1)} collective-permute-done((f32[8,896]{1,0:T(8,128)S(1)}, f32[8,896]{1,0:T(8,128)S(1)}, u32[]{:S(2)}, u32[]{:S(2)}) %collective-permute-start.11) | collective-permute-done | bytes 28704 | tf_op jit(solution)/shard_map/ppermute | solution.py:249
  35.8 2.7 %collective-permute-start.14 = (f32[8,896]{1,0:T(8,128)S(1)}, f32[8,896]{1,0:T(8,128)S(1)}, u32[]{:S(2)}, u32[]{:S(2)}) collective-permute-start(f32[8,896]{1,0:T(8,128)S(1)} %add_add_fusion.one_ref), channel_id=1, source_target_pairs={{0,9},{1,8},{2,11},{3,10},{4,13},{5,12},{6,15},{7,14},{8,1},{9,0},... | collective-permute-start | bytes 86024 | tf_op jit(solution)/shard_map/ppermute | solution.py:249
  38.5 1.3 %products_store.1 = f32[33,16,1024]{2,1,0:T(8,128)} custom-call(s32[1]{0:T(128)} %bitcast.side_ref, f32[16,16,1024]{2,1,0:T(8,128)S(1)} %get-tuple-element.23.mine_ref, f32[16,16,1024]{2,1,0:T(8,128)S(1)} %get-tuple-element.25.theirs_ref, f32[1,16,1024]{2,1,0:T(8,128)S(1)} %get-tuple-element.26.last_ref), custom_call_target="tpu_custom_call" | custom-call | bytes 2162688 | tf_op jit(solution)/shard_map/products_store/pallas_call | solution.py:348
  39.8 0.2 collective-permute-done.14.two_ref
  40.1 1.0 %gram_unpack.1 = f32[16,16,33]{2,1,0:T(8,128)} custom-call(f32[8,896]{1,0:T(8,128)S(1)} %add_add_fusion.one_ref, f32[8,896]{1,0:T(8,128)S(1)} %collective-permute-done.14.two_ref), custom_call_target="tpu_custom_call" | custom-call | tf_op jit(solution)/shard_map/gram_unpack/pallas_call | solution.py:367
  (11 shorter events, 0.1 us)
Async XLA Ops:
  0.6 2.3 %copy-start = (s32[32,1024]{1,0:T(8,128)S(1)}, s32[32,1024]{1,0:T(8,128)}, u32[]{:S(2)}) copy-start(s32[32,1024]{1,0:T(8,128)} %signs_ref.3) | copy-start | bytes 393220
  0.7 2.3 %copy-start.1 = (f32[1024]{0:T(1024)S(1)}, f32[1024]{0:T(1024)}, u32[]{:S(2)}) copy-start(f32[1024]{0:T(1024)} %param.8) | copy-start | bytes 12292
  3.6 18.7 %copy-start.2 = (f32[2048]{0:T(1024)S(1)}, f32[2048]{0:T(1024)}, u32[]{:S(2)}) copy-start(f32[2048]{0:T(1024)} %param.9) | copy-start | bytes 24580
  3.6 18.7 %copy-start.3 = (f32[2048]{0:T(1024)S(1)}, f32[2048]{0:T(1024)}, u32[]{:S(2)}) copy-start(f32[2048]{0:T(1024)} %param.10) | copy-start | bytes 24580
  3.6 18.7 %copy-start.4 = (s32[2048]{0:T(1024)S(1)}, s32[2048]{0:T(1024)}, u32[]{:S(2)}) copy-start(s32[2048]{0:T(1024)} %param.11) | copy-start | bytes 24580
  3.6 3.2 %collective-permute-start.4 = (f32[16,1152]{1,0:T(8,128)S(1)}, f32[16,1152]{1,0:T(8,128)S(1)}, u32[]{:S(2)}, u32[]{:S(2)}) collective-permute-start(f32[16,1152]{1,0:T(8,128)S(1)} %get-tuple-element.18), channel_id=1, source_target_pairs={{0,1},{1,0},{2,3},{3,2},{4,5},{5,4},{6,7},{7,6},{8,9},{9,8},{10,11... | collective-permute-start | bytes 221192 | tf_op jit(solution)/shard_map/ppermute | solution.py:249
  6.6 2.9 %collective-permute-start = (f32[16,1152]{1,0:T(8,128)S(1)}, f32[16,1152]{1,0:T(8,128)S(1)}, u32[]{:S(2)}, u32[]{:S(2)}) collective-permute-start(f32[16,1152]{1,0:T(8,128)S(1)} %get-tuple-element.16), channel_id=1, source_target_pairs={{0,1},{1,0},{2,3},{3,2},{4,5},{5,4},{6,7},{7,6},{8,9},{9,8},{10,11... | collective-permute-start | bytes 221192 | tf_op jit(solution)/shard_map/ppermute | solution.py:249
  6.8 5.5 %collective-permute-start.5 = (f32[16,1152]{1,0:T(8,128)S(1)}, f32[16,1152]{1,0:T(8,128)S(1)}, u32[]{:S(2)}, u32[]{:S(2)}) collective-permute-start(f32[16,1152]{1,0:T(8,128)S(1)} %add.39), channel_id=1, source_target_pairs={{0,5},{1,2},{2,1},{3,6},{4,7},{5,0},{6,3},{7,4},{8,11},{9,12},{10,... | collective-permute-start | bytes 221192 | tf_op jit(solution)/shard_map/ppermute | solution.py:249
  9.5 4.9 %collective-permute-start.1 = (f32[16,1152]{1,0:T(8,128)S(1)}, f32[16,1152]{1,0:T(8,128)S(1)}, u32[]{:S(2)}, u32[]{:S(2)}) collective-permute-start(f32[16,1152]{1,0:T(8,128)S(1)} %add.36), channel_id=1, source_target_pairs={{0,9},{1,2},{2,1},{3,10},{4,7},{5,12},{6,15},{7,4},{8,11},{9,0},{1... | collective-permute-start | bytes 221192 | tf_op jit(solution)/shard_map/ppermute | solution.py:249
  12.3 4.8 %collective-permute-start.6 = (f32[16,1152]{1,0:T(8,128)S(1)}, f32[16,1152]{1,0:T(8,128)S(1)}, u32[]{:S(2)}, u32[]{:S(2)}) collective-permute-start(f32[16,1152]{1,0:T(8,128)S(1)} %add.40), channel_id=1, source_target_pairs={{0,9},{1,4},{2,7},{3,10},{4,1},{5,12},{6,15},{7,2},{8,13},{9,0},{1... | collective-permute-start | bytes 221192 | tf_op jit(solution)/shard_map/ppermute | solution.py:249
  14.5 4.5 %collective-permute-start.2 = (f32[16,1152]{1,0:T(8,128)S(1)}, f32[16,1152]{1,0:T(8,128)S(1)}, u32[]{:S(2)}, u32[]{:S(2)}) collective-permute-start(f32[16,1152]{1,0:T(8,128)S(1)} %add.37), channel_id=1, source_target_pairs={{0,3},{1,4},{2,7},{3,0},{4,1},{5,6},{6,5},{7,2},{8,13},{9,10},{10,... | collective-permute-start | bytes 221192 | tf_op jit(solution)/shard_map/ppermute | solution.py:249
  17.1 3.9 %collective-permute-start.7 = (f32[16,1152]{1,0:T(8,128)S(1)}, f32[16,1152]{1,0:T(8,128)S(1)}, u32[]{:S(2)}, u32[]{:S(2)}) collective-permute-start(f32[16,1152]{1,0:T(8,128)S(1)} %add.41), channel_id=1, source_target_pairs={{0,3},{1,8},{2,11},{3,0},{4,13},{5,6},{6,5},{7,14},{8,1},{9,10},{1... | collective-permute-start | bytes 221192 | tf_op jit(solution)/shard_map/ppermute | solution.py:249
  19.0 6.2 %collective-permute-start.3 = (f32[16,1152]{1,0:T(8,128)S(1)}, f32[16,1152]{1,0:T(8,128)S(1)}, u32[]{:S(2)}, u32[]{:S(2)}) collective-permute-start(f32[16,1152]{1,0:T(8,128)S(1)} %add.38), channel_id=1, source_target_pairs={{0,5},{1,8},{2,11},{3,6},{4,13},{5,0},{6,3},{7,14},{8,1},{9,12},{1... | collective-permute-start | bytes 221192 | tf_op jit(solution)/shard_map/ppermute | solution.py:249
  21.0 2.7 %collective-permute-start.8 = (f32[16,1152]{1,0:T(8,128)S(1)}, f32[16,1152]{1,0:T(8,128)S(1)}, u32[]{:S(2)}, u32[]{:S(2)}) collective-permute-start(f32[16,1152]{1,0:T(8,128)S(1)} %add.42.sums_a), channel_id=1, source_target_pairs={{0,1},{1,0},{2,3},{3,2},{4,5},{5,4},{6,7},{7,6},{8,9},{9,8},{10,11... | collective-permute-start | bytes 221192 | tf_op jit(solution)/shard_map/ppermute | solution.py:249
  25.2 2.1 %collective-permute-start.9 = (f32[16,1152]{1,0:T(8,128)S(1)}, f32[16,1152]{1,0:T(8,128)S(1)}, u32[]{:S(2)}, u32[]{:S(2)}) collective-permute-start(f32[16,1152]{1,0:T(8,128)S(1)} %add.43.own_b), channel_id=1, source_target_pairs={{0,1},{1,0},{2,3},{3,2},{4,5},{5,4},{6,7},{7,6},{8,9},{9,8},{10,11... | collective-permute-start | bytes 221192 | tf_op jit(solution)/shard_map/ppermute | solution.py:249
  29.1 1.3 %collective-permute-start.10 = (f32[8,896]{1,0:T(8,128)S(1)}, f32[8,896]{1,0:T(8,128)S(1)}, u32[]{:S(2)}, u32[]{:S(2)}) collective-permute-start(f32[8,896]{1,0:T(8,128)S(1)} %get-tuple-element.27), channel_id=1, source_target_pairs={{0,1},{1,0},{2,3},{3,2},{4,5},{5,4},{6,7},{7,6},{8,9},{9,8},{10,11... | collective-permute-start | bytes 86024 | tf_op jit(solution)/shard_map/ppermute | solution.py:249
  30.4 4.2 %collective-permute-start.13 = (f32[8,896]{1,0:T(8,128)S(1)}, f32[8,896]{1,0:T(8,128)S(1)}, u32[]{:S(2)}, u32[]{:S(2)}) collective-permute-start(f32[8,896]{1,0:T(8,128)S(1)} %add.44), channel_id=1, source_target_pairs={{0,7},{1,6},{2,5},{3,4},{4,3},{5,2},{6,1},{7,0},{8,15},{9,14},{10,... | collective-permute-start | bytes 86024 | tf_op jit(solution)/shard_map/ppermute | solution.py:249
  32.0 3.3 %collective-permute-start.12 = (f32[8,896]{1,0:T(8,128)S(1)}, f32[8,896]{1,0:T(8,128)S(1)}, u32[]{:S(2)}, u32[]{:S(2)}) collective-permute-start(f32[8,896]{1,0:T(8,128)S(1)} %add.44), channel_id=1, source_target_pairs={{0,5},{1,4},{2,7},{3,6},{4,1},{5,0},{6,3},{7,2},{8,13},{9,12},{10,... | collective-permute-start | bytes 86024 | tf_op jit(solution)/shard_map/ppermute | solution.py:249
  32.5 3.3 %collective-permute-start.11 = (f32[8,896]{1,0:T(8,128)S(1)}, f32[8,896]{1,0:T(8,128)S(1)}, u32[]{:S(2)}, u32[]{:S(2)}) collective-permute-start(f32[8,896]{1,0:T(8,128)S(1)} %add.44), channel_id=1, source_target_pairs={{0,3},{1,2},{2,1},{3,0},{4,7},{5,6},{6,5},{7,4},{8,11},{9,10},{10,... | collective-permute-start | bytes 86024 | tf_op jit(solution)/shard_map/ppermute | solution.py:249
  35.8 4.3 %collective-permute-start.14 = (f32[8,896]{1,0:T(8,128)S(1)}, f32[8,896]{1,0:T(8,128)S(1)}, u32[]{:S(2)}, u32[]{:S(2)}) collective-permute-start(f32[8,896]{1,0:T(8,128)S(1)} %add_add_fusion.one_ref), channel_id=1, source_target_pairs={{0,9},{1,8},{2,11},{3,10},{4,13},{5,12},{6,15},{7,14},{8,1},{9,0},... | collective-permute-start | bytes 86024 | tf_op jit(solution)/shard_map/ppermute | solution.py:249
